TPU v7x, 256 devices: a whole 4x4x8 slice. The times are simulated.
256 devices in a mesh: layer: 4 (over x), feat: 64 (over z, y, core).
Axes of the slice: x: 4, y: 4, z: 8, core: 2. Of those that a mesh axis runs over, the one named last changes fastest.
Arguments:
- resid: bfloat16 [512, 4, 2048], P(('layer', 'feat')), may hold values from -6 to 6
- target: bfloat16 [512, 4, 2048], P(('layer', 'feat')), may hold values from -6 to 6
- enc_weight: bfloat16 [4, 2048, 16384], P('layer', None, 'feat'), may hold values from -0.125 to 0.125
- enc_bias: float32 [4, 16384], P('layer', 'feat'), may hold values from -3 to 3
- dec_weight: bfloat16 [4, 4, 16384, 2048], P('layer', None, 'feat'), may hold values from -5 to 5
- dec_bias: float32 [4, 2048], P('layer'), may hold values from -3 to 3
Outputs:
- dec_grad: bfloat16 [4, 4, 16384, 2048], P('layer', None, 'feat')
All inputs are finite; a program needn't handle non-finite values.
Results may differ from a plain program's by a relative error of at most 0.0023.
Values may be sent and summed in bfloat16 or wider, within the bound.
No kernel may reach another device: no remote copies, remote signals or barrier semaphores. Data moves between devices by JAX's collectives and lax.ppermute only.
A program may use at most 128 MiB of HBM per device.

v0:
```python
import math

import jax
import jax.numpy as jnp
from jax import lax
from jax.sharding import PartitionSpec as P


def body(resid, target, enc_weight, enc_bias, dec_weight, dec_bias):
    layers = lax.axis_size("layer")
    owner = lax.axis_index("layer")
    moved_x, moved_t = (
        lax.all_to_all(resid, "layer", split_axis=1, concat_axis=0, tiled=True),
        lax.all_to_all(target, "layer", split_axis=1, concat_axis=0, tiled=True),
    )
    inputs = lax.all_gather(moved_x[:, 0, :], "feat", axis=0, tiled=True)
    total_tokens = inputs.shape[0]
    factor = 1.0 / math.sqrt(total_tokens)
    preact = (
        jnp.dot(inputs, enc_weight[0], preferred_element_type=jnp.float32) + enc_bias[0][None, :]
    )
    activity = jax.nn.relu(preact).astype(jnp.bfloat16)
    later_mask = (jnp.arange(layers) >= owner).astype(jnp.float32)
    partials = jnp.einsum(
        "tf,mfd->mtd", activity, dec_weight[0], preferred_element_type=jnp.float32
    )
    partials = partials * later_mask[:, None, None]
    width = partials.shape[2]
    summed = lax.psum_scatter(
        partials.reshape(layers * total_tokens, width),
        ("layer", "feat"),
        scatter_dimension=0,
        tiled=True,
    )
    misfit = summed + dec_bias[0][None, :] - moved_t[:, 0, :].astype(jnp.float32)
    cotangent = (misfit * factor).astype(jnp.bfloat16)
    stacked = lax.all_gather(cotangent[None], "layer", axis=0, tiled=True)
    grads = jnp.einsum(
        "tf,mtd->mfd",
        activity,
        lax.all_gather(stacked, "feat", axis=1, tiled=True),
        preferred_element_type=jnp.float32,
    )
    dec_grad = (grads * later_mask[:, None, None]).astype(jnp.bfloat16)
    return dec_grad[None]


def solution(mesh):
    return jax.shard_map(
        body,
        mesh=mesh,
        in_specs=(
            P(("layer", "feat"), None, None),
            P(("layer", "feat"), None, None),
            P("layer", None, "feat"),
            P("layer", "feat"),
            P("layer", None, "feat", None),
            P("layer", None),
        ),
        out_specs=P("layer", None, "feat", None),
        check_vma=False,
    )
```

profile of v0, /device:TPU:1, one launch (start us, length us, event | category | flops | bytes accessed | tf_op | source)
XLA Modules:
  0.0 1513.7 jit_solution(9959380401361912224)
XLA Ops:
  6.5 0.0 copy-start
  6.5 0.0 all-gather.4.cloned.1.call-start
  6.5 0.9 copy.11
  7.4 8.9 all_to_all.24
  16.4 0.6 squeeze.10
  17.0 0.0 all-gather.4.cloned.1.call-update
  17.0 0.0 reduce-scatter.2.cloned.1.call-start
  17.1 80.4 %all-gather.4.cloned.1.call-done = bf16[512,2048]{1,0:T(8,128)(2,1)} async-done(((bf16[8,2048]{1,0:T(8,128)(2,1)}), bf16[512,2048]{1,0:T(8,128)(2,1)}) %all-gather.4.cloned.1.call-update) | async-done | bytes 2097168 | tf_op jit(solution)/shard_map/all_gather | solution.py:16
  97.4 0.0 copy-done
  97.5 2.3 fusion.4
  99.8 10.3 broadcast_multiply_fusion
  110.1 0.0 copy-start.1
  110.1 0.0 copy-start.2
  110.1 0.0 reduce-scatter.2.cloned.1.call-update
  110.1 0.0 all-gather.6.cloned.1.call-start
  110.1 0.7 copy-done.1
  110.8 8.1 all_to_all.25
  119.0 1277.4 %reduce-scatter.2.cloned.1.call-done = f32[8,2048]{1,0:T(8,128)} async-done(((f32[2048,2048]{1,0:T(8,128)}), f32[8,2048]{1,0:T(8,128)}) %reduce-scatter.2.cloned.1.call-update) | async-done | bytes 65552 | tf_op jit(solution)/shard_map/reduce_scatter | solution.py:29
  1396.4 0.0 copy-done.2
  1396.4 0.9 multiply_convert_fusion.1
  1397.2 10.1 all-gather
  1407.4 0.0 all-gather.6.cloned.1.call-update
  1407.4 85.4 %all-gather.6.cloned.1.call-done = bf16[4,512,2048]{2,1,0:T(8,128)(2,1)} async-done(((bf16[4,8,2048]{2,1,0:T(8,128)(2,1)}), bf16[4,512,2048]{2,1,0:T(8,128)(2,1)}) %all-gather.6.cloned.1.call-update) | async-done | bytes 8388624 | tf_op jit(solution)/shard_map/all_gather | solution.py:41
  1492.8 8.2 fusion.1
  1501.0 6.2 copy.13
  (4 shorter events, 0.1 us)
Async XLA Ops:
  6.5 90.9 %copy-start = (bf16[1,2048,256]{2,1,0:T(8,128)(2,1)S(1)}, bf16[1,2048,256]{2,1,0:T(8,128)(2,1)}, u32[]{:S(2)}) copy-start(bf16[1,2048,256]{2,1,0:T(8,128)(2,1)} %param.8) | copy-start | bytes 3145732
  6.5 90.9 %all-gather.4.cloned.1.call-start = ((), (), s32[]{:S(2)}) async-start(), calls=%async_computation.3 | async-start | bytes 2129920 | tf_op jit(solution)/shard_map/all_gather | solution.py:16
  17.0 1379.4 %reduce-scatter.2.cloned.1.call-start = ((), (), s32[]{:S(2)}) async-start(), calls=%async_computation.4 | async-start | bytes 16842752 | tf_op jit(solution)/shard_map/reduce_scatter | solution.py:29
  110.1 0.8 copy-start.1
  110.1 1286.3 %copy-start.2 = (f32[1,2048]{1,0:T(1,128)S(1)}, f32[1,2048]{1,0:T(1,128)}, u32[]{:S(2)}) copy-start(f32[1,2048]{1,0:T(1,128)} %param.11) | copy-start | bytes 24580
  110.1 1382.8 %all-gather.6.cloned.1.call-start = ((), (), s32[]{:S(2)}) async-start(), calls=%async_computation.5 | async-start | bytes 8519680 | tf_op jit(solution)/shard_map/all_gather | solution.py:41
Sparse Core Ops, SparseCore 0:
  17.1 80.2 all-gather.3
  110.2 1286.1 reduce-scatter.1
  1407.5 85.2 all-gather.5
where the time goes:
time: 1510 us
  waiting for transfers between devices  1440 us (95%)
  blocking collectives  27.2 us (2%)
  matrix products  20.8 us (1%)
    reduce_scatter x1, waiting for transfers between devices, body(): lax.psum_scatter(partials.reshape(layers * total_tokens, width), ('layer'...  1280 us
    all_gather x1, waiting for transfers between devices, body(): lax.all_gather(stacked, 'feat', axis=1, tiled=True)  85.4 us
    all_gather x1, waiting for transfers between devices, body(): inputs = lax.all_gather(moved_x[:, 0, :], 'feat', axis=0, tiled=True)  80.4 us
  transfers between devices with their start and end apart: 3, of which 3 were waited for; matrix products, arithmetic and copies ran while one was open for 0% of the time, Pallas kernels for 0%

commit v1 on v0

v1 whole, which is shorter than its diff:
```python
import functools
import math

import jax
import jax.numpy as jnp
from jax import lax
from jax.experimental import pallas as pl
from jax.experimental.pallas import tpu as pltpu
from jax.sharding import Mesh
from jax.sharding import PartitionSpec as P

BF = jnp.bfloat16
F32 = jnp.float32
NX, NZ, NY, NC = 4, 8, 4, 2
XZ = NX * NZ
VMEM_LIMIT = 48 * 1024 * 1024


def shift(value, axis, step):
    size = lax.axis_size(axis)
    return lax.ppermute(value, axis, [(i, (i + step) % size) for i in range(size)])


def encoder_kernel(x0, x1, x2, x3, others, weight, bias, place, out, rows):
    chunk = x0.shape[0]
    for i, ref in enumerate((x0, x1, x2, x3)):
        rows[i * chunk:(i + 1) * chunk, :] = ref[...]
        rows[(NY + i) * chunk:(NY + i + 1) * chunk, :] = others[i]
    preact = jnp.dot(rows[...], weight[...], preferred_element_type=F32) + bias[...]
    activity = jnp.maximum(preact, 0.0).astype(BF)
    out[...] = jnp.dot(place[...], activity, preferred_element_type=F32).astype(BF)


def encode(own, others, weight, bias, place):
    tokens = place.shape[0]
    return pl.pallas_call(
        encoder_kernel,
        out_shape=jax.ShapeDtypeStruct((tokens, weight.shape[1]), BF),
        scratch_shapes=[pltpu.VMEM((tokens, weight.shape[0]), BF)],
        compiler_params=pltpu.CompilerParams(vmem_limit_bytes=VMEM_LIMIT),
        name="encode",
    )(*own, others, weight, bias, place)


def decoder_kernel(layer, r0, r1, r2, r3, a0, a1, a2, a3, others, bias, out):
    sink = pl.program_id(0)

    @pl.when(sink >= layer[0])
    def _():
        total = jnp.zeros(a0.shape[:1] + r0.shape[3:], F32)
        for i, (r, a) in enumerate(((r0, a0), (r1, a1), (r2, a2), (r3, a3))):
            total += jnp.dot(a[...], r[0, 0], preferred_element_type=F32)
            total += jnp.dot(others[i], r[1, 0], preferred_element_type=F32)
        total += bias[0]
        out[...] = total.astype(BF).reshape(out.shape)

    @pl.when(sink < layer[0])
    def _():
        out[...] = jnp.zeros(out.shape, BF)


def decode(layer, weights, own, others, bias):
    sinks, feats, cols = weights[0].shape[1:]
    tokens = own[0].shape[0]
    part = tokens // XZ
    return pl.pallas_call(
        decoder_kernel,
        grid_spec=pltpu.PrefetchScalarGridSpec(
            num_scalar_prefetch=1,
            grid=(sinks,),
            in_specs=[pl.BlockSpec((2, 1, feats, cols), lambda m, _: (0, m, 0, 0))] * NY
            + [pl.BlockSpec((tokens, feats), lambda m, _: (0, 0))] * NY
            + [pl.BlockSpec((NY, tokens, feats), lambda m, _: (0, 0, 0))]
            + [pl.BlockSpec((1, 1, cols), lambda m, _: (m, 0, 0))],
            out_specs=pl.BlockSpec((XZ, 1, part, cols), lambda m, _: (0, m, 0, 0)),
        ),
        out_shape=jax.ShapeDtypeStruct((XZ, sinks, part, cols), BF),
        compiler_params=pltpu.CompilerParams(vmem_limit_bytes=VMEM_LIMIT),
        name="decode",
    )(layer, *weights, *own, others, bias)


def gradient_kernel(place, c0, c1, c2, c3, others, activity, out):
    sink = pl.program_id(0)
    layer, y, core = place[0], place[1], place[2]
    cols = c0.shape[3]

    @pl.when(sink >= layer)
    def _():
        for i, c in enumerate((c0, c1, c2, c3)):
            quarter = lax.rem(y + NY - i, NY)
            for half, block in ((core, c[:, 0]), (1 - core, others[i, :, 0])):
                start = pl.multiple_of((half * NY + quarter) * cols, cols)
                grad = jnp.dot(activity[...], block.reshape(-1, cols), preferred_element_type=F32)
                out[0, :, pl.ds(start, cols)] = grad.astype(BF)

    @pl.when(sink < layer)
    def _():
        out[...] = jnp.zeros(out.shape, BF)


def gradient(place, own, others, activity):
    slots, sinks, part, cols = own[0].shape
    feats, tokens = activity.shape
    return pl.pallas_call(
        gradient_kernel,
        grid_spec=pltpu.PrefetchScalarGridSpec(
            num_scalar_prefetch=1,
            grid=(sinks,),
            in_specs=[pl.BlockSpec((slots, 1, part, cols), lambda m, _: (0, m, 0, 0))] * NY
            + [pl.BlockSpec((NY, slots, 1, part, cols), lambda m, _: (0, 0, m, 0, 0))]
            + [pl.BlockSpec((feats, tokens), lambda m, _: (0, 0))],
            out_specs=pl.BlockSpec((1, feats, NY * NC * cols), lambda m, _: (m, 0, 0)),
        ),
        out_shape=jax.ShapeDtypeStruct((sinks, feats, NY * NC * cols), BF),
        compiler_params=pltpu.CompilerParams(vmem_limit_bytes=VMEM_LIMIT),
        name="gradient",
    )(place, *own, others, activity)


def body(resid, target, enc_weight, enc_bias, dec_weight, dec_bias):
    x, z, y, core = (lax.axis_index(a) for a in ("x", "z", "y", "c"))
    mine, layers, width = resid.shape
    tokens = mine * XZ * NY * NC
    half, cols = width // NC, width // (NC * NY)
    factor = 1.0 / math.sqrt(tokens)
    weight = dec_weight[0]
    feats = weight.shape[1]

    keep = lax.dynamic_slice_in_dim(weight, core * half, half, axis=2)
    give = lax.dynamic_slice_in_dim(weight, (1 - core) * half, half, axis=2)
    both = jnp.stack([keep, shift(give, "c", 1)])
    weights = []
    for step in range(NY):
        piece = lax.dynamic_slice_in_dim(both, lax.rem(y + step, NY) * cols, cols, axis=3)
        weights.append(piece if step == 0 else shift(piece, "y", step))

    rows = jnp.broadcast_to(resid.transpose(1, 0, 2)[:, None], (layers, NZ, mine, width))
    rows = lax.all_to_all(rows.reshape(XZ * mine, width), ("x", "z"), 0, 0, tiled=True)
    own = [rows] + [shift(rows, "y", step) for step in range(1, NY)]
    others = shift(jnp.stack(own), "c", 1)
    r = jnp.arange(tokens)
    r_half, r_step, r_slot, r_i = r // (tokens // 2), r // (tokens // 8) % NY, r // mine % XZ, r % mine
    r_core = jnp.where(r_half == 0, core, 1 - core)
    token = ((r_slot * NY + (y + NY - r_step) % NY) * NC + r_core) * mine + r_i
    place = (jnp.arange(tokens)[:, None] == token[None, :]).astype(BF)
    activity = encode(own, others, enc_weight[0], enc_bias, place)

    acts = [activity] + [shift(activity, "y", step) for step in range(1, NY)]
    act_others = shift(jnp.stack(acts), "c", 1)
    column = core * half + y * cols
    bias = lax.dynamic_slice_in_dim(dec_bias[0], column, cols)
    bias = jnp.where(((jnp.arange(layers) == x) & (z == 0))[:, None, None], bias[None, None, :], 0.0)
    parts = decode(x.reshape(1), weights, acts, act_others, bias)

    wanted = target.reshape(mine, layers, NC, NY, cols).transpose(3, 2, 1, 0, 4)
    wanted = lax.all_to_all(wanted.reshape(NY * NC, layers, mine, cols), ("y", "c"), 0, 0, tiled=True)
    wanted = wanted.transpose(1, 0, 2, 3).reshape(layers, NY * NC * mine, cols)
    got = lax.all_to_all(parts, ("x", "z"), 0, 0, tiled=True)
    misfit = jnp.sum(got.astype(F32), axis=0) - wanted.astype(F32)
    cotangent = (misfit * factor).astype(BF)

    copies = jnp.broadcast_to(cotangent[None], (XZ,) + cotangent.shape)
    block = lax.all_to_all(copies, ("x", "z"), 0, 0, tiled=True)
    blocks = [block] + [shift(block, "y", step) for step in range(1, NY)]
    block_others = shift(jnp.stack(blocks), "c", 1)
    grads = gradient(jnp.stack([x, y, core]), blocks, block_others, activity.T)
    return grads[None]


def solution(mesh):
    fine = Mesh(mesh.devices.reshape(NX, NZ, NY, NC), ("x", "z", "y", "c"))
    feat = ("z", "y", "c")
    return jax.shard_map(
        body,
        mesh=fine,
        in_specs=(
            P(("x",) + feat, None, None),
            P(("x",) + feat, None, None),
            P("x", None, feat),
            P("x", feat),
            P("x", None, feat, None),
            P("x", None),
        ),
        out_specs=P("x", None, feat, None),
        check_vma=False,
    )
```

time: 1510 us -> 261 us (0.17)
  waiting for transfers between devices: 1440 us -> 153 us
  starting transfers between devices: 0.09 us -> 35.8 us
  matrix products: 20.8 us -> 0 us
    reduce_scatter x1 -> x0, waiting for transfers between devices: 1280 us -> none  [body(): lax.psum_scatter(partials.reshape(layers * total_tokens, width), ('layer'...]
    all_gather x2 -> x0, waiting for transfers between devices: 166 us -> none  [the longest x1 85.4 us: body(): lax.all_gather(stacked, 'feat', axis=1, tiled=True)]
    ppermute x0 -> x16, waiting for transfers between devices: none -> 125 us  [shift(): lax.ppermute(value, axis, [(i, (i + step) % size) for i in range(size)])]
    all_to_all x0 -> x3, waiting for transfers between devices: none -> 28.6 us  [the longest x1 24.7 us: body(): got = lax.all_to_all(parts, ('x', 'z'), 0, 0, tiled=True)]
    all_to_all x0 -> x3, starting transfers between devices: none -> 22.5 us  [the longest x1 11.9 us: body(): lax.all_to_all(rows.reshape(XZ * mine, width), ('x', 'z'), 0, 0, tiled=True)]
    dot_general x3 -> x0, matrix products: 20.8 us -> none  [the longest x1 10.3 us: body(): jnp.einsum('tf,mfd->mtd', activity, dec_weight[0], preferred_element_type...]
    all_to_all x2 -> x1, blocking collectives: 17 us -> 33.1 us  [body(): block = lax.all_to_all(copies, ('x', 'z'), 0, 0, tiled=True)]
  transfers between devices with their start and end apart: 3 -> 19, of which waited for: 3 -> 15; matrix products, arithmetic and copies ran while one was open for 0% -> 5% of each run, Pallas kernels for 0% -> 3%
where the time goes in v1:
time: 261 us; the launch traced here: 260 us
  waiting for transfers between devices  153 us (59%)
  starting transfers between devices  35.8 us (14%)
  blocking collectives  33.1 us (13%)
  local copies, waits for them, and re-layouts  15.3 us (6%)
  Pallas kernels  13.6 us (5%)
  other arithmetic  9.14 us (4%)
    ppermute x16, waiting for transfers between devices, shift(): lax.ppermute(value, axis, [(i, (i + step) % size) for i in range(size)])  125 us
    all_to_all x1, blocking collectives, body(): block = lax.all_to_all(copies, ('x', 'z'), 0, 0, tiled=True)  33.1 us
    all_to_all x1, waiting for transfers between devices, body(): got = lax.all_to_all(parts, ('x', 'z'), 0, 0, tiled=True)  24.7 us
    ppermute x16, starting transfers between devices, shift(): lax.ppermute(value, axis, [(i, (i + step) % size) for i in range(size)])  13.3 us
    all_to_all x1, starting transfers between devices, body(): lax.all_to_all(rows.reshape(XZ * mine, width), ('x', 'z'), 0, 0, tiled=True)  11.9 us
    unnamed x34, local copies, waits for them, and re-layouts  6.97 us
    pallas_call x1, Pallas kernels, gradient(): pl.pallas_call(gradient_kernel, grid_spec=pltpu.PrefetchScalarGridSpec(nu...  6.95 us
    all_to_all x1, starting transfers between devices, body(): got = lax.all_to_all(parts, ('x', 'z'), 0, 0, tiled=True)  5.59 us
  transfers between devices with their start and end apart: 19, of which 15 were waited for; matrix products, arithmetic and copies ran while one was open for 5% of the time, Pallas kernels for 3%

profile of v1, /device:TPU:1, one launch (start us, length us, event | category | flops | bytes accessed | tf_op | source)
XLA Modules:
  0.0 260.1 jit_solution(7159550963366617625)
XLA Ops:
  0.0 0.8 copy.17
  0.8 0.9 broadcast_in_dim.47
  1.7 11.9 %all-to-all-start = ((bf16[32,2,2048]{2,1,0:T(2,128)(2,1)}), bf16[32,2,2048]{2,1,0:T(2,128)(2,1)S(1)}, u32[]{:S(2)}, u32[]{:S(2)}) async-start(bf16[32,2,2048]{2,1,0:T(2,128)(2,1)} %bitcast.6), calls=%async_computation | async-start | bytes 524288 | tf_op jit(solution)/shard_map/all_to_all | solution.py:139
  13.6 0.0 copy-start.3
  13.6 0.0 copy-start.15
  13.6 4.8 %dynamic-slice_bitcast_fusion = (bf16[4,256,1024]{2,1,0:T(8,128)(2,1)}, bf16[1,4,256,1024]{3,2,1,0:T(8,128)(2,1)}) fusion(bf16[1,4,256,2048]{3,2,1,0:T(8,128)(2,1)} %param.10, s32[]{:T(128)S(6)} %select_n.92, s32[]{:T(128)S(6)} %select_n.91), kind=kLoop, calls=%fused_computation.10 | loop fusion | bytes 8388616 | tf_op jit(solution)/shard_map/dynamic_slice | solution.py:131
  18.4 1.0 collective-permute-start
  19.3 3.9 %all-to-all-done = bf16[32,2,2048]{2,1,0:T(2,128)(2,1)S(1)} async-done(((bf16[32,2,2048]{2,1,0:T(2,128)(2,1)}), bf16[32,2,2048]{2,1,0:T(2,128)(2,1)S(1)}, u32[]{:S(2)}, u32[]{:S(2)}) %all-to-all-start) | async-done | bytes 262176 | tf_op jit(solution)/shard_map/all_to_all | solution.py:139
  23.2 0.1 all_to_all.18.x0
  23.4 2.8 %collective-permute-start.6 = (bf16[64,2048]{1,0:T(8,128)(2,1)S(1)}, bf16[64,2048]{1,0:T(8,128)(2,1)S(1)}, u32[]{:S(2)}, u32[]{:S(2)}) collective-permute-start(bf16[64,2048]{1,0:T(8,128)(2,1)S(1)} %all_to_all.18.x0), channel_id=1, source_target_pairs={{0,6},{2,0},{4,2},{6,4},{1,7},{3,1},{5,3},{7,5},{8,14},{10,8},{12,... | collective-permute-start | bytes 786440 | tf_op jit(solution)/shard_map/ppermute | solution.py:21
  26.2 0.3 collective-permute-start.5
  26.5 0.7 collective-permute-start.4
  27.2 0.1 stack.70
  27.3 5.5 %collective-permute-done.6.x3 = bf16[64,2048]{1,0:T(8,128)(2,1)S(1)} collective-permute-done((bf16[64,2048]{1,0:T(8,128)(2,1)S(1)}, bf16[64,2048]{1,0:T(8,128)(2,1)S(1)}, u32[]{:S(2)}, u32[]{:S(2)}) %collective-permute-start.6) | collective-permute-done | bytes 262176 | tf_op jit(solution)/shard_map/ppermute | solution.py:21
  32.8 0.2 collective-permute-done.5.x2
  33.0 6.7 %collective-permute-done.4.x1 = bf16[64,2048]{1,0:T(8,128)(2,1)S(1)} collective-permute-done((bf16[64,2048]{1,0:T(8,128)(2,1)S(1)}, bf16[64,2048]{1,0:T(8,128)(2,1)S(1)}, u32[]{:S(2)}, u32[]{:S(2)}) %collective-permute-start.4) | collective-permute-done | bytes 262176 | tf_op jit(solution)/shard_map/ppermute | solution.py:21
  39.7 1.1 pad_maximum_fusion.1
  40.8 2.3 collective-permute-start.7
  43.2 0.1 fusion.4.place
  43.3 2.3 collective-permute-done.7.others
  45.7 0.9 copy-done.12
  46.6 0.9 copy-done.14
  47.6 1.2 encode.1.a0
  48.7 0.4 collective-permute-start.10
  49.2 0.3 collective-permute-start.9
  49.5 0.8 collective-permute-start.8
  50.3 6.0 %collective-permute-done.10.a3 = bf16[512,256]{1,0:T(8,128)(2,1)S(1)} collective-permute-done((bf16[512,256]{1,0:T(8,128)(2,1)S(1)}, bf16[512,256]{1,0:T(8,128)(2,1)S(1)}, u32[]{:S(2)}, u32[]{:S(2)}) %collective-permute-start.10) | collective-permute-done | bytes 262176 | tf_op jit(solution)/shard_map/ppermute | solution.py:21
  56.3 1.6 collective-permute-done.9.a2
  57.9 6.6 %collective-permute-done.8.a1 = bf16[512,256]{1,0:T(8,128)(2,1)S(1)} collective-permute-done((bf16[512,256]{1,0:T(8,128)(2,1)S(1)}, bf16[512,256]{1,0:T(8,128)(2,1)S(1)}, u32[]{:S(2)}, u32[]{:S(2)}) %collective-permute-start.8) | collective-permute-done | bytes 262176 | tf_op jit(solution)/shard_map/ppermute | solution.py:21
  64.5 1.1 pad_maximum_fusion.2
  65.6 0.5 collective-permute-start.11
  66.2 0.0 copy-start.16
  66.2 4.0 %fusion = (bf16[2,4,256,256]{3,2,1,0:T(8,128)(2,1)}, bf16[2,4,256,256]{3,2,1,0:T(8,128)(2,1)S(1)}, bf16[2,4,256,256]{3,2,1,0:T(8,128)(2,1)}, bf16[2,4,256,256]{3,2,1,0:T(8,128)(2,1)}) fusion(s32[]{:T(128)S(6)} %select_n.96, bf16[1,4,256,1024]{3,2,1,0:T(8,128)(2,1)} %get-tuple-element.10, bf16[1,4,256,1024]{3,2,1,0:T(8,128)(2,1)} %bitcast.4, ...), kind=kLoop, calls=%fused_computation.11 | loop fusion | flops 8388608 | bytes 8388624 | tf_op jit(solution)/shard_map/stack | solution.py:132
  70.2 0.6 collective-permute-start.3
  70.8 0.9 collective-permute-start.1
  71.7 0.3 collective-permute-start.2
  72.0 0.6 copy.18
  72.7 5.1 %all-to-all-start.2 = ((bf16[8,4,2,256]{3,2,1,0:T(2,128)(2,1)}), bf16[8,4,2,256]{3,2,1,0:T(2,128)(2,1)S(1)}, u32[]{:S(2)}, u32[]{:S(2)}) async-start(bf16[8,4,2,256]{3,2,1,0:T(2,128)(2,1)} %bitcast.17), calls=%async_computation.2 | async-start | bytes 65536 | tf_op jit(solution)/shard_map/all_to_all | solution.py:157
  77.7 0.1 broadcast_select_fusion.bias
  77.8 17.5 %collective-permute-done.3.r3 = bf16[2,4,256,256]{3,2,1,0:T(8,128)(2,1)} collective-permute-done((bf16[2,4,256,256]{3,2,1,0:T(8,128)(2,1)}, bf16[2,4,256,256]{3,2,1,0:T(8,128)(2,1)}, u32[]{:S(2)}, u32[]{:S(2)}) %collective-permute-start.3) | collective-permute-done | bytes 1048608 | tf_op jit(solution)/shard_map/ppermute | solution.py:21
  95.3 24.0 %collective-permute-done.1.r1 = bf16[2,4,256,256]{3,2,1,0:T(8,128)(2,1)S(1)} collective-permute-done((bf16[2,4,256,256]{3,2,1,0:T(8,128)(2,1)}, bf16[2,4,256,256]{3,2,1,0:T(8,128)(2,1)S(1)}, u32[]{:S(2)}, u32[]{:S(2)}) %collective-permute-start.1) | collective-permute-done | bytes 1048608 | tf_op jit(solution)/shard_map/ppermute | solution.py:21
  119.3 0.9 copy-done.6
  120.2 0.9 copy-done.8
  121.2 0.9 copy-done.10
  122.1 5.4 %decode.1 = bf16[32,4,16,256]{3,2,1,0:T(8,128)(2,1)} custom-call(s32[1]{0:T(128)} %bitcast.layer, bf16[2,4,256,256]{3,2,1,0:T(8,128)(2,1)S(1)} %get-tuple-element.6.r0, bf16[2,4,256,256]{3,2,1,0:T(8,128)(2,1)S(1)} %collective-permute-done.1.r1, bf16[2,4,256,256]{3,2,1,0:T(8,128)(2,1)S(1)} %collective-permute-done.2.r2, ...), custom_call_target="tpu_custom_call" | custom-call | tf_op jit(solution)/shard_map/decode/pallas_call | solution.py:66
  127.6 5.6 %all-to-all-start.1 = ((bf16[32,4,16,256]{3,2,1,0:T(8,128)(2,1)}), bf16[32,4,16,256]{3,2,1,0:T(8,128)(2,1)S(1)}, u32[]{:S(2)}, u32[]{:S(2)}) async-start(bf16[32,4,16,256]{3,2,1,0:T(8,128)(2,1)} %decode.1), calls=%async_computation.1 | async-start | bytes 2097152 | tf_op jit(solution)/shard_map/all_to_all | solution.py:159
  133.2 24.7 %all-to-all-done.1 = bf16[32,4,16,256]{3,2,1,0:T(8,128)(2,1)S(1)} async-done(((bf16[32,4,16,256]{3,2,1,0:T(8,128)(2,1)}), bf16[32,4,16,256]{3,2,1,0:T(8,128)(2,1)S(1)}, u32[]{:S(2)}, u32[]{:S(2)}) %all-to-all-start.1) | async-done | bytes 1048608 | tf_op jit(solution)/shard_map/all_to_all | solution.py:159
  157.9 0.2 convert_reduce_fusion
  158.1 0.1 broadcast_in_dim.53
  158.2 33.1 %all_to_all.26.c0 = bf16[32,4,16,256]{3,2,1,0:T(8,128)(2,1)S(1)} all-to-all(bf16[32,4,16,256]{3,2,1,0:T(8,128)(2,1)S(1)} %broadcast_in_dim.53), channel_id=1, replica_groups=mesh['x'=4,'z'=8,'y'=4,'c'=2] {'x','z'}, dimensions={0} | all-to-all | bytes 2097152 | tf_op jit(solution)/shard_map/all_to_all | solution.py:164
  191.3 0.7 collective-permute-start.14
  192.0 0.3 collective-permute-start.13
  192.2 0.9 collective-permute-start.12
  193.1 17.8 %collective-permute-done.14.c3 = bf16[32,4,16,256]{3,2,1,0:T(8,128)(2,1)S(1)} collective-permute-done((bf16[32,4,16,256]{3,2,1,0:T(8,128)(2,1)S(1)}, bf16[32,4,16,256]{3,2,1,0:T(8,128)(2,1)S(1)}, u32[]{:S(2)}, u32[]{:S(2)}) %collective-permute-start.14) | collective-permute-done | bytes 1048608 | tf_op jit(solution)/shard_map/ppermute | solution.py:21
  210.9 2.0 collective-permute-done.13.c2
  212.9 28.1 %collective-permute-done.12.c1 = bf16[32,4,16,256]{3,2,1,0:T(8,128)(2,1)S(1)} collective-permute-done((bf16[32,4,16,256]{3,2,1,0:T(8,128)(2,1)S(1)}, bf16[32,4,16,256]{3,2,1,0:T(8,128)(2,1)S(1)}, u32[]{:S(2)}, u32[]{:S(2)}) %collective-permute-start.12) | collective-permute-done | bytes 1048608 | tf_op jit(solution)/shard_map/ppermute | solution.py:21
  241.0 2.4 pad_maximum_fusion
  243.4 0.5 collective-permute-start.15
  243.9 0.1 pad_add_fusion.place
  243.9 0.8 copy.21
  244.8 6.2 %collective-permute-done.15.others = bf16[4,32,4,16,256]{4,3,2,1,0:T(8,128)(2,1)} collective-permute-done((bf16[4,32,4,16,256]{4,3,2,1,0:T(8,128)(2,1)}, bf16[4,32,4,16,256]{4,3,2,1,0:T(8,128)(2,1)}, u32[]{:S(2)}, u32[]{:S(2)}) %collective-permute-start.15) | collective-permute-done | bytes 4194336 | tf_op jit(solution)/shard_map/ppermute | solution.py:21
  251.0 1.2 copy-done.2
  252.2 0.9 copy-done.4
  253.2 6.9 %gradient.1 = bf16[4,256,2048]{2,1,0:T(8,128)(2,1)} custom-call(s32[3]{0:T(128)S(1)} %pad_add_fusion.place, bf16[32,4,16,256]{3,2,1,0:T(8,128)(2,1)S(1)} %all_to_all.26.c0, bf16[32,4,16,256]{3,2,1,0:T(8,128)(2,1)S(1)} %copy-done.2, bf16[32,4,16,256]{3,2,1,0:T(8,128)(2,1)S(1)} %collective-permute-done.13.c2, ...), custom_call_target="tpu_custom_call" | custom-call | tf_op jit(solution)/shard_map/gradient/pallas_call | solution.py:105
  (35 shorter events, 0.2 us)
Async XLA Ops:
  0.0 77.7 %copy-start = (f32[1,2048]{1,0:T(1,128)S(1)}, f32[1,2048]{1,0:T(1,128)}, u32[]{:S(2)}) copy-start(f32[1,2048]{1,0:T(1,128)} %param.11) | copy-start | bytes 24580
  1.7 21.6 %all-to-all-start = ((bf16[32,2,2048]{2,1,0:T(2,128)(2,1)}), bf16[32,2,2048]{2,1,0:T(2,128)(2,1)S(1)}, u32[]{:S(2)}, u32[]{:S(2)}) async-start(bf16[32,2,2048]{2,1,0:T(2,128)(2,1)} %bitcast.6), calls=%async_computation | async-start | bytes 524288 | tf_op jit(solution)/shard_map/all_to_all | solution.py:139
  13.6 32.1 %copy-start.3 = (bf16[1,2048,256]{2,1,0:T(8,128)(2,1)S(1)}, bf16[1,2048,256]{2,1,0:T(8,128)(2,1)}, u32[]{:S(2)}) copy-start(bf16[1,2048,256]{2,1,0:T(8,128)(2,1)} %param.8) | copy-start | bytes 3145732
  13.6 32.1 %copy-start.15 = (f32[1,256]{1,0:T(1,128)S(1)}, f32[1,256]{1,0:T(1,128)}, u32[]{:S(2)}) copy-start(f32[1,256]{1,0:T(1,128)} %bias.1) | copy-start | bytes 3076
  18.4 47.7 %collective-permute-start = (bf16[4,256,1024]{2,1,0:T(8,128)(2,1)}, bf16[4,256,1024]{2,1,0:T(8,128)(2,1)}, u32[]{:S(2)}, u32[]{:S(2)}) collective-permute-start(bf16[4,256,1024]{2,1,0:T(8,128)(2,1)} %get-tuple-element.9), channel_id=1, source_target_pairs={{0,1},{1,0},{2,3},{3,2},{4,5},{5,4},{6,7},{7,6},{8,9},{9,8},{10,11... | collective-permute-start | bytes 6291464 | tf_op jit(solution)/shard_map/ppermute | solution.py:21
  23.4 9.5 %collective-permute-start.6 = (bf16[64,2048]{1,0:T(8,128)(2,1)S(1)}, bf16[64,2048]{1,0:T(8,128)(2,1)S(1)}, u32[]{:S(2)}, u32[]{:S(2)}) collective-permute-start(bf16[64,2048]{1,0:T(8,128)(2,1)S(1)} %all_to_all.18.x0), channel_id=1, source_target_pairs={{0,6},{2,0},{4,2},{6,4},{1,7},{3,1},{5,3},{7,5},{8,14},{10,8},{12,... | collective-permute-start | bytes 786440 | tf_op jit(solution)/shard_map/ppermute | solution.py:21
  26.2 6.8 %collective-permute-start.5 = (bf16[64,2048]{1,0:T(8,128)(2,1)S(1)}, bf16[64,2048]{1,0:T(8,128)(2,1)S(1)}, u32[]{:S(2)}, u32[]{:S(2)}) collective-permute-start(bf16[64,2048]{1,0:T(8,128)(2,1)S(1)} %all_to_all.18.x0), channel_id=1, source_target_pairs={{0,4},{2,6},{4,0},{6,2},{1,5},{3,7},{5,1},{7,3},{8,12},{10,14},{12... | collective-permute-start | bytes 786440 | tf_op jit(solution)/shard_map/ppermute | solution.py:21
  26.5 13.2 %collective-permute-start.4 = (bf16[64,2048]{1,0:T(8,128)(2,1)S(1)}, bf16[64,2048]{1,0:T(8,128)(2,1)S(1)}, u32[]{:S(2)}, u32[]{:S(2)}) collective-permute-start(bf16[64,2048]{1,0:T(8,128)(2,1)S(1)} %all_to_all.18.x0), channel_id=1, source_target_pairs={{0,2},{2,4},{4,6},{6,0},{1,3},{3,5},{5,7},{7,1},{8,10},{10,12},{12... | collective-permute-start | bytes 786440 | tf_op jit(solution)/shard_map/ppermute | solution.py:21
  33.0 12.7 %copy-start.11 = (bf16[64,2048]{1,0:T(8,128)(2,1)}, bf16[64,2048]{1,0:T(8,128)(2,1)S(1)}, u32[]{:S(2)}) copy-start(bf16[64,2048]{1,0:T(8,128)(2,1)S(1)} %collective-permute-done.5.x2) | copy-start | bytes 786436
  39.7 3.5 %copy-start.13 = (bf16[64,2048]{1,0:T(8,128)(2,1)}, bf16[64,2048]{1,0:T(8,128)(2,1)S(1)}, u32[]{:S(2)}) copy-start(bf16[64,2048]{1,0:T(8,128)(2,1)S(1)} %collective-permute-done.4.x1) | copy-start | bytes 786436
  40.8 4.8 %collective-permute-start.7 = (bf16[4,64,2048]{2,1,0:T(8,128)(2,1)}, bf16[4,64,2048]{2,1,0:T(8,128)(2,1)S(1)}, u32[]{:S(2)}, u32[]{:S(2)}) collective-permute-start(bf16[4,64,2048]{2,1,0:T(8,128)(2,1)} %pad_maximum_fusion.1), channel_id=1, source_target_pairs={{0,1},{1,0},{2,3},{3,2},{4,5},{5,4},{6,7},{7,6},{8,9},{9,8},{10,11... | collective-permute-start | bytes 3145736 | tf_op jit(solution)/shard_map/ppermute | solution.py:21
  45.7 1.0 copy-start.12
  46.6 0.9 copy-start.14
  48.7 7.6 %collective-permute-start.10 = (bf16[512,256]{1,0:T(8,128)(2,1)S(1)}, bf16[512,256]{1,0:T(8,128)(2,1)S(1)}, u32[]{:S(2)}, u32[]{:S(2)}) collective-permute-start(bf16[512,256]{1,0:T(8,128)(2,1)S(1)} %encode.1.a0), channel_id=1, source_target_pairs={{0,6},{2,0},{4,2},{6,4},{1,7},{3,1},{5,3},{7,5},{8,14},{10,8},{12,... | collective-permute-start | bytes 786440 | tf_op jit(solution)/shard_map/ppermute | solution.py:21
  49.2 8.7 %collective-permute-start.9 = (bf16[512,256]{1,0:T(8,128)(2,1)S(1)}, bf16[512,256]{1,0:T(8,128)(2,1)S(1)}, u32[]{:S(2)}, u32[]{:S(2)}) collective-permute-start(bf16[512,256]{1,0:T(8,128)(2,1)S(1)} %encode.1.a0), channel_id=1, source_target_pairs={{0,4},{2,6},{4,0},{6,2},{1,5},{3,7},{5,1},{7,3},{8,12},{10,14},{12... | collective-permute-start | bytes 786440 | tf_op jit(solution)/shard_map/ppermute | solution.py:21
  49.5 15.0 %collective-permute-start.8 = (bf16[512,256]{1,0:T(8,128)(2,1)S(1)}, bf16[512,256]{1,0:T(8,128)(2,1)S(1)}, u32[]{:S(2)}, u32[]{:S(2)}) collective-permute-start(bf16[512,256]{1,0:T(8,128)(2,1)S(1)} %encode.1.a0), channel_id=1, source_target_pairs={{0,2},{2,4},{4,6},{6,0},{1,3},{3,5},{5,7},{7,1},{8,10},{10,12},{12... | collective-permute-start | bytes 786440 | tf_op jit(solution)/shard_map/ppermute | solution.py:21
  56.3 9.8 %copy-start.5 = (bf16[512,256]{1,0:T(8,128)(2,1)}, bf16[512,256]{1,0:T(8,128)(2,1)S(1)}, u32[]{:S(2)}) copy-start(bf16[512,256]{1,0:T(8,128)(2,1)S(1)} %collective-permute-done.10.a3) | copy-start | bytes 786436
  57.9 8.2 %copy-start.7 = (bf16[512,256]{1,0:T(8,128)(2,1)}, bf16[512,256]{1,0:T(8,128)(2,1)S(1)}, u32[]{:S(2)}) copy-start(bf16[512,256]{1,0:T(8,128)(2,1)S(1)} %collective-permute-done.9.a2) | copy-start | bytes 786436
  64.5 1.6 copy-start.9
  65.6 12.2 %collective-permute-start.11 = (bf16[4,512,256]{2,1,0:T(8,128)(2,1)}, bf16[4,512,256]{2,1,0:T(8,128)(2,1)}, u32[]{:S(2)}, u32[]{:S(2)}) collective-permute-start(bf16[4,512,256]{2,1,0:T(8,128)(2,1)} %pad_maximum_fusion.2), channel_id=1, source_target_pairs={{0,1},{1,0},{2,3},{3,2},{4,5},{5,4},{6,7},{7,6},{8,9},{9,8},{10,11... | collective-permute-start | bytes 3145736 | tf_op jit(solution)/shard_map/ppermute | solution.py:21
  66.2 5.8 %copy-start.16 = (bf16[2,4,2048]{2,1,0:T(4,128)(2,1)S(1)}, bf16[2,4,2048]{2,1,0:T(4,128)(2,1)}, u32[]{:S(2)}) copy-start(bf16[2,4,2048]{2,1,0:T(4,128)(2,1)} %param.7) | copy-start | bytes 98308
  70.2 25.1 %collective-permute-start.3 = (bf16[2,4,256,256]{3,2,1,0:T(8,128)(2,1)}, bf16[2,4,256,256]{3,2,1,0:T(8,128)(2,1)}, u32[]{:S(2)}, u32[]{:S(2)}) collective-permute-start(bf16[2,4,256,256]{3,2,1,0:T(8,128)(2,1)} %get-tuple-element.5), channel_id=1, source_target_pairs={{0,6},{2,0},{4,2},{6,4},{1,7},{3,1},{5,3},{7,5},{8,14},{10,8},{12,... | collective-permute-start | bytes 3145736 | tf_op jit(solution)/shard_map/ppermute | solution.py:21
  70.8 48.5 %collective-permute-start.1 = (bf16[2,4,256,256]{3,2,1,0:T(8,128)(2,1)}, bf16[2,4,256,256]{3,2,1,0:T(8,128)(2,1)S(1)}, u32[]{:S(2)}, u32[]{:S(2)}) collective-permute-start(bf16[2,4,256,256]{3,2,1,0:T(8,128)(2,1)} %get-tuple-element.7), channel_id=1, source_target_pairs={{0,2},{2,4},{4,6},{6,0},{1,3},{3,5},{5,7},{7,1},{8,10},{10,12},{12... | collective-permute-start | bytes 3145736 | tf_op jit(solution)/shard_map/ppermute | solution.py:21
  71.7 47.6 %collective-permute-start.2 = (bf16[2,4,256,256]{3,2,1,0:T(8,128)(2,1)}, bf16[2,4,256,256]{3,2,1,0:T(8,128)(2,1)S(1)}, u32[]{:S(2)}, u32[]{:S(2)}) collective-permute-start(bf16[2,4,256,256]{3,2,1,0:T(8,128)(2,1)} %get-tuple-element.8), channel_id=1, source_target_pairs={{0,4},{2,6},{4,0},{6,2},{1,5},{3,7},{5,1},{7,3},{8,12},{10,14},{12... | collective-permute-start | bytes 3145736 | tf_op jit(solution)/shard_map/ppermute | solution.py:21
  72.7 54.9 %all-to-all-start.2 = ((bf16[8,4,2,256]{3,2,1,0:T(2,128)(2,1)}), bf16[8,4,2,256]{3,2,1,0:T(2,128)(2,1)S(1)}, u32[]{:S(2)}, u32[]{:S(2)}) async-start(bf16[8,4,2,256]{3,2,1,0:T(2,128)(2,1)} %bitcast.17), calls=%async_computation.2 | async-start | bytes 65536 | tf_op jit(solution)/shard_map/all_to_all | solution.py:157
  119.3 1.0 copy-start.6
  120.2 0.9 copy-start.8
  121.2 0.9 copy-start.10
  127.6 30.3 %all-to-all-start.1 = ((bf16[32,4,16,256]{3,2,1,0:T(8,128)(2,1)}), bf16[32,4,16,256]{3,2,1,0:T(8,128)(2,1)S(1)}, u32[]{:S(2)}, u32[]{:S(2)}) async-start(bf16[32,4,16,256]{3,2,1,0:T(8,128)(2,1)} %decode.1), calls=%async_computation.1 | async-start | bytes 2097152 | tf_op jit(solution)/shard_map/all_to_all | solution.py:159
  191.3 19.7 %collective-permute-start.14 = (bf16[32,4,16,256]{3,2,1,0:T(8,128)(2,1)S(1)}, bf16[32,4,16,256]{3,2,1,0:T(8,128)(2,1)S(1)}, u32[]{:S(2)}, u32[]{:S(2)}) collective-permute-start(bf16[32,4,16,256]{3,2,1,0:T(8,128)(2,1)S(1)} %all_to_all.26.c0), channel_id=1, source_target_pairs={{0,6},{2,0},{4,2},{6,4},{1,7},{3,1},{5,3},{7,5},{8,14},{10,8},{12,... | collective-permute-start | bytes 3145736 | tf_op jit(solution)/shard_map/ppermute | solution.py:21
  192.0 21.0 %collective-permute-start.13 = (bf16[32,4,16,256]{3,2,1,0:T(8,128)(2,1)S(1)}, bf16[32,4,16,256]{3,2,1,0:T(8,128)(2,1)S(1)}, u32[]{:S(2)}, u32[]{:S(2)}) collective-permute-start(bf16[32,4,16,256]{3,2,1,0:T(8,128)(2,1)S(1)} %all_to_all.26.c0), channel_id=1, source_target_pairs={{0,4},{2,6},{4,0},{6,2},{1,5},{3,7},{5,1},{7,3},{8,12},{10,14},{12... | collective-permute-start | bytes 3145736 | tf_op jit(solution)/shard_map/ppermute | solution.py:21
  192.2 48.8 %collective-permute-start.12 = (bf16[32,4,16,256]{3,2,1,0:T(8,128)(2,1)S(1)}, bf16[32,4,16,256]{3,2,1,0:T(8,128)(2,1)S(1)}, u32[]{:S(2)}, u32[]{:S(2)}) collective-permute-start(bf16[32,4,16,256]{3,2,1,0:T(8,128)(2,1)S(1)} %all_to_all.26.c0), channel_id=1, source_target_pairs={{0,2},{2,4},{4,6},{6,0},{1,3},{3,5},{5,7},{7,1},{8,10},{10,12},{12... | collective-permute-start | bytes 3145736 | tf_op jit(solution)/shard_map/ppermute | solution.py:21
  241.0 2.4 copy-start.1
  243.4 7.6 %collective-permute-start.15 = (bf16[4,32,4,16,256]{4,3,2,1,0:T(8,128)(2,1)}, bf16[4,32,4,16,256]{4,3,2,1,0:T(8,128)(2,1)}, u32[]{:S(2)}, u32[]{:S(2)}) collective-permute-start(bf16[4,32,4,16,256]{4,3,2,1,0:T(8,128)(2,1)} %pad_maximum_fusion), channel_id=1, source_target_pairs={{0,1},{1,0},{2,3},{3,2},{4,5},{5,4},{6,7},{7,6},{8,9},{9,8},{10,11... | collective-permute-start | bytes 12582920 | tf_op jit(solution)/shard_map/ppermute | solution.py:21
  251.0 1.2 copy-start.2
  252.2 0.9 copy-start.4

commit v2 on v0

v2 whole, which is shorter than its diff:
```python
import functools
import math

import jax
import jax.numpy as jnp
from jax import lax
from jax.experimental import pallas as pl
from jax.experimental.pallas import tpu as pltpu
from jax.sharding import Mesh
from jax.sharding import PartitionSpec as P

BF = jnp.bfloat16
F32 = jnp.float32
NX, NZ, NY, NC = 4, 8, 4, 2
XZ = NX * NZ

ALL = ("x", "z", "y", "c")
VMEM_LIMIT = 24 * 1024 * 1024


def device(x, z, y, core):
    return ((x * NZ + z) * NY + y) * NC + core


def coordinates():
    return [(x, z, y, core) for x in range(NX) for z in range(NZ) for y in range(NY) for core in range(NC)]


def shift(value, axis, step):
    size = lax.axis_size(axis)
    return lax.ppermute(value, axis, [(i, (i + step) % size) for i in range(size)])


def ring(value, step):
    pairs = []
    for x, z, y, core in coordinates():
        there = (x, z, (y + step) % NY, core) if core == 0 else ((x + step) % NX, z, y, core)
        pairs.append((device(x, z, y, core), device(*there)))
    return lax.ppermute(value, ALL, pairs)


def trade(value):
    groups = [[device(x, z, y, 0) for x in range(NX) for z in range(NZ)] for y in range(NY)]
    groups += [[device(x, z, y, 1) for y in range(NY) for z in range(NZ)] for x in range(NX)]
    return lax.all_to_all(value, ALL, 0, 0, axis_index_groups=groups, tiled=True)


def encoder_kernel(*refs):
    pieces, (weight, bias, place, mine, give, rows) = refs[:NY * NC], refs[NY * NC:]
    chunk = pieces[0].shape[0]
    for i, ref in enumerate(pieces):
        rows[i * chunk:(i + 1) * chunk, :] = ref[...]
    preact = jnp.dot(rows[...], weight[...], preferred_element_type=F32) + bias[...]
    activity = jnp.maximum(preact, 0.0).astype(BF)
    mine[...] = jnp.dot(place[0], activity, preferred_element_type=F32).astype(BF)
    give[...] = jnp.dot(place[1], activity, preferred_element_type=F32).astype(BF)


def encode(pieces, weight, bias, place):
    tokens = place.shape[1]
    result = jax.ShapeDtypeStruct((tokens, weight.shape[1]), BF)
    return pl.pallas_call(
        encoder_kernel,
        out_shape=(result, result),
        scratch_shapes=[pltpu.VMEM((tokens, weight.shape[0]), BF)],
        compiler_params=pltpu.CompilerParams(vmem_limit_bytes=VMEM_LIMIT),
        cost_estimate=pl.CostEstimate(flops=8 * 10**8, bytes_accessed=4 * 10**6, transcendentals=0),
        name="encode",
    )(*pieces, weight, bias, place)


def decoder_kernel(where, a0, a1, a2, a3, w0, w1, w2, w3, bias, out, total):
    feats = a0.shape[2]
    x, z, y, core = (where[i] for i in range(4))
    adds_bias = (z == 0) & (((core == 0) & (x == y)) | ((core == 1) & (y == 0)))
    total[...] = jnp.broadcast_to(jnp.where(adds_bias, bias[...], 0.0), total.shape)
    for i, (a, w) in enumerate(((a0, w0), (a1, w1), (a2, w2), (a3, w3))):

        @pl.when(((core == 0) & (y >= x)) | ((core == 1) & (x >= i)))
        def _():
            total[...] += jnp.dot(a[0], w[:feats, :], preferred_element_type=F32) + jnp.dot(
                a[1], w[feats:2 * feats, :], preferred_element_type=F32
            )

    out[...] = total[...].astype(BF).reshape(out.shape)


def decode(where, acts, weights, bias):
    cores, tokens, feats = acts[0].shape
    rows, width = weights[0].shape
    part, cols = tokens // XZ, 256
    blocks = width // cols
    return pl.pallas_call(
        decoder_kernel,
        grid_spec=pltpu.PrefetchScalarGridSpec(
            num_scalar_prefetch=1,
            grid=(blocks,),
            in_specs=[pl.BlockSpec((cores, tokens, feats), lambda n, _: (0, 0, 0))] * NY
            + [pl.BlockSpec((rows, cols), lambda n, _: (0, n))] * NY
            + [pl.BlockSpec((1, cols), lambda n, where: (0, where[3] * blocks + n))],
            out_specs=pl.BlockSpec((XZ, part, cols), lambda n, _: (0, 0, n)),
            scratch_shapes=[pltpu.VMEM((tokens, cols), F32)],
        ),
        out_shape=jax.ShapeDtypeStruct((XZ, part, width), BF),
        compiler_params=pltpu.CompilerParams(vmem_limit_bytes=VMEM_LIMIT),
        cost_estimate=pl.CostEstimate(flops=22 * 10**8, bytes_accessed=8 * 10**6, transcendentals=0),
        name="decode",
    )(where, *acts, *weights, bias)


def sinks_at(where, step):
    x, y, core = where[0], where[2], where[3]
    first, second = jnp.where(core == 0, y, x), jnp.where(core == 0, x, y)
    return lax.rem(first + NY - step, NY), lax.rem(second + NY - step, NY)


def gradient_kernel(step, where, own, other, mine, give, *rest):
    out = rest[-1]
    half = pl.program_id(0)
    sinks = sinks_at(where, step)
    for i, (block, activity) in enumerate(((own, mine), (other, give))):

        @pl.when((half == i) & (sinks[i] >= where[0]))
        def _():
            rhs = block[...].reshape(-1, block.shape[2])
            out[0] = jnp.dot(activity[...], rhs, preferred_element_type=F32).astype(BF)

        @pl.when((half == i) & (sinks[i] < where[0]))
        def _():
            out[...] = jnp.zeros(out.shape, BF)


def gradient(step, where, layers, own, other, mine, give, before):
    slots, part, cols = own.shape
    feats, tokens = mine.shape
    more = [] if before is None else [before]

    def place(half, where):
        first, second = sinks_at(where, step)
        return jnp.where(half == 0, first, second), 0, jnp.where(half == 0, where[3], 1 - where[3])

    return pl.pallas_call(
        functools.partial(gradient_kernel, step),
        grid_spec=pltpu.PrefetchScalarGridSpec(
            num_scalar_prefetch=1,
            grid=(NC,),
            in_specs=[pl.BlockSpec((slots, part, cols), lambda h, _: (0, 0, 0))] * 2
            + [pl.BlockSpec((feats, tokens), lambda h, _: (0, 0))] * 2
            + [pl.BlockSpec(memory_space=pl.ANY)] * len(more),
            out_specs=pl.BlockSpec((1, feats, cols), place),
        ),
        out_shape=jax.ShapeDtypeStruct((layers, feats, NC * cols), BF),
        input_output_aliases={5: 0} if more else {},
        compiler_params=pltpu.CompilerParams(vmem_limit_bytes=VMEM_LIMIT),
        cost_estimate=pl.CostEstimate(flops=55 * 10**7, bytes_accessed=4 * 10**6, transcendentals=0),
        name="gradient",
    )(where, own, other, mine, give, *more)


def pack_kernel(where, own, other, target, out):
    feats = own.shape[1]
    out[:feats, :] = own[0]
    out[feats:2 * feats, :] = other[0]
    out[2 * feats:, :] = target[0]


def pack(step, where, weight, other, target):
    layers, feats, half = other.shape
    extra = target.shape[1]

    def sink(where):
        return lax.rem(jnp.where(where[3] == 0, where[2], where[0]) + step, NY)

    return pl.pallas_call(
        pack_kernel,
        grid_spec=pltpu.PrefetchScalarGridSpec(
            num_scalar_prefetch=1,
            grid=(2,),
            in_specs=[
                pl.BlockSpec((1, feats, half // 2), lambda n, where: (sink(where), 0, where[3] * 2 + n)),
                pl.BlockSpec((1, feats, half // 2), lambda n, where: (sink(where), 0, n)),
                pl.BlockSpec((1, extra, half // 2), lambda n, where: (sink(where), 0, n)),
            ],
            out_specs=pl.BlockSpec((2 * feats + extra, half // 2), lambda n, where: (0, n)),
        ),
        out_shape=jax.ShapeDtypeStruct((2 * feats + extra, half), BF),
        compiler_params=pltpu.CompilerParams(vmem_limit_bytes=VMEM_LIMIT),
        cost_estimate=pl.CostEstimate(flops=0, bytes_accessed=2 * 10**6, transcendentals=0),
        name="pack",
    )(where, weight, other, target)


def body(resid, target, enc_weight, enc_bias, dec_weight, dec_bias):
    x, z, y, core = (lax.axis_index(a) for a in ALL)
    mine, layers, width = resid.shape
    tokens = mine * XZ * NY * NC
    half = width // NC
    factor = 1.0 / math.sqrt(tokens)
    feats = dec_weight.shape[2]
    sink = jnp.where(core == 0, y, x)
    where = jnp.stack([x, z, y, core])

    give = lax.dynamic_slice_in_dim(dec_weight[0], (1 - core) * half, half, axis=2)
    aims = target.transpose(1, 0, 2).reshape(layers, mine, NC, half)
    aims = jnp.where(core == 0, jnp.stack([aims[:, :, 0], aims[:, :, 1]]), jnp.stack([aims[:, :, 1], aims[:, :, 0]]))
    rows = jnp.broadcast_to(resid.transpose(1, 0, 2)[:, None], (layers, NZ, mine, width))
    rows = rows.reshape(XZ * mine, width)
    rows, give, aims, where = lax.optimization_barrier((rows, give, aims, where))
    extra = jnp.concatenate([aims[0], shift(aims[1], "c", 1), jnp.zeros((layers, 16 - 2 * mine, half), BF)], axis=1)
    give = shift(give, "c", 1)
    weights = [pack(step, where, dec_weight[0], give, extra) for step in range(NY)]
    rows = lax.all_to_all(rows, ("x", "z"), 0, 0, tiled=True)
    rows, *weights = lax.optimization_barrier((rows, *weights))
    weights = [ring(piece, step) if step else piece for step, piece in enumerate(weights)]
    pieces = [rows] + [shift(rows, "y", step) for step in range(1, NY)]
    pieces = pieces + [shift(piece, "c", 1) for piece in pieces]
    r = jnp.arange(tokens)
    r_core = jnp.where(r // (tokens // 2) == 0, core, 1 - core)
    r_y = (y + NY - r // (tokens // 8) % NY) % NY
    r_x, r_z, r_i = r // (mine * NZ) % NX, r // mine % NZ, r % mine
    order = [((a * NZ + r_z) * 4 + b) * NC * mine + r_core * mine + r_i for a, b in ((r_x, r_y), (r_y, r_x))]
    order = jnp.stack([jnp.where(core == 0, order[0], order[1]), jnp.where(core == 0, order[1], order[0])])
    place = (jnp.arange(tokens)[None, :, None] == order[:, None, :]).astype(BF)
    own, away = encode(pieces, enc_weight[0], enc_bias, place)

    act = jnp.stack([own, shift(away, "c", 1)])
    acts = [act] + [ring(act, step) for step in range(1, NY)]
    parts = decode(where, acts, weights, dec_bias)

    wanted = jnp.concatenate([w[2 * feats:2 * feats + 2 * mine] for w in weights])
    q = jnp.arange(NY * NC * mine)
    q_core = jnp.where(q // mine % NC == 0, core, 1 - core)
    q = (sink + NY - q // (NC * mine)) % NY * NC * mine + q_core * mine + q % mine
    wanted = jnp.dot((jnp.arange(q.shape[0])[:, None] == q[None, :]).astype(BF), wanted, preferred_element_type=F32)

    got = trade(parts)
    own, away = own.T, away.T
    got, own, away = lax.optimization_barrier((got, own, away))
    misfit = jnp.sum(got.astype(F32), axis=0) - wanted
    cotangent = (misfit * factor).astype(BF)
    block = trade(jnp.broadcast_to(cotangent[None], (XZ,) + cotangent.shape))

    grads = None
    blocks = [block] + [ring(block, step) for step in range(1, NY)]
    for step in (0, 1, 3, 2):
        grads = gradient(step, where, layers, blocks[step], shift(blocks[step], "c", 1), own, away, grads)
    return grads[None]


def solution(mesh):
    fine = Mesh(mesh.devices.reshape(NX, NZ, NY, NC), ("x", "z", "y", "c"))
    feat = ("z", "y", "c")
    return jax.shard_map(
        body,
        mesh=fine,
        in_specs=(
            P(("x",) + feat, None, None),
            P(("x",) + feat, None, None),
            P("x", None, feat),
            P("x", feat),
            P("x", None, feat, None),
            P("x", None),
        ),
        out_specs=P("x", None, feat, None),
        check_vma=False,
    )
```

time: 1510 us -> 210 us (0.14)
  waiting for transfers between devices: 1440 us -> 66.9 us
  starting transfers between devices: 0.09 us -> 77.5 us
  Pallas kernels: 0 us -> 21.2 us
  matrix products: 20.8 us -> 0.15 us
    reduce_scatter x1 -> x0, waiting for transfers between devices: 1280 us -> none  [body(): lax.psum_scatter(partials.reshape(layers * total_tokens, width), ('layer'...]
    all_gather x2 -> x0, waiting for transfers between devices: 166 us -> none  [the longest x1 85.4 us: body(): lax.all_gather(stacked, 'feat', axis=1, tiled=True)]
    ppermute x0 -> x23, starting transfers between devices: none -> 61.7 us  [the longest x14 40.2 us: shift(): lax.ppermute(value, axis, [(i, (i + step) % size) for i in range(size)])]
    ppermute x0 -> x23, waiting for transfers between devices: none -> 37.8 us  [the longest x9 34.2 us: ring(): return lax.ppermute(value, ALL, pairs)]
    all_to_all x0 -> x2, waiting for transfers between devices: none -> 29.2 us  [the longest x1 20.2 us: trade(): lax.all_to_all(value, ALL, 0, 0, axis_index_groups=groups, tiled=True)]
    pallas_call x0 -> x10, Pallas kernels: none -> 21.2 us  [the longest x4 9.51 us: gradient(): pl.pallas_call(functools.partial(gradient_kernel, step), grid_spec=pltpu....]
    dot_general x3 -> x1, matrix products: 20.8 us -> 0.15 us  [body(): jnp.dot((jnp.arange(q.shape[0])[:, None] == q[None, :]).astype(BF), wante...]
    all_to_all x0 -> x2, starting transfers between devices: none -> 15.8 us  [the longest x1 9.3 us: body(): rows = lax.all_to_all(rows, ('x', 'z'), 0, 0, tiled=True)]
  transfers between devices with their start and end apart: 3 -> 25, of which waited for: 3 -> 11; matrix products, arithmetic and copies ran while one was open for 0% -> 1% of each run, Pallas kernels for 0% -> 5%
where the time goes in v2:
time: 210 us; the launch traced here: 209 us
  starting transfers between devices  77.5 us (37%)
  waiting for transfers between devices  66.9 us (32%)
  blocking collectives  28.2 us (13%)
  Pallas kernels  21.2 us (10%)
  local copies, waits for them, and re-layouts  14.3 us (7%)
    ppermute x14, starting transfers between devices, shift(): lax.ppermute(value, axis, [(i, (i + step) % size) for i in range(size)])  40.2 us
    ppermute x9, waiting for transfers between devices, ring(): return lax.ppermute(value, ALL, pairs)  34.2 us
    all_to_all x1, blocking collectives, trade(): lax.all_to_all(value, ALL, 0, 0, axis_index_groups=groups, tiled=True)  28.2 us
    ppermute x9, starting transfers between devices, ring(): return lax.ppermute(value, ALL, pairs)  21.5 us
    all_to_all x1, waiting for transfers between devices, trade(): lax.all_to_all(value, ALL, 0, 0, axis_index_groups=groups, tiled=True)  20.2 us
    pallas_call x4, Pallas kernels, gradient(): pl.pallas_call(functools.partial(gradient_kernel, step), grid_spec=pltpu....  9.51 us
    all_to_all x1, starting transfers between devices, body(): rows = lax.all_to_all(rows, ('x', 'z'), 0, 0, tiled=True)  9.3 us
    all_to_all x1, waiting for transfers between devices, body(): rows = lax.all_to_all(rows, ('x', 'z'), 0, 0, tiled=True)  8.93 us
  transfers between devices with their start and end apart: 25, of which 11 were waited for; matrix products, arithmetic and copies ran while one was open for 1% of the time, Pallas kernels for 5%

profile of v2, /device:TPU:1, one launch (start us, length us, event | category | flops | bytes accessed | tf_op | source)
XLA Modules:
  0.0 209.5 jit_solution(14642631171524813442)
XLA Ops:
  0.0 0.8 reshape.385
  0.8 0.8 copy.13
  1.6 0.1 broadcast_in_dim.38
  1.9 3.1 %dynamic-slice_bitcast_fusion = bf16[4,256,1024]{2,1,0:T(8,128)(2,1)} fusion(bf16[1,4,256,2048]{3,2,1,0:T(8,128)(2,1)} %param.10, s32[]{:T(128)S(6)} %select_n.251), kind=kLoop, calls=%fused_computation.2 | loop fusion | bytes 4194308 | tf_op jit(solution)/shard_map/dynamic_slice | solution.py:203
  5.2 3.3 %collective-permute-start = (bf16[4,256,1024]{2,1,0:T(8,128)(2,1)}, bf16[4,256,1024]{2,1,0:T(8,128)(2,1)S(1)}, u32[]{:S(2)}, u32[]{:S(2)}) collective-permute-start(bf16[4,256,1024]{2,1,0:T(8,128)(2,1)} %dynamic-slice_bitcast_fusion), channel_id=1, source_target_pairs={{0,1},{1,0},{2,3},{3,2},{4,5},{5,4},{6,7},{7,6},{8,9},{9,8},{10,11... | collective-permute-start | bytes 6291464 | tf_op jit(solution)/shard_map/ppermute | solution.py:31
  8.5 0.9 all_to_all.14
  9.3 9.3 %all-to-all-start = ((bf16[32,2,2048]{2,1,0:T(2,128)(2,1)}), bf16[32,2,2048]{2,1,0:T(2,128)(2,1)S(1)}, u32[]{:S(2)}, u32[]{:S(2)}) async-start(bf16[32,2,2048]{2,1,0:T(2,128)(2,1)} %all_to_all.14), calls=%async_computation | async-start | bytes 524288 | tf_op jit(solution)/shard_map/all_to_all | solution.py:212
  18.7 0.4 collective-permute-start.1
  19.1 0.8 collective-permute-done.1
  20.0 8.9 %all-to-all-done = bf16[32,2,2048]{2,1,0:T(2,128)(2,1)S(1)} async-done(((bf16[32,2,2048]{2,1,0:T(2,128)(2,1)}), bf16[32,2,2048]{2,1,0:T(2,128)(2,1)S(1)}, u32[]{:S(2)}, u32[]{:S(2)}) %all-to-all-start) | async-done | bytes 262176 | tf_op jit(solution)/shard_map/all_to_all | solution.py:212
  29.0 0.8 all_to_all.16.refs_0_
  29.8 2.2 %copy-done = bf16[1,4,256,2048]{3,2,1,0:T(8,128)(2,1)S(1)} copy-done((bf16[1,4,256,2048]{3,2,1,0:T(8,128)(2,1)S(1)}, bf16[1,4,256,2048]{3,2,1,0:T(8,128)(2,1)}, u32[]{:S(2)}) %copy-start) | copy-done | bytes 4194328
  32.0 0.9 pack.7
  32.9 0.9 pack.6
  33.9 1.0 copy-done.3
  34.9 1.7 pack.5
  36.6 0.9 pack.4.w0
  37.5 1.4 collective-permute-start.2
  38.9 2.6 %collective-permute-start.3 = (bf16[64,2048]{1,0:T(8,128)(2,1)}, bf16[64,2048]{1,0:T(8,128)(2,1)S(1)}, u32[]{:S(2)}, u32[]{:S(2)}) collective-permute-start(bf16[64,2048]{1,0:T(8,128)(2,1)} %all_to_all.16.refs_0_), channel_id=1, source_target_pairs={{0,4},{2,6},{4,0},{6,2},{1,5},{3,7},{5,1},{7,3},{8,12},{10,14},{12... | collective-permute-start | bytes 786440 | tf_op jit(solution)/shard_map/ppermute | solution.py:31
  41.5 1.1 collective-permute-start.4
  42.6 0.3 collective-permute-start.13
  42.9 3.5 %collective-permute-start.5 = (bf16[64,2048]{1,0:T(8,128)(2,1)}, bf16[64,2048]{1,0:T(8,128)(2,1)S(1)}, u32[]{:S(2)}, u32[]{:S(2)}) collective-permute-start(bf16[64,2048]{1,0:T(8,128)(2,1)} %all_to_all.16.refs_0_), channel_id=1, source_target_pairs={{0,1},{1,0},{2,3},{3,2},{4,5},{5,4},{6,7},{7,6},{8,9},{9,8},{10,11... | collective-permute-start | bytes 786440 | tf_op jit(solution)/shard_map/ppermute | solution.py:31
  46.5 3.0 %collective-permute-start.6 = (bf16[64,2048]{1,0:T(8,128)(2,1)S(1)}, bf16[64,2048]{1,0:T(8,128)(2,1)S(1)}, u32[]{:S(2)}, u32[]{:S(2)}) collective-permute-start(bf16[64,2048]{1,0:T(8,128)(2,1)S(1)} %collective-permute-done.2.refs_1_), channel_id=1, source_target_pairs={{0,1},{1,0},{2,3},{3,2},{4,5},{5,4},{6,7},{7,6},{8,9},{9,8},{10,11... | collective-permute-start | bytes 786440 | tf_op jit(solution)/shard_map/ppermute | solution.py:31
  49.5 1.5 collective-permute-done.3.refs_2_
  51.1 3.6 %collective-permute-start.7 = (bf16[64,2048]{1,0:T(8,128)(2,1)S(1)}, bf16[64,2048]{1,0:T(8,128)(2,1)S(1)}, u32[]{:S(2)}, u32[]{:S(2)}) collective-permute-start(bf16[64,2048]{1,0:T(8,128)(2,1)S(1)} %collective-permute-done.3.refs_2_), channel_id=1, source_target_pairs={{0,1},{1,0},{2,3},{3,2},{4,5},{5,4},{6,7},{7,6},{8,9},{9,8},{10,11... | collective-permute-start | bytes 786440 | tf_op jit(solution)/shard_map/ppermute | solution.py:31
  54.7 1.9 collective-permute-start.14
  56.6 0.9 collective-permute-start.15
  57.5 0.3 fusion.refs_10_
  57.9 1.2 copy-done.4
  59.1 2.5 %encode.1 = (bf16[512,256]{1,0:T(8,128)(2,1)S(1)}, bf16[512,256]{1,0:T(8,128)(2,1)S(1)}) custom-call(bf16[64,2048]{1,0:T(8,128)(2,1)} %all_to_all.16.refs_0_, bf16[64,2048]{1,0:T(8,128)(2,1)S(1)} %collective-permute-done.2.refs_1_, bf16[64,2048]{1,0:T(8,128)(2,1)S(1)} %collective-permute-done.3.refs_2_, bf16[64,2048]{1,0:T(8,128)(2,1)S(1)} %collective-permute-done.4.refs_3_, ...), custom_call_target="tpu_custom_call" | custom-call | flops 800000000 | bytes 4000000 | tf_op jit(solution)/shard_map/encode/pallas_call | solution.py:62
  61.6 1.2 collective-permute-start.9
  62.9 1.2 collective-permute-done.9
  64.1 0.6 collective-permute-start.10
  64.7 2.5 %collective-permute-start.11 = (bf16[2,512,256]{2,1,0:T(8,128)(2,1)S(1)}, bf16[2,512,256]{2,1,0:T(8,128)(2,1)S(1)}, u32[]{:S(2)}, u32[]{:S(2)}) collective-permute-start(bf16[2,512,256]{2,1,0:T(8,128)(2,1)S(1)} %pad_maximum_fusion.a0), channel_id=1, source_target_pairs={{0,4},{1,129},{2,6},{3,131},{4,0},{5,133},{6,2},{7,135},{8,12},{9,... | collective-permute-start | bytes 1572872 | tf_op jit(solution)/shard_map/ppermute | solution.py:39
  67.1 1.1 collective-permute-start.12
  68.2 2.6 %collective-permute-done.14.w2 = bf16[528,1024]{1,0:T(8,128)(2,1)S(1)} collective-permute-done((bf16[528,1024]{1,0:T(8,128)(2,1)}, bf16[528,1024]{1,0:T(8,128)(2,1)S(1)}, u32[]{:S(2)}, u32[]{:S(2)}) %collective-permute-start.14) | collective-permute-done | bytes 1081376 | tf_op jit(solution)/shard_map/ppermute | solution.py:39
  70.8 10.8 %collective-permute-done.15.w3 = bf16[528,1024]{1,0:T(8,128)(2,1)S(1)} collective-permute-done((bf16[528,1024]{1,0:T(8,128)(2,1)}, bf16[528,1024]{1,0:T(8,128)(2,1)S(1)}, u32[]{:S(2)}, u32[]{:S(2)}) %collective-permute-start.15) | collective-permute-done | bytes 1081376 | tf_op jit(solution)/shard_map/ppermute | solution.py:39
  81.6 0.1 collective-permute-done.11.a2
  81.8 11.1 %collective-permute-done.12.a3 = bf16[2,512,256]{2,1,0:T(8,128)(2,1)S(1)} collective-permute-done((bf16[2,512,256]{2,1,0:T(8,128)(2,1)S(1)}, bf16[2,512,256]{2,1,0:T(8,128)(2,1)S(1)}, u32[]{:S(2)}, u32[]{:S(2)}) %collective-permute-start.12) | collective-permute-done | bytes 524320 | tf_op jit(solution)/shard_map/ppermute | solution.py:39
  92.9 4.7 %decode.1 = bf16[32,16,1024]{2,1,0:T(8,128)(2,1)} custom-call(s32[4]{0:T(128)S(1)} %pad_add_fusion.1.where, bf16[2,512,256]{2,1,0:T(8,128)(2,1)S(1)} %pad_maximum_fusion.a0, bf16[2,512,256]{2,1,0:T(8,128)(2,1)S(1)} %collective-permute-done.10.a1, bf16[2,512,256]{2,1,0:T(8,128)(2,1)S(1)} %collective-permute-done.11.a2, ...), custom_call_target="tpu_custom_call" | custom-call | flops 2200000000 | bytes 8000000 | tf_op jit(solution)/shard_map/decode/pallas_call | solution.py:93
  97.6 1.0 copy-done.6
  98.6 1.0 copy-done.7
  99.6 6.5 %all-to-all-start.1 = ((bf16[32,16,1024]{2,1,0:T(8,128)(2,1)}), bf16[32,16,1024]{2,1,0:T(8,128)(2,1)S(1)}, u32[]{:S(2)}, u32[]{:S(2)}) async-start(bf16[32,16,1024]{2,1,0:T(8,128)(2,1)} %decode.1), calls=%async_computation.1 | async-start | bytes 2097152 | tf_op jit(solution)/shard_map/all_to_all | solution.py:45
  106.1 0.1 copy.17
  106.3 0.1 copy.18
  106.4 0.7 slice.36
  107.2 20.2 %all-to-all-done.1 = bf16[32,16,1024]{2,1,0:T(8,128)(2,1)S(1)} async-done(((bf16[32,16,1024]{2,1,0:T(8,128)(2,1)}), bf16[32,16,1024]{2,1,0:T(8,128)(2,1)S(1)}, u32[]{:S(2)}, u32[]{:S(2)}) %all-to-all-start.1) | async-done | bytes 1048608 | tf_op jit(solution)/shard_map/all_to_all | solution.py:45
  127.4 0.2 convert_reduce_fusion
  127.6 0.1 fusion.2
  127.8 0.1 broadcast_in_dim.44
  127.9 28.2 %all_to_all.22.own = bf16[32,16,1024]{2,1,0:T(8,128)(2,1)S(1)} all-to-all(bf16[32,16,1024]{2,1,0:T(8,128)(2,1)S(1)} %broadcast_in_dim.44), channel_id=1, replica_groups={{0,8,16,24,32,40,48,56,64,72,80,88,96,104,112,120,128,136,144,152,160,1..., dimensions={0} | all-to-all | bytes 2097152 | tf_op jit(solution)/shard_map/all_to_all | solution.py:45
  156.1 2.8 %collective-permute-start.20 = (bf16[32,16,1024]{2,1,0:T(8,128)(2,1)S(1)}, bf16[32,16,1024]{2,1,0:T(8,128)(2,1)S(1)}, u32[]{:S(2)}, u32[]{:S(2)}) collective-permute-start(bf16[32,16,1024]{2,1,0:T(8,128)(2,1)S(1)} %all_to_all.22.own), channel_id=1, source_target_pairs={{0,2},{1,65},{2,4},{3,67},{4,6},{5,69},{6,0},{7,71},{8,10},{9,73},... | collective-permute-start | bytes 3145736 | tf_op jit(solution)/shard_map/ppermute | solution.py:39
  158.9 10.2 %collective-permute-start.18 = (bf16[32,16,1024]{2,1,0:T(8,128)(2,1)S(1)}, bf16[32,16,1024]{2,1,0:T(8,128)(2,1)S(1)}, u32[]{:S(2)}, u32[]{:S(2)}) collective-permute-start(bf16[32,16,1024]{2,1,0:T(8,128)(2,1)S(1)} %all_to_all.22.own), channel_id=1, source_target_pairs={{0,6},{1,193},{2,0},{3,195},{4,2},{5,197},{6,4},{7,199},{8,14},{9,... | collective-permute-start | bytes 3145736 | tf_op jit(solution)/shard_map/ppermute | solution.py:39
  169.1 1.2 collective-permute-start.16
  170.3 6.4 %collective-permute-start.22 = (bf16[32,16,1024]{2,1,0:T(8,128)(2,1)S(1)}, bf16[32,16,1024]{2,1,0:T(8,128)(2,1)S(1)}, u32[]{:S(2)}, u32[]{:S(2)}) collective-permute-start(bf16[32,16,1024]{2,1,0:T(8,128)(2,1)S(1)} %all_to_all.22.own), channel_id=1, source_target_pairs={{0,1},{1,0},{2,3},{3,2},{4,5},{5,4},{6,7},{7,6},{8,9},{9,8},{10,11... | collective-permute-start | bytes 3145736 | tf_op jit(solution)/shard_map/ppermute | solution.py:31
  176.7 5.2 %collective-permute-done.20.own = bf16[32,16,1024]{2,1,0:T(8,128)(2,1)S(1)} collective-permute-done((bf16[32,16,1024]{2,1,0:T(8,128)(2,1)S(1)}, bf16[32,16,1024]{2,1,0:T(8,128)(2,1)S(1)}, u32[]{:S(2)}, u32[]{:S(2)}) %collective-permute-start.20) | collective-permute-done | bytes 1048608 | tf_op jit(solution)/shard_map/ppermute | solution.py:39
  182.0 5.8 %collective-permute-start.21 = (bf16[32,16,1024]{2,1,0:T(8,128)(2,1)S(1)}, bf16[32,16,1024]{2,1,0:T(8,128)(2,1)S(1)}, u32[]{:S(2)}, u32[]{:S(2)}) collective-permute-start(bf16[32,16,1024]{2,1,0:T(8,128)(2,1)S(1)} %collective-permute-done.20.own), channel_id=1, source_target_pairs={{0,1},{1,0},{2,3},{3,2},{4,5},{5,4},{6,7},{7,6},{8,9},{9,8},{10,11... | collective-permute-start | bytes 3145736 | tf_op jit(solution)/shard_map/ppermute | solution.py:31
  187.8 4.4 %collective-permute-done.18.own = bf16[32,16,1024]{2,1,0:T(8,128)(2,1)S(1)} collective-permute-done((bf16[32,16,1024]{2,1,0:T(8,128)(2,1)S(1)}, bf16[32,16,1024]{2,1,0:T(8,128)(2,1)S(1)}, u32[]{:S(2)}, u32[]{:S(2)}) %collective-permute-start.18) | collective-permute-done | bytes 1048608 | tf_op jit(solution)/shard_map/ppermute | solution.py:39
  192.1 6.5 %collective-permute-start.19 = (bf16[32,16,1024]{2,1,0:T(8,128)(2,1)S(1)}, bf16[32,16,1024]{2,1,0:T(8,128)(2,1)S(1)}, u32[]{:S(2)}, u32[]{:S(2)}) collective-permute-start(bf16[32,16,1024]{2,1,0:T(8,128)(2,1)S(1)} %collective-permute-done.18.own), channel_id=1, source_target_pairs={{0,1},{1,0},{2,3},{3,2},{4,5},{5,4},{6,7},{7,6},{8,9},{9,8},{10,11... | collective-permute-start | bytes 3145736 | tf_op jit(solution)/shard_map/ppermute | solution.py:31
  198.6 1.4 collective-permute-start.17
  199.9 2.4 %gradient.4.rest_0_ = bf16[4,256,2048]{2,1,0:T(8,128)(2,1)} custom-call(s32[4]{0:T(128)S(1)} %pad_add_fusion.1.where, bf16[32,16,1024]{2,1,0:T(8,128)(2,1)S(1)} %all_to_all.22.own, bf16[32,16,1024]{2,1,0:T(8,128)(2,1)S(1)} %collective-permute-done.22.other, bf16[256,512]{1,0:T(8,128)(2,1)S(1)} %bitcast.29, bf16[256,512]{1,0:T(8,128)(2,1)S(1)} %bitcast.33), custom_call_target="tpu_custom_call" | custom-call | flops 550000000 | bytes 4000000 | tf_op jit(solution)/shard_map/gradient/pallas_call | solution.py:142
  202.3 2.4 %gradient.5.rest_0_ = bf16[4,256,2048]{2,1,0:T(8,128)(2,1)} custom-call(s32[4]{0:T(128)S(1)} %pad_add_fusion.1.where, bf16[32,16,1024]{2,1,0:T(8,128)(2,1)S(1)} %collective-permute-done.20.own, bf16[32,16,1024]{2,1,0:T(8,128)(2,1)S(1)} %collective-permute-done.21.other, bf16[256,512]{1,0:T(8,128)(2,1)S(1)} %bitcast.30, ...), custom_call_target="tpu_custom_call", output_to_operand_aliasing={{}: (5, {})} | custom-call | flops 550000000 | bytes 4000000 | tf_op jit(solution)/shard_map/gradient/pallas_call | solution.py:142
  204.7 2.4 %gradient.6.rest_0_ = bf16[4,256,2048]{2,1,0:T(8,128)(2,1)} custom-call(s32[4]{0:T(128)S(1)} %pad_add_fusion.1.where, bf16[32,16,1024]{2,1,0:T(8,128)(2,1)S(1)} %collective-permute-done.18.own, bf16[32,16,1024]{2,1,0:T(8,128)(2,1)S(1)} %collective-permute-done.19.other, bf16[256,512]{1,0:T(8,128)(2,1)S(1)} %bitcast.31, ...), custom_call_target="tpu_custom_call", output_to_operand_aliasing={{}: (5, {})} | custom-call | flops 550000000 | bytes 4000000 | tf_op jit(solution)/shard_map/gradient/pallas_call | solution.py:142
  207.1 2.4 %gradient.7 = bf16[4,256,2048]{2,1,0:T(8,128)(2,1)} custom-call(s32[4]{0:T(128)S(1)} %pad_add_fusion.1.where, bf16[32,16,1024]{2,1,0:T(8,128)(2,1)S(1)} %collective-permute-done.16.own, bf16[32,16,1024]{2,1,0:T(8,128)(2,1)S(1)} %collective-permute-done.17.other, bf16[256,512]{1,0:T(8,128)(2,1)S(1)} %bitcast.32, ...), custom_call_target="tpu_custom_call", output_to_operand_aliasing={{}: (5, {})} | custom-call | flops 550000000 | bytes 4000000 | tf_op jit(solution)/shard_map/gradient/pallas_call | solution.py:142
  (47 shorter events, 0.8 us)
Async XLA Ops:
  5.2 24.6 %collective-permute-start = (bf16[4,256,1024]{2,1,0:T(8,128)(2,1)}, bf16[4,256,1024]{2,1,0:T(8,128)(2,1)S(1)}, u32[]{:S(2)}, u32[]{:S(2)}) collective-permute-start(bf16[4,256,1024]{2,1,0:T(8,128)(2,1)} %dynamic-slice_bitcast_fusion), channel_id=1, source_target_pairs={{0,1},{1,0},{2,3},{3,2},{4,5},{5,4},{6,7},{7,6},{8,9},{9,8},{10,11... | collective-permute-start | bytes 6291464 | tf_op jit(solution)/shard_map/ppermute | solution.py:31
  9.3 19.6 %all-to-all-start = ((bf16[32,2,2048]{2,1,0:T(2,128)(2,1)}), bf16[32,2,2048]{2,1,0:T(2,128)(2,1)S(1)}, u32[]{:S(2)}, u32[]{:S(2)}) async-start(bf16[32,2,2048]{2,1,0:T(2,128)(2,1)} %all_to_all.14), calls=%async_computation | async-start | bytes 524288 | tf_op jit(solution)/shard_map/all_to_all | solution.py:212
  18.7 1.3 collective-permute-start.1
  29.8 2.2 %copy-start = (bf16[1,4,256,2048]{3,2,1,0:T(8,128)(2,1)S(1)}, bf16[1,4,256,2048]{3,2,1,0:T(8,128)(2,1)}, u32[]{:S(2)}) copy-start(bf16[1,4,256,2048]{3,2,1,0:T(8,128)(2,1)} %param.10) | copy-start | bytes 12582916
  32.9 1.0 copy-start.2
  33.9 1.0 copy-start.3
  36.6 21.3 %copy-start.5 = (f32[1,256]{1,0:T(1,128)S(1)}, f32[1,256]{1,0:T(1,128)}, u32[]{:S(2)}) copy-start(f32[1,256]{1,0:T(1,128)} %refs_9_.1) | copy-start | bytes 3076
  37.5 68.6 %copy-start.1 = (bf16[528,1024]{1,0:T(8,128)(2,1)}, bf16[528,1024]{1,0:T(8,128)(2,1)S(1)}, u32[]{:S(2)}) copy-start(bf16[528,1024]{1,0:T(8,128)(2,1)S(1)} %pack.4.w0) | copy-start | bytes 3244036
  37.5 8.9 %collective-permute-start.2 = (bf16[64,2048]{1,0:T(8,128)(2,1)}, bf16[64,2048]{1,0:T(8,128)(2,1)S(1)}, u32[]{:S(2)}, u32[]{:S(2)}) collective-permute-start(bf16[64,2048]{1,0:T(8,128)(2,1)} %all_to_all.16.refs_0_), channel_id=1, source_target_pairs={{0,2},{2,4},{4,6},{6,0},{1,3},{3,5},{5,7},{7,1},{8,10},{10,12},{12... | collective-permute-start | bytes 786440 | tf_op jit(solution)/shard_map/ppermute | solution.py:31
  38.9 12.1 %collective-permute-start.3 = (bf16[64,2048]{1,0:T(8,128)(2,1)}, bf16[64,2048]{1,0:T(8,128)(2,1)S(1)}, u32[]{:S(2)}, u32[]{:S(2)}) collective-permute-start(bf16[64,2048]{1,0:T(8,128)(2,1)} %all_to_all.16.refs_0_), channel_id=1, source_target_pairs={{0,4},{2,6},{4,0},{6,2},{1,5},{3,7},{5,1},{7,3},{8,12},{10,14},{12... | collective-permute-start | bytes 786440 | tf_op jit(solution)/shard_map/ppermute | solution.py:31
  41.5 13.1 %collective-permute-start.4 = (bf16[64,2048]{1,0:T(8,128)(2,1)}, bf16[64,2048]{1,0:T(8,128)(2,1)S(1)}, u32[]{:S(2)}, u32[]{:S(2)}) collective-permute-start(bf16[64,2048]{1,0:T(8,128)(2,1)} %all_to_all.16.refs_0_), channel_id=1, source_target_pairs={{0,6},{2,0},{4,2},{6,4},{1,7},{3,1},{5,3},{7,5},{8,14},{10,8},{12,... | collective-permute-start | bytes 786440 | tf_op jit(solution)/shard_map/ppermute | solution.py:31
  42.6 24.5 %collective-permute-start.13 = (bf16[528,1024]{1,0:T(8,128)(2,1)}, bf16[528,1024]{1,0:T(8,128)(2,1)}, u32[]{:S(2)}, u32[]{:S(2)}) collective-permute-start(bf16[528,1024]{1,0:T(8,128)(2,1)} %pack.5), channel_id=1, source_target_pairs={{0,2},{1,65},{2,4},{3,67},{4,6},{5,69},{6,0},{7,71},{8,10},{9,73},... | collective-permute-start | bytes 3244040 | tf_op jit(solution)/shard_map/ppermute | solution.py:39
  42.9 11.8 %collective-permute-start.5 = (bf16[64,2048]{1,0:T(8,128)(2,1)}, bf16[64,2048]{1,0:T(8,128)(2,1)S(1)}, u32[]{:S(2)}, u32[]{:S(2)}) collective-permute-start(bf16[64,2048]{1,0:T(8,128)(2,1)} %all_to_all.16.refs_0_), channel_id=1, source_target_pairs={{0,1},{1,0},{2,3},{3,2},{4,5},{5,4},{6,7},{7,6},{8,9},{9,8},{10,11... | collective-permute-start | bytes 786440 | tf_op jit(solution)/shard_map/ppermute | solution.py:31
  46.5 10.2 %collective-permute-start.6 = (bf16[64,2048]{1,0:T(8,128)(2,1)S(1)}, bf16[64,2048]{1,0:T(8,128)(2,1)S(1)}, u32[]{:S(2)}, u32[]{:S(2)}) collective-permute-start(bf16[64,2048]{1,0:T(8,128)(2,1)S(1)} %collective-permute-done.2.refs_1_), channel_id=1, source_target_pairs={{0,1},{1,0},{2,3},{3,2},{4,5},{5,4},{6,7},{7,6},{8,9},{9,8},{10,11... | collective-permute-start | bytes 786440 | tf_op jit(solution)/shard_map/ppermute | solution.py:31
  51.1 6.8 %collective-permute-start.7 = (bf16[64,2048]{1,0:T(8,128)(2,1)S(1)}, bf16[64,2048]{1,0:T(8,128)(2,1)S(1)}, u32[]{:S(2)}, u32[]{:S(2)}) collective-permute-start(bf16[64,2048]{1,0:T(8,128)(2,1)S(1)} %collective-permute-done.3.refs_2_), channel_id=1, source_target_pairs={{0,1},{1,0},{2,3},{3,2},{4,5},{5,4},{6,7},{7,6},{8,9},{9,8},{10,11... | collective-permute-start | bytes 786440 | tf_op jit(solution)/shard_map/ppermute | solution.py:31
  54.7 3.2 %collective-permute-start.8 = (bf16[64,2048]{1,0:T(8,128)(2,1)S(1)}, bf16[64,2048]{1,0:T(8,128)(2,1)S(1)}, u32[]{:S(2)}, u32[]{:S(2)}) collective-permute-start(bf16[64,2048]{1,0:T(8,128)(2,1)S(1)} %collective-permute-done.4.refs_3_), channel_id=1, source_target_pairs={{0,1},{1,0},{2,3},{3,2},{4,5},{5,4},{6,7},{7,6},{8,9},{9,8},{10,11... | collective-permute-start | bytes 786440 | tf_op jit(solution)/shard_map/ppermute | solution.py:31
  54.7 16.1 %collective-permute-start.14 = (bf16[528,1024]{1,0:T(8,128)(2,1)}, bf16[528,1024]{1,0:T(8,128)(2,1)S(1)}, u32[]{:S(2)}, u32[]{:S(2)}) collective-permute-start(bf16[528,1024]{1,0:T(8,128)(2,1)} %copy-done.3), channel_id=1, source_target_pairs={{0,4},{1,129},{2,6},{3,131},{4,0},{5,133},{6,2},{7,135},{8,12},{9,... | collective-permute-start | bytes 3244040 | tf_op jit(solution)/shard_map/ppermute | solution.py:39
  56.6 25.0 %collective-permute-start.15 = (bf16[528,1024]{1,0:T(8,128)(2,1)}, bf16[528,1024]{1,0:T(8,128)(2,1)S(1)}, u32[]{:S(2)}, u32[]{:S(2)}) collective-permute-start(bf16[528,1024]{1,0:T(8,128)(2,1)} %copy-done.2), channel_id=1, source_target_pairs={{0,6},{1,193},{2,0},{3,195},{4,2},{5,197},{6,4},{7,199},{8,14},{9,... | collective-permute-start | bytes 3244040 | tf_op jit(solution)/shard_map/ppermute | solution.py:39
  57.9 1.2 copy-start.4
  59.1 33.8 %copy-start.8 = (f32[1,2048]{1,0:T(1,128)S(1)}, f32[1,2048]{1,0:T(1,128)}, u32[]{:S(2)}) copy-start(f32[1,2048]{1,0:T(1,128)} %bias.1) | copy-start | bytes 24580
  61.6 2.4 %collective-permute-start.9 = (bf16[512,256]{1,0:T(8,128)(2,1)S(1)}, bf16[512,256]{1,0:T(8,128)(2,1)S(1)}, u32[]{:S(2)}, u32[]{:S(2)}) collective-permute-start(bf16[512,256]{1,0:T(8,128)(2,1)S(1)} %get-tuple-element.25), channel_id=1, source_target_pairs={{0,1},{1,0},{2,3},{3,2},{4,5},{5,4},{6,7},{7,6},{8,9},{9,8},{10,11... | collective-permute-start | bytes 786440 | tf_op jit(solution)/shard_map/ppermute | solution.py:31
  64.1 17.6 %collective-permute-start.10 = (bf16[2,512,256]{2,1,0:T(8,128)(2,1)S(1)}, bf16[2,512,256]{2,1,0:T(8,128)(2,1)S(1)}, u32[]{:S(2)}, u32[]{:S(2)}) collective-permute-start(bf16[2,512,256]{2,1,0:T(8,128)(2,1)S(1)} %pad_maximum_fusion.a0), channel_id=1, source_target_pairs={{0,2},{1,65},{2,4},{3,67},{4,6},{5,69},{6,0},{7,71},{8,10},{9,73},... | collective-permute-start | bytes 1572872 | tf_op jit(solution)/shard_map/ppermute | solution.py:39
  64.7 17.1 %collective-permute-start.11 = (bf16[2,512,256]{2,1,0:T(8,128)(2,1)S(1)}, bf16[2,512,256]{2,1,0:T(8,128)(2,1)S(1)}, u32[]{:S(2)}, u32[]{:S(2)}) collective-permute-start(bf16[2,512,256]{2,1,0:T(8,128)(2,1)S(1)} %pad_maximum_fusion.a0), channel_id=1, source_target_pairs={{0,4},{1,129},{2,6},{3,131},{4,0},{5,133},{6,2},{7,135},{8,12},{9,... | collective-permute-start | bytes 1572872 | tf_op jit(solution)/shard_map/ppermute | solution.py:39
  67.1 25.8 %collective-permute-start.12 = (bf16[2,512,256]{2,1,0:T(8,128)(2,1)S(1)}, bf16[2,512,256]{2,1,0:T(8,128)(2,1)S(1)}, u32[]{:S(2)}, u32[]{:S(2)}) collective-permute-start(bf16[2,512,256]{2,1,0:T(8,128)(2,1)S(1)} %pad_maximum_fusion.a0), channel_id=1, source_target_pairs={{0,6},{1,193},{2,0},{3,195},{4,2},{5,197},{6,4},{7,199},{8,14},{9,... | collective-permute-start | bytes 1572872 | tf_op jit(solution)/shard_map/ppermute | solution.py:39
  97.6 1.0 copy-start.6
  98.6 1.0 copy-start.7
  99.6 27.8 %all-to-all-start.1 = ((bf16[32,16,1024]{2,1,0:T(8,128)(2,1)}), bf16[32,16,1024]{2,1,0:T(8,128)(2,1)S(1)}, u32[]{:S(2)}, u32[]{:S(2)}) async-start(bf16[32,16,1024]{2,1,0:T(8,128)(2,1)} %decode.1), calls=%async_computation.1 | async-start | bytes 2097152 | tf_op jit(solution)/shard_map/all_to_all | solution.py:45
  106.1 21.5 %slice-start.1 = ((bf16[528,1024]{1,0:T(8,128)(2,1)}), bf16[4,1024]{1,0:T(4,128)(2,1)S(1)}, s32[]{:S(2)}) async-start(bf16[528,1024]{1,0:T(8,128)(2,1)} %copy-done.6), calls=%async_computation.4 | async-start | bytes 16384 | tf_op jit(solution)/shard_map/slice | solution.py:230
  106.1 21.5 %slice-start.2 = ((bf16[528,1024]{1,0:T(8,128)(2,1)}), bf16[4,1024]{1,0:T(4,128)(2,1)S(1)}, s32[]{:S(2)}) async-start(bf16[528,1024]{1,0:T(8,128)(2,1)} %copy-done.7), calls=%async_computation.5 | async-start | bytes 16384 | tf_op jit(solution)/shard_map/slice | solution.py:230
  106.1 21.5 %slice-start = ((bf16[528,1024]{1,0:T(8,128)(2,1)}), bf16[4,1024]{1,0:T(4,128)(2,1)S(1)}, s32[]{:S(2)}) async-start(bf16[528,1024]{1,0:T(8,128)(2,1)} %copy-done.1), calls=%async_computation.3 | async-start | bytes 16384 | tf_op jit(solution)/shard_map/slice | solution.py:230
  156.1 25.9 %collective-permute-start.20 = (bf16[32,16,1024]{2,1,0:T(8,128)(2,1)S(1)}, bf16[32,16,1024]{2,1,0:T(8,128)(2,1)S(1)}, u32[]{:S(2)}, u32[]{:S(2)}) collective-permute-start(bf16[32,16,1024]{2,1,0:T(8,128)(2,1)S(1)} %all_to_all.22.own), channel_id=1, source_target_pairs={{0,2},{1,65},{2,4},{3,67},{4,6},{5,69},{6,0},{7,71},{8,10},{9,73},... | collective-permute-start | bytes 3145736 | tf_op jit(solution)/shard_map/ppermute | solution.py:39
  158.9 33.2 %collective-permute-start.18 = (bf16[32,16,1024]{2,1,0:T(8,128)(2,1)S(1)}, bf16[32,16,1024]{2,1,0:T(8,128)(2,1)S(1)}, u32[]{:S(2)}, u32[]{:S(2)}) collective-permute-start(bf16[32,16,1024]{2,1,0:T(8,128)(2,1)S(1)} %all_to_all.22.own), channel_id=1, source_target_pairs={{0,6},{1,193},{2,0},{3,195},{4,2},{5,197},{6,4},{7,199},{8,14},{9,... | collective-permute-start | bytes 3145736 | tf_op jit(solution)/shard_map/ppermute | solution.py:39
  169.1 29.4 %collective-permute-start.16 = (bf16[32,16,1024]{2,1,0:T(8,128)(2,1)S(1)}, bf16[32,16,1024]{2,1,0:T(8,128)(2,1)S(1)}, u32[]{:S(2)}, u32[]{:S(2)}) collective-permute-start(bf16[32,16,1024]{2,1,0:T(8,128)(2,1)S(1)} %all_to_all.22.own), channel_id=1, source_target_pairs={{0,4},{1,129},{2,6},{3,131},{4,0},{5,133},{6,2},{7,135},{8,12},{9,... | collective-permute-start | bytes 3145736 | tf_op jit(solution)/shard_map/ppermute | solution.py:39
  170.3 29.6 %collective-permute-start.22 = (bf16[32,16,1024]{2,1,0:T(8,128)(2,1)S(1)}, bf16[32,16,1024]{2,1,0:T(8,128)(2,1)S(1)}, u32[]{:S(2)}, u32[]{:S(2)}) collective-permute-start(bf16[32,16,1024]{2,1,0:T(8,128)(2,1)S(1)} %all_to_all.22.own), channel_id=1, source_target_pairs={{0,1},{1,0},{2,3},{3,2},{4,5},{5,4},{6,7},{7,6},{8,9},{9,8},{10,11... | collective-permute-start | bytes 3145736 | tf_op jit(solution)/shard_map/ppermute | solution.py:31
  182.0 20.4 %collective-permute-start.21 = (bf16[32,16,1024]{2,1,0:T(8,128)(2,1)S(1)}, bf16[32,16,1024]{2,1,0:T(8,128)(2,1)S(1)}, u32[]{:S(2)}, u32[]{:S(2)}) collective-permute-start(bf16[32,16,1024]{2,1,0:T(8,128)(2,1)S(1)} %collective-permute-done.20.own), channel_id=1, source_target_pairs={{0,1},{1,0},{2,3},{3,2},{4,5},{5,4},{6,7},{7,6},{8,9},{9,8},{10,11... | collective-permute-start | bytes 3145736 | tf_op jit(solution)/shard_map/ppermute | solution.py:31
  192.1 12.6 %collective-permute-start.19 = (bf16[32,16,1024]{2,1,0:T(8,128)(2,1)S(1)}, bf16[32,16,1024]{2,1,0:T(8,128)(2,1)S(1)}, u32[]{:S(2)}, u32[]{:S(2)}) collective-permute-start(bf16[32,16,1024]{2,1,0:T(8,128)(2,1)S(1)} %collective-permute-done.18.own), channel_id=1, source_target_pairs={{0,1},{1,0},{2,3},{3,2},{4,5},{5,4},{6,7},{7,6},{8,9},{9,8},{10,11... | collective-permute-start | bytes 3145736 | tf_op jit(solution)/shard_map/ppermute | solution.py:31
  198.6 8.5 %collective-permute-start.17 = (bf16[32,16,1024]{2,1,0:T(8,128)(2,1)S(1)}, bf16[32,16,1024]{2,1,0:T(8,128)(2,1)S(1)}, u32[]{:S(2)}, u32[]{:S(2)}) collective-permute-start(bf16[32,16,1024]{2,1,0:T(8,128)(2,1)S(1)} %collective-permute-done.16.own), channel_id=1, source_target_pairs={{0,1},{1,0},{2,3},{3,2},{4,5},{5,4},{6,7},{7,6},{8,9},{9,8},{10,11... | collective-permute-start | bytes 3145736 | tf_op jit(solution)/shard_map/ppermute | solution.py:31

commit v3 on v2

--- a/solution.py
+++ b/solution.py
@@ -39,10 +39,12 @@
     return lax.ppermute(value, ALL, pairs)
 
 
-def trade(value):
-    groups = [[device(x, z, y, 0) for x in range(NX) for z in range(NZ)] for y in range(NY)]
-    groups += [[device(x, z, y, 1) for y in range(NY) for z in range(NZ)] for x in range(NX)]
-    return lax.all_to_all(value, ALL, 0, 0, axis_index_groups=groups, tiled=True)
+def cross(value, step):
+    pairs = []
+    for x, z, y, core in coordinates():
+        there = (x, z, (y + step) % NY, core) if core == 1 else ((x + step) % NX, z, y, core)
+        pairs.append((device(x, z, y, core), device(*there)))
+    return lax.ppermute(value, ALL, pairs)
 
 
 def encoder_kernel(*refs):
@@ -69,20 +71,22 @@
     )(*pieces, weight, bias, place)
 
 
-def decoder_kernel(where, a0, a1, a2, a3, w0, w1, w2, w3, bias, out, total):
+def decoder_kernel(where, a0, a1, a2, a3, w0, w1, w2, w3, bias, *refs):
+    outs, total = refs[:-1], refs[-1]
     feats = a0.shape[2]
     x, z, y, core = (where[i] for i in range(4))
     adds_bias = (z == 0) & (((core == 0) & (x == y)) | ((core == 1) & (y == 0)))
-    total[...] = jnp.broadcast_to(jnp.where(adds_bias, bias[...], 0.0), total.shape)
+    value = jnp.where(adds_bias, bias[...], 0.0)
     for i, (a, w) in enumerate(((a0, w0), (a1, w1), (a2, w2), (a3, w3))):
-
-        @pl.when(((core == 0) & (y >= x)) | ((core == 1) & (x >= i)))
-        def _():
-            total[...] += jnp.dot(a[0], w[:feats, :], preferred_element_type=F32) + jnp.dot(
-                a[1], w[feats:2 * feats, :], preferred_element_type=F32
-            )
-
-    out[...] = total[...].astype(BF).reshape(out.shape)
+        term = jnp.dot(a[0], w[:feats, :], preferred_element_type=F32)
+        term += jnp.dot(a[1], w[feats:2 * feats, :], preferred_element_type=F32)
+        value += term if i == 0 else jnp.where((core == 0) | (x >= i), term, 0.0)
+    total[...] = jnp.where((core == 1) | (y >= x), value, 0.0)
+    first = jnp.where(core == 0, x, y)
+    for step, out in enumerate(outs):
+        span = total.shape[0] // len(outs)
+        start = pl.multiple_of(lax.rem(first + step, len(outs)) * span, span)
+        out[...] = total[pl.ds(start, span), :].astype(BF).reshape(out.shape)
 
 
 def decode(where, acts, weights, bias):
@@ -98,10 +102,10 @@
             in_specs=[pl.BlockSpec((cores, tokens, feats), lambda n, _: (0, 0, 0))] * NY
             + [pl.BlockSpec((rows, cols), lambda n, _: (0, n))] * NY
             + [pl.BlockSpec((1, cols), lambda n, where: (0, where[3] * blocks + n))],
-            out_specs=pl.BlockSpec((XZ, part, cols), lambda n, _: (0, 0, n)),
+            out_specs=[pl.BlockSpec((NZ, part, cols), lambda n, _: (0, 0, n))] * NX,
             scratch_shapes=[pltpu.VMEM((tokens, cols), F32)],
         ),
-        out_shape=jax.ShapeDtypeStruct((XZ, part, width), BF),
+        out_shape=[jax.ShapeDtypeStruct((NZ, part, width), BF)] * NX,
         compiler_params=pltpu.CompilerParams(vmem_limit_bytes=VMEM_LIMIT),
         cost_estimate=pl.CostEstimate(flops=22 * 10**8, bytes_accessed=8 * 10**6, transcendentals=0),
         name="decode",
@@ -114,16 +118,20 @@
     return lax.rem(first + NY - step, NY), lax.rem(second + NY - step, NY)
 
 
-def gradient_kernel(step, where, own, other, mine, give, *rest):
-    out = rest[-1]
+def gradient_kernel(step, count, where, *refs):
+    own, other, (mine, give), out = refs[:count], refs[count:2 * count], refs[2 * count:2 * count + 2], refs[-1]
     half = pl.program_id(0)
     sinks = sinks_at(where, step)
-    for i, (block, activity) in enumerate(((own, mine), (other, give))):
+    for i, (blocks, activity) in enumerate(((own, mine), (other, give))):
 
         @pl.when((half == i) & (sinks[i] >= where[0]))
         def _():
-            rhs = block[...].reshape(-1, block.shape[2])
-            out[0] = jnp.dot(activity[...], rhs, preferred_element_type=F32).astype(BF)
+            grad, start = 0.0, 0
+            for block in blocks:
+                rhs = block[...].reshape(-1, block.shape[2])
+                grad += jnp.dot(activity[:, start:start + rhs.shape[0]], rhs, preferred_element_type=F32)
+                start += rhs.shape[0]
+            out[0] = grad.astype(BF)
 
         @pl.when((half == i) & (sinks[i] < where[0]))
         def _():
@@ -131,7 +139,7 @@
 
 
 def gradient(step, where, layers, own, other, mine, give, before):
-    slots, part, cols = own.shape
+    _, part, cols = own[0].shape
     feats, tokens = mine.shape
     more = [] if before is None else [before]
 
@@ -140,21 +148,47 @@
         return jnp.where(half == 0, first, second), 0, jnp.where(half == 0, where[3], 1 - where[3])
 
     return pl.pallas_call(
-        functools.partial(gradient_kernel, step),
+        functools.partial(gradient_kernel, step, len(own)),
         grid_spec=pltpu.PrefetchScalarGridSpec(
             num_scalar_prefetch=1,
             grid=(NC,),
-            in_specs=[pl.BlockSpec((slots, part, cols), lambda h, _: (0, 0, 0))] * 2
+            in_specs=[pl.BlockSpec((piece.shape[0], part, cols), lambda h, _: (0, 0, 0)) for piece in own] * 2
             + [pl.BlockSpec((feats, tokens), lambda h, _: (0, 0))] * 2
             + [pl.BlockSpec(memory_space=pl.ANY)] * len(more),
             out_specs=pl.BlockSpec((1, feats, cols), place),
         ),
         out_shape=jax.ShapeDtypeStruct((layers, feats, NC * cols), BF),
-        input_output_aliases={5: 0} if more else {},
+        input_output_aliases={2 * len(own) + 3: 0} if more else {},
         compiler_params=pltpu.CompilerParams(vmem_limit_bytes=VMEM_LIMIT),
         cost_estimate=pl.CostEstimate(flops=55 * 10**7, bytes_accessed=4 * 10**6, transcendentals=0),
         name="gradient",
-    )(where, own, other, mine, give, *more)
+    )(where, *own, *other, mine, give, *more)
+
+
+def collect_kernel(where, *refs):
+    pieces, out = refs[:-1], refs[-1]
+    first = jnp.where(where[3] == 0, where[0], where[2])
+    for step, piece in enumerate(pieces):
+        source = lax.rem(first + len(pieces) - step, len(pieces))
+        out[pl.ds(source * piece.shape[0], piece.shape[0])] = piece[...]
+
+
+def collect(where, pieces):
+    count, part, width = pieces[0].shape
+    cols = width // 2
+    return pl.pallas_call(
+        collect_kernel,
+        grid_spec=pltpu.PrefetchScalarGridSpec(
+            num_scalar_prefetch=1,
+            grid=(2,),
+            in_specs=[pl.BlockSpec((count, part, cols), lambda n, _: (0, 0, n))] * len(pieces),
+            out_specs=pl.BlockSpec((count * len(pieces), part, cols), lambda n, _: (0, 0, n)),
+        ),
+        out_shape=jax.ShapeDtypeStruct((count * len(pieces), part, width), BF),
+        compiler_params=pltpu.CompilerParams(vmem_limit_bytes=VMEM_LIMIT),
+        cost_estimate=pl.CostEstimate(flops=0, bytes_accessed=2 * 10**6, transcendentals=0),
+        name="collect",
+    )(where, *pieces)
 
 
 def pack_kernel(where, own, other, target, out):
@@ -203,21 +237,24 @@
     give = lax.dynamic_slice_in_dim(dec_weight[0], (1 - core) * half, half, axis=2)
     aims = target.transpose(1, 0, 2).reshape(layers, mine, NC, half)
     aims = jnp.where(core == 0, jnp.stack([aims[:, :, 0], aims[:, :, 1]]), jnp.stack([aims[:, :, 1], aims[:, :, 0]]))
-    rows = jnp.broadcast_to(resid.transpose(1, 0, 2)[:, None], (layers, NZ, mine, width))
-    rows = rows.reshape(XZ * mine, width)
+    rows = resid.transpose(1, 0, 2)
     rows, give, aims, where = lax.optimization_barrier((rows, give, aims, where))
     extra = jnp.concatenate([aims[0], shift(aims[1], "c", 1), jnp.zeros((layers, 16 - 2 * mine, half), BF)], axis=1)
     give = shift(give, "c", 1)
     weights = [pack(step, where, dec_weight[0], give, extra) for step in range(NY)]
-    rows = lax.all_to_all(rows, ("x", "z"), 0, 0, tiled=True)
-    rows, *weights = lax.optimization_barrier((rows, *weights))
-    weights = [ring(piece, step) if step else piece for step, piece in enumerate(weights)]
+    rows = lax.all_to_all(rows, "x", 0, 0, tiled=True)
+    rows, *sent = lax.optimization_barrier((rows, *weights[1:]))
+    weights = weights[:1] + [ring(piece, step) for step, piece in enumerate(sent, 1)]
+    rows = jnp.broadcast_to(rows.reshape(1, layers * mine, width), (NZ, layers * mine, width))
+    rows = lax.all_to_all(rows, "z", 0, 0, tiled=True).reshape(XZ * mine, width)
+    rows, w1, w3 = lax.optimization_barrier((rows, weights[1], weights[3]))
+    weights = [weights[0], w1, weights[2], w3]
     pieces = [rows] + [shift(rows, "y", step) for step in range(1, NY)]
     pieces = pieces + [shift(piece, "c", 1) for piece in pieces]
     r = jnp.arange(tokens)
     r_core = jnp.where(r // (tokens // 2) == 0, core, 1 - core)
     r_y = (y + NY - r // (tokens // 8) % NY) % NY
-    r_x, r_z, r_i = r // (mine * NZ) % NX, r // mine % NZ, r % mine
+    r_x, r_z, r_i = r // mine % NX, r // (mine * NX) % NZ, r % mine
     order = [((a * NZ + r_z) * 4 + b) * NC * mine + r_core * mine + r_i for a, b in ((r_x, r_y), (r_y, r_x))]
     order = jnp.stack([jnp.where(core == 0, order[0], order[1]), jnp.where(core == 0, order[1], order[0])])
     place = (jnp.arange(tokens)[None, :, None] == order[:, None, :]).astype(BF)
@@ -233,17 +270,25 @@
     q = (sink + NY - q // (NC * mine)) % NY * NC * mine + q_core * mine + q % mine
     wanted = jnp.dot((jnp.arange(q.shape[0])[:, None] == q[None, :]).astype(BF), wanted, preferred_element_type=F32)
 
-    got = trade(parts)
+    parts = [part if step == 0 else cross(part, step) for step, part in enumerate(parts)]
     own, away = own.T, away.T
-    got, own, away = lax.optimization_barrier((got, own, away))
+    *parts, own, away = lax.optimization_barrier((*parts, own, away))
+    total = sum(part.astype(F32) for part in parts).astype(BF)
+    got = lax.all_to_all(total, "z", 0, 0, tiled=True)
     misfit = jnp.sum(got.astype(F32), axis=0) - wanted
     cotangent = (misfit * factor).astype(BF)
-    block = trade(jnp.broadcast_to(cotangent[None], (XZ,) + cotangent.shape))
-
+
+    block = lax.all_to_all(jnp.broadcast_to(cotangent[None], (NZ,) + cotangent.shape), "z", 0, 0, tiled=True)
+    block = collect(where, [block] + [cross(block, step) for step in range(1, NX)])
+    before, after = ring(block, 1), ring(block, 3)
+    middle = XZ // 2
+    far = [ring(after[:middle], 3), ring(before[middle:], 1)]
     grads = None
-    blocks = [block] + [ring(block, step) for step in range(1, NY)]
-    for step in (0, 1, 3, 2):
-        grads = gradient(step, where, layers, blocks[step], shift(blocks[step], "c", 1), own, away, grads)
+    for step, pieces in ((0, [block]), (1, [before]), (3, [after]), (2, far)):
+        if step == 2:
+            *pieces, grads = lax.optimization_barrier((*pieces, grads))
+        others = [shift(piece, "c", 1) for piece in pieces]
+        grads = gradient(step, where, layers, pieces, others, own, away, grads)
     return grads[None]
 
 

time: 210 us -> 183 us (0.87)
  starting transfers between devices: 77.5 us -> 59.4 us
  waiting for transfers between devices: 66.9 us -> 57.3 us
  local copies, waits for them, and re-layouts: 14.3 us -> 11.8 us
  Pallas kernels: 21.2 us -> 23.5 us
    all_to_all x2, waiting for transfers between devices: 29.2 us -> 7.87 us  [the longest x1 7.86 us: body(): got = lax.all_to_all(total, 'z', 0, 0, tiled=True)]
    ppermute x0 -> x6, waiting for transfers between devices: none -> 12 us  [cross(): return lax.ppermute(value, ALL, pairs)]
    ppermute x0 -> x6, starting transfers between devices: none -> 10.6 us  [cross(): return lax.ppermute(value, ALL, pairs)]
    ppermute x14 -> x15, starting transfers between devices: 40.2 us -> 30.3 us  [shift(): lax.ppermute(value, axis, [(i, (i + step) % size) for i in range(size)])]
    ppermute x9 -> x10, starting transfers between devices: 21.5 us -> 11.8 us  [ring(): return lax.ppermute(value, ALL, pairs)]
    ppermute x9 -> x10, waiting for transfers between devices: 34.2 us -> 24.6 us  [ring(): return lax.ppermute(value, ALL, pairs)]
    ppermute x14 -> x15, waiting for transfers between devices: 3.51 us -> 12.9 us  [shift(): lax.ppermute(value, axis, [(i, (i + step) % size) for i in range(size)])]
    all_to_all x2, starting transfers between devices: 15.8 us -> 6.68 us  [the longest x1 3.41 us: body(): got = lax.all_to_all(total, 'z', 0, 0, tiled=True)]
  transfers between devices with their start and end apart: 25 -> 33, of which waited for: 11 -> 18; matrix products, arithmetic and copies ran while one was open for 1% -> 1% of each run, Pallas kernels for 5% -> 8%
where the time goes in v3:
time: 183 us; the launch traced here: 182 us
  starting transfers between devices  59.4 us (32%)
  waiting for transfers between devices  57.3 us (31%)
  blocking collectives  28.3 us (15%)
  Pallas kernels  23.5 us (13%)
  local copies, waits for them, and re-layouts  11.8 us (6%)
    ppermute x15, starting transfers between devices, shift(): lax.ppermute(value, axis, [(i, (i + step) % size) for i in range(size)])  30.3 us
    ppermute x10, waiting for transfers between devices, ring(): return lax.ppermute(value, ALL, pairs)  24.6 us
    all_to_all x1, blocking collectives, body(): rows = lax.all_to_all(rows, 'z', 0, 0, tiled=True).reshape(XZ * mine, width)  16.5 us
    ppermute x15, waiting for transfers between devices, shift(): lax.ppermute(value, axis, [(i, (i + step) % size) for i in range(size)])  12.9 us
    ppermute x6, waiting for transfers between devices, cross(): return lax.ppermute(value, ALL, pairs)  12 us
    all_to_all x1, blocking collectives, body(): lax.all_to_all(jnp.broadcast_to(cotangent[None], (NZ,) + cotangent.shape)...  11.8 us
    ppermute x10, starting transfers between devices, ring(): return lax.ppermute(value, ALL, pairs)  11.8 us
    ppermute x6, starting transfers between devices, cross(): return lax.ppermute(value, ALL, pairs)  10.6 us
  transfers between devices with their start and end apart: 33, of which 18 were waited for; matrix products, arithmetic and copies ran while one was open for 1% of the time, Pallas kernels for 8%

profile of v3, /device:TPU:1, one launch (start us, length us, event | category | flops | bytes accessed | tf_op | source)
XLA Modules:
  0.0 182.3 jit_solution(817822991496929634)
XLA Ops:
  0.0 0.8 reshape.384
  0.8 1.4 copy.32
  2.2 3.1 %dynamic-slice_bitcast_fusion = bf16[4,256,1024]{2,1,0:T(8,128)(2,1)} fusion(bf16[1,4,256,2048]{3,2,1,0:T(8,128)(2,1)} %param.10, s32[]{:T(128)S(6)} %select_n.251), kind=kLoop, calls=%fused_computation.1 | loop fusion | bytes 4194308 | tf_op jit(solution)/shard_map/dynamic_slice | solution.py:237
  5.5 3.3 %collective-permute-start = (bf16[4,256,1024]{2,1,0:T(8,128)(2,1)}, bf16[4,256,1024]{2,1,0:T(8,128)(2,1)S(1)}, u32[]{:S(2)}, u32[]{:S(2)}) collective-permute-start(bf16[4,256,1024]{2,1,0:T(8,128)(2,1)} %dynamic-slice_bitcast_fusion), channel_id=1, source_target_pairs={{0,1},{1,0},{2,3},{3,2},{4,5},{5,4},{6,7},{7,6},{8,9},{9,8},{10,11... | collective-permute-start | bytes 6291464 | tf_op jit(solution)/shard_map/ppermute | solution.py:31
  8.9 3.3 %all-to-all-start = ((bf16[4,2,2048]{2,1,0:T(2,128)(2,1)}), bf16[4,2,2048]{2,1,0:T(2,128)(2,1)S(1)}, u32[]{:S(2)}, u32[]{:S(2)}) async-start(bf16[4,2,2048]{2,1,0:T(2,128)(2,1)} %bitcast.27), calls=%async_computation | async-start | bytes 65536 | tf_op jit(solution)/shard_map/all_to_all | solution.py:245
  12.3 0.2 collective-permute-done.1
  12.6 0.3 collective-permute-done.other
  12.8 2.2 %copy-done = bf16[1,4,256,2048]{3,2,1,0:T(8,128)(2,1)S(1)} copy-done((bf16[1,4,256,2048]{3,2,1,0:T(8,128)(2,1)S(1)}, bf16[1,4,256,2048]{3,2,1,0:T(8,128)(2,1)}, u32[]{:S(2)}) %copy-start) | copy-done | bytes 4194328
  15.0 0.9 pack.6
  15.9 1.8 pack.5
  17.7 0.9 pack.4
  18.6 1.0 copy-done.2
  19.6 1.0 collective-permute-start.2
  20.6 1.7 collective-permute-start.3
  22.3 16.5 %all_to_all.20 = bf16[8,8,2048]{2,1,0:T(8,128)(2,1)} all-to-all(bf16[8,8,2048]{2,1,0:T(8,128)(2,1)S(1)} %broadcast_in_dim.41), channel_id=1, replica_groups=mesh['x'=4,'z'=8,'y'=4,'c'=2] {'z'}, dimensions={0} | all-to-all | bytes 524288 | tf_op jit(solution)/shard_map/all_to_all | solution.py:249
  38.8 5.3 %collective-permute-start.6 = (bf16[64,2048]{1,0:T(8,128)(2,1)}, bf16[64,2048]{1,0:T(8,128)(2,1)S(1)}, u32[]{:S(2)}, u32[]{:S(2)}) collective-permute-start(bf16[64,2048]{1,0:T(8,128)(2,1)} %bitcast.12.refs_0_), channel_id=1, source_target_pairs={{0,6},{2,0},{4,2},{6,4},{1,7},{3,1},{5,3},{7,5},{8,14},{10,8},{12,... | collective-permute-start | bytes 786440 | tf_op jit(solution)/shard_map/ppermute | solution.py:31
  44.1 1.6 collective-permute-start.5
  45.8 1.4 collective-permute-start.7
  47.2 7.9 %collective-permute-done.6.refs_3_ = bf16[64,2048]{1,0:T(8,128)(2,1)S(1)} collective-permute-done((bf16[64,2048]{1,0:T(8,128)(2,1)}, bf16[64,2048]{1,0:T(8,128)(2,1)S(1)}, u32[]{:S(2)}, u32[]{:S(2)}) %collective-permute-start.6) | collective-permute-done | bytes 262176 | tf_op jit(solution)/shard_map/ppermute | solution.py:31
  55.1 1.5 collective-permute-start.10
  56.6 3.3 %collective-permute-start.8 = (bf16[64,2048]{1,0:T(8,128)(2,1)S(1)}, bf16[64,2048]{1,0:T(8,128)(2,1)S(1)}, u32[]{:S(2)}, u32[]{:S(2)}) collective-permute-start(bf16[64,2048]{1,0:T(8,128)(2,1)S(1)} %collective-permute-done.4.refs_1_), channel_id=1, source_target_pairs={{0,1},{1,0},{2,3},{3,2},{4,5},{5,4},{6,7},{7,6},{8,9},{9,8},{10,11... | collective-permute-start | bytes 786440 | tf_op jit(solution)/shard_map/ppermute | solution.py:31
  60.0 0.3 fusion.refs_10_
  60.4 0.7 collective-permute-done.8.refs_5_
  61.0 0.4 collective-permute-done.9.refs_6_
  61.4 1.2 copy-done.3
  62.6 2.7 %encode.1 = (bf16[512,256]{1,0:T(8,128)(2,1)S(1)}, bf16[512,256]{1,0:T(8,128)(2,1)S(1)}) custom-call(bf16[64,2048]{1,0:T(8,128)(2,1)} %bitcast.12.refs_0_, bf16[64,2048]{1,0:T(8,128)(2,1)S(1)} %collective-permute-done.4.refs_1_, bf16[64,2048]{1,0:T(8,128)(2,1)S(1)} %collective-permute-done.5.refs_2_, bf16[64,2048]{1,0:T(8,128)(2,1)S(1)} %collective-permute-done.6.refs_3_, ...), custom_call_target="tpu_custom_call" | custom-call | flops 800000000 | bytes 4000000 | tf_op jit(solution)/shard_map/encode/pallas_call | solution.py:64
  65.3 0.5 collective-permute-start.11
  65.8 1.2 collective-permute-done.11
  67.1 2.2 %collective-permute-start.13 = (bf16[2,512,256]{2,1,0:T(8,128)(2,1)S(1)}, bf16[2,512,256]{2,1,0:T(8,128)(2,1)S(1)}, u32[]{:S(2)}, u32[]{:S(2)}) collective-permute-start(bf16[2,512,256]{2,1,0:T(8,128)(2,1)S(1)} %pad_maximum_fusion.a0), channel_id=1, source_target_pairs={{0,4},{1,129},{2,6},{3,131},{4,0},{5,133},{6,2},{7,135},{8,12},{9,... | collective-permute-start | bytes 1572872 | tf_op jit(solution)/shard_map/ppermute | solution.py:39
  69.3 1.8 collective-permute-start.14
  71.1 0.9 pack.7.w0
  72.0 4.0 %collective-permute-done.15.w2 = bf16[528,1024]{1,0:T(8,128)(2,1)S(1)} collective-permute-done((bf16[528,1024]{1,0:T(8,128)(2,1)}, bf16[528,1024]{1,0:T(8,128)(2,1)S(1)}, u32[]{:S(2)}, u32[]{:S(2)}) %collective-permute-start.15) | collective-permute-done | bytes 1081376 | tf_op jit(solution)/shard_map/ppermute | solution.py:39
  76.0 5.6 %collective-permute-done.12.a1 = bf16[2,512,256]{2,1,0:T(8,128)(2,1)S(1)} collective-permute-done((bf16[2,512,256]{2,1,0:T(8,128)(2,1)S(1)}, bf16[2,512,256]{2,1,0:T(8,128)(2,1)S(1)}, u32[]{:S(2)}, u32[]{:S(2)}) %collective-permute-start.12) | collective-permute-done | bytes 524320 | tf_op jit(solution)/shard_map/ppermute | solution.py:39
  81.6 5.7 %collective-permute-done.13.a2 = bf16[2,512,256]{2,1,0:T(8,128)(2,1)S(1)} collective-permute-done((bf16[2,512,256]{2,1,0:T(8,128)(2,1)S(1)}, bf16[2,512,256]{2,1,0:T(8,128)(2,1)S(1)}, u32[]{:S(2)}, u32[]{:S(2)}) %collective-permute-start.13) | collective-permute-done | bytes 524320 | tf_op jit(solution)/shard_map/ppermute | solution.py:39
  87.3 6.0 %decode.1 = (bf16[8,16,1024]{2,1,0:T(8,128)(2,1)S(1)}, bf16[8,16,1024]{2,1,0:T(8,128)(2,1)}, bf16[8,16,1024]{2,1,0:T(8,128)(2,1)}, bf16[8,16,1024]{2,1,0:T(8,128)(2,1)}) custom-call(s32[4]{0:T(128)S(1)} %pad_add_fusion.1.where, bf16[2,512,256]{2,1,0:T(8,128)(2,1)S(1)} %pad_maximum_fusion.a0, bf16[2,512,256]{2,1,0:T(8,128)(2,1)S(1)} %collective-permute-done.12.a1, ...), custom_call_target="tpu_custom_call" | custom-call | flops 2200000000 | bytes 8000000 | tf_op jit(solution)/shard_map/decode/pallas_call | solution.py:97
  93.4 1.3 collective-permute-start.17
  94.7 1.4 collective-permute-start.18
  96.4 6.8 %collective-permute-done.16 = bf16[8,16,1024]{2,1,0:T(8,128)(2,1)S(1)} collective-permute-done((bf16[8,16,1024]{2,1,0:T(8,128)(2,1)}, bf16[8,16,1024]{2,1,0:T(8,128)(2,1)S(1)}, u32[]{:S(2)}, u32[]{:S(2)}) %collective-permute-start.16) | collective-permute-done | bytes 262176 | tf_op jit(solution)/shard_map/ppermute | solution.py:47
  103.1 0.6 collective-permute-done.18
  103.8 0.9 add_convert_fusion
  104.6 3.4 %all-to-all-start.2 = ((bf16[8,16,1024]{2,1,0:T(8,128)(2,1)}), bf16[8,16,1024]{2,1,0:T(8,128)(2,1)S(1)}, u32[]{:S(2)}, u32[]{:S(2)}) async-start(bf16[8,16,1024]{2,1,0:T(8,128)(2,1)} %add_convert_fusion), calls=%async_computation.2 | async-start | bytes 524288 | tf_op jit(solution)/shard_map/all_to_all | solution.py:277
  108.1 0.7 slice.37
  108.8 0.7 slice.39
  109.5 7.9 %all-to-all-done.2 = bf16[8,16,1024]{2,1,0:T(8,128)(2,1)S(1)} async-done(((bf16[8,16,1024]{2,1,0:T(8,128)(2,1)}), bf16[8,16,1024]{2,1,0:T(8,128)(2,1)S(1)}, u32[]{:S(2)}, u32[]{:S(2)}) %all-to-all-start.2) | async-done | bytes 262176 | tf_op jit(solution)/shard_map/all_to_all | solution.py:277
  117.6 11.8 %all_to_all.21.refs_0_ = bf16[8,16,1024]{2,1,0:T(8,128)(2,1)S(1)} all-to-all(bf16[8,16,1024]{2,1,0:T(8,128)(2,1)S(1)} %broadcast_in_dim.46), channel_id=1, replica_groups=mesh['x'=4,'z'=8,'y'=4,'c'=2] {'z'}, dimensions={0} | all-to-all | bytes 524288 | tf_op jit(solution)/shard_map/all_to_all | solution.py:281
  129.5 5.5 %collective-permute-start.19 = (bf16[8,16,1024]{2,1,0:T(8,128)(2,1)S(1)}, bf16[8,16,1024]{2,1,0:T(8,128)(2,1)S(1)}, u32[]{:S(2)}, u32[]{:S(2)}) collective-permute-start(bf16[8,16,1024]{2,1,0:T(8,128)(2,1)S(1)} %all_to_all.21.refs_0_), channel_id=1, source_target_pairs={{0,64},{1,3},{2,66},{3,5},{4,68},{5,7},{6,70},{7,1},{8,72},{9,11},... | collective-permute-start | bytes 786440 | tf_op jit(solution)/shard_map/ppermute | solution.py:47
  134.9 2.4 %collective-permute-start.21 = (bf16[8,16,1024]{2,1,0:T(8,128)(2,1)S(1)}, bf16[8,16,1024]{2,1,0:T(8,128)(2,1)S(1)}, u32[]{:S(2)}, u32[]{:S(2)}) collective-permute-start(bf16[8,16,1024]{2,1,0:T(8,128)(2,1)S(1)} %all_to_all.21.refs_0_), channel_id=1, source_target_pairs={{0,192},{1,7},{2,194},{3,1},{4,196},{5,3},{6,198},{7,5},{8,200},{9... | collective-permute-start | bytes 786440 | tf_op jit(solution)/shard_map/ppermute | solution.py:47
  137.3 0.9 collective-permute-done.19.refs_1_
  138.3 3.7 %collective-permute-done.20.refs_2_ = bf16[8,16,1024]{2,1,0:T(8,128)(2,1)S(1)} collective-permute-done((bf16[8,16,1024]{2,1,0:T(8,128)(2,1)S(1)}, bf16[8,16,1024]{2,1,0:T(8,128)(2,1)S(1)}, u32[]{:S(2)}, u32[]{:S(2)}) %collective-permute-start.20) | collective-permute-done | bytes 262176 | tf_op jit(solution)/shard_map/ppermute | solution.py:47
  142.0 0.8 collect.1.refs_0_
  142.9 2.7 %collective-permute-start.22 = (bf16[32,16,1024]{2,1,0:T(8,128)(2,1)S(1)}, bf16[32,16,1024]{2,1,0:T(8,128)(2,1)S(1)}, u32[]{:S(2)}, u32[]{:S(2)}) collective-permute-start(bf16[32,16,1024]{2,1,0:T(8,128)(2,1)S(1)} %collect.1.refs_0_), channel_id=1, source_target_pairs={{0,6},{1,193},{2,0},{3,195},{4,2},{5,197},{6,4},{7,199},{8,14},{9,... | collective-permute-start | bytes 3145736 | tf_op jit(solution)/shard_map/ppermute | solution.py:39
  145.6 5.2 %collective-permute-start.28 = (bf16[32,16,1024]{2,1,0:T(8,128)(2,1)S(1)}, bf16[32,16,1024]{2,1,0:T(8,128)(2,1)S(1)}, u32[]{:S(2)}, u32[]{:S(2)}) collective-permute-start(bf16[32,16,1024]{2,1,0:T(8,128)(2,1)S(1)} %collect.1.refs_0_), channel_id=1, source_target_pairs={{0,1},{1,0},{2,3},{3,2},{4,5},{5,4},{6,7},{7,6},{8,9},{9,8},{10,11... | collective-permute-start | bytes 3145736 | tf_op jit(solution)/shard_map/ppermute | solution.py:31
  150.8 7.3 %collective-permute-done.24.refs_0_ = bf16[32,16,1024]{2,1,0:T(8,128)(2,1)S(1)} collective-permute-done((bf16[32,16,1024]{2,1,0:T(8,128)(2,1)S(1)}, bf16[32,16,1024]{2,1,0:T(8,128)(2,1)S(1)}, u32[]{:S(2)}, u32[]{:S(2)}) %collective-permute-start.24) | collective-permute-done | bytes 1048608 | tf_op jit(solution)/shard_map/ppermute | solution.py:39
  158.1 5.5 %collective-permute-start.27 = (bf16[32,16,1024]{2,1,0:T(8,128)(2,1)S(1)}, bf16[32,16,1024]{2,1,0:T(8,128)(2,1)S(1)}, u32[]{:S(2)}, u32[]{:S(2)}) collective-permute-start(bf16[32,16,1024]{2,1,0:T(8,128)(2,1)S(1)} %collective-permute-done.24.refs_0_), channel_id=1, source_target_pairs={{0,1},{1,0},{2,3},{3,2},{4,5},{5,4},{6,7},{7,6},{8,9},{9,8},{10,11... | collective-permute-start | bytes 3145736 | tf_op jit(solution)/shard_map/ppermute | solution.py:31
  163.6 1.6 collective-permute-start.23
  165.2 0.7 collective-permute-start.25
  165.9 2.4 %gradient.4.refs_4_ = bf16[4,256,2048]{2,1,0:T(8,128)(2,1)} custom-call(s32[4]{0:T(128)S(1)} %pad_add_fusion.1.where, bf16[32,16,1024]{2,1,0:T(8,128)(2,1)S(1)} %collect.1.refs_0_, bf16[32,16,1024]{2,1,0:T(8,128)(2,1)S(1)} %collective-permute-done.28.refs_1_, bf16[256,512]{1,0:T(8,128)(2,1)S(1)} %bitcast.32, bf16[256,512]{1,0:T(8,128)(2,1)S(1)} %bitcast.36), custom_call_target="tpu_custom_call" | custom-call | flops 550000000 | bytes 4000000 | tf_op jit(solution)/shard_map/gradient/pallas_call | solution.py:150
  168.3 2.4 %gradient.5.refs_4_ = bf16[4,256,2048]{2,1,0:T(8,128)(2,1)} custom-call(s32[4]{0:T(128)S(1)} %pad_add_fusion.1.where, bf16[32,16,1024]{2,1,0:T(8,128)(2,1)S(1)} %collective-permute-done.24.refs_0_, bf16[32,16,1024]{2,1,0:T(8,128)(2,1)S(1)} %collective-permute-done.27.refs_1_, bf16[256,512]{1,0:T(8,128)(2,1)S(1)} %bitcast.33, ...), custom_call_target="tpu_custom_call", output_to_operand_aliasing={{}: (5, {})} | custom-call | flops 550000000 | bytes 4000000 | tf_op jit(solution)/shard_map/gradient/pallas_call | solution.py:150
  170.6 2.4 %gradient.6.refs_6_ = bf16[4,256,2048]{2,1,0:T(8,128)(2,1)} custom-call(s32[4]{0:T(128)S(1)} %pad_add_fusion.1.where, bf16[32,16,1024]{2,1,0:T(8,128)(2,1)S(1)} %collective-permute-done.22.refs_0_, bf16[32,16,1024]{2,1,0:T(8,128)(2,1)S(1)} %collective-permute-done.26.refs_1_, bf16[256,512]{1,0:T(8,128)(2,1)S(1)} %bitcast.34, ...), custom_call_target="tpu_custom_call", output_to_operand_aliasing={{}: (5, {})} | custom-call | flops 550000000 | bytes 4000000 | tf_op jit(solution)/shard_map/gradient/pallas_call | solution.py:150
  173.0 2.1 %collective-permute-done.25.refs_1_ = bf16[16,16,1024]{2,1,0:T(8,128)(2,1)S(1)} collective-permute-done((bf16[16,16,1024]{2,1,0:T(8,128)(2,1)S(1)}, bf16[16,16,1024]{2,1,0:T(8,128)(2,1)S(1)}, u32[]{:S(2)}, u32[]{:S(2)}) %collective-permute-start.25) | collective-permute-done | bytes 524320 | tf_op jit(solution)/shard_map/ppermute | solution.py:39
  175.0 2.6 %collective-permute-start.29 = (bf16[16,16,1024]{2,1,0:T(8,128)(2,1)S(1)}, bf16[16,16,1024]{2,1,0:T(8,128)(2,1)S(1)}, u32[]{:S(2)}, u32[]{:S(2)}) collective-permute-start(bf16[16,16,1024]{2,1,0:T(8,128)(2,1)S(1)} %collective-permute-done.23.refs_0_), channel_id=1, source_target_pairs={{0,1},{1,0},{2,3},{3,2},{4,5},{5,4},{6,7},{7,6},{8,9},{9,8},{10,11... | collective-permute-start | bytes 1572872 | tf_op jit(solution)/shard_map/ppermute | solution.py:31
  177.7 1.5 collective-permute-done.29.refs_2_
  179.2 0.7 collective-permute-done.30.refs_3_
  179.9 2.4 %gradient.7 = bf16[4,256,2048]{2,1,0:T(8,128)(2,1)} custom-call(s32[4]{0:T(128)S(1)} %pad_add_fusion.1.where, bf16[16,16,1024]{2,1,0:T(8,128)(2,1)S(1)} %collective-permute-done.23.refs_0_, bf16[16,16,1024]{2,1,0:T(8,128)(2,1)S(1)} %collective-permute-done.25.refs_1_, ...), custom_call_target="tpu_custom_call", output_to_operand_aliasing={{}: (7, {})} | custom-call | flops 550000000 | bytes 4000000 | tf_op jit(solution)/shard_map/gradient/pallas_call | solution.py:150
  (68 shorter events, 1.7 us)
Async XLA Ops:
  5.5 7.3 %collective-permute-start = (bf16[4,256,1024]{2,1,0:T(8,128)(2,1)}, bf16[4,256,1024]{2,1,0:T(8,128)(2,1)S(1)}, u32[]{:S(2)}, u32[]{:S(2)}) collective-permute-start(bf16[4,256,1024]{2,1,0:T(8,128)(2,1)} %dynamic-slice_bitcast_fusion), channel_id=1, source_target_pairs={{0,1},{1,0},{2,3},{3,2},{4,5},{5,4},{6,7},{7,6},{8,9},{9,8},{10,11... | collective-permute-start | bytes 6291464 | tf_op jit(solution)/shard_map/ppermute | solution.py:31
  8.8 3.7 %collective-permute-start.1 = (bf16[4,2,1024]{2,1,0:T(2,128)(2,1)S(1)}, bf16[4,2,1024]{2,1,0:T(2,128)(2,1)S(1)}, u32[]{:S(2)}, u32[]{:S(2)}) collective-permute-start(bf16[4,2,1024]{2,1,0:T(2,128)(2,1)S(1)} %get-tuple-element.58), channel_id=1, source_target_pairs={{0,1},{1,0},{2,3},{3,2},{4,5},{5,4},{6,7},{7,6},{8,9},{9,8},{10,11... | collective-permute-start | bytes 49160 | tf_op jit(solution)/shard_map/ppermute | solution.py:31
  8.9 10.7 %all-to-all-start = ((bf16[4,2,2048]{2,1,0:T(2,128)(2,1)}), bf16[4,2,2048]{2,1,0:T(2,128)(2,1)S(1)}, u32[]{:S(2)}, u32[]{:S(2)}) async-start(bf16[4,2,2048]{2,1,0:T(2,128)(2,1)} %bitcast.27), calls=%async_computation | async-start | bytes 65536 | tf_op jit(solution)/shard_map/all_to_all | solution.py:245
  12.8 2.2 %copy-start = (bf16[1,4,256,2048]{3,2,1,0:T(8,128)(2,1)S(1)}, bf16[1,4,256,2048]{3,2,1,0:T(8,128)(2,1)}, u32[]{:S(2)}) copy-start(bf16[1,4,256,2048]{3,2,1,0:T(8,128)(2,1)} %param.10) | copy-start | bytes 12582916
  17.7 43.7 %copy-start.8 = (f32[1,256]{1,0:T(1,128)S(1)}, f32[1,256]{1,0:T(1,128)}, u32[]{:S(2)}) copy-start(f32[1,256]{1,0:T(1,128)} %refs_9_.1) | copy-start | bytes 3076
  18.6 1.0 copy-start.2
  19.6 19.2 %collective-permute-start.2 = (bf16[528,1024]{1,0:T(8,128)(2,1)}, bf16[528,1024]{1,0:T(8,128)(2,1)}, u32[]{:S(2)}, u32[]{:S(2)}) collective-permute-start(bf16[528,1024]{1,0:T(8,128)(2,1)} %copy-done.2), channel_id=1, source_target_pairs={{0,2},{1,65},{2,4},{3,67},{4,6},{5,69},{6,0},{7,71},{8,10},{9,73},... | collective-permute-start | bytes 3244040 | tf_op jit(solution)/shard_map/ppermute | solution.py:39
  20.6 18.2 %collective-permute-start.3 = (bf16[528,1024]{1,0:T(8,128)(2,1)S(1)}, bf16[528,1024]{1,0:T(8,128)(2,1)}, u32[]{:S(2)}, u32[]{:S(2)}) collective-permute-start(bf16[528,1024]{1,0:T(8,128)(2,1)S(1)} %pack.6), channel_id=1, source_target_pairs={{0,6},{1,193},{2,0},{3,195},{4,2},{5,197},{6,4},{7,199},{8,14},{9,... | collective-permute-start | bytes 3244040 | tf_op jit(solution)/shard_map/ppermute | solution.py:39
  38.8 16.3 %collective-permute-start.6 = (bf16[64,2048]{1,0:T(8,128)(2,1)}, bf16[64,2048]{1,0:T(8,128)(2,1)S(1)}, u32[]{:S(2)}, u32[]{:S(2)}) collective-permute-start(bf16[64,2048]{1,0:T(8,128)(2,1)} %bitcast.12.refs_0_), channel_id=1, source_target_pairs={{0,6},{2,0},{4,2},{6,4},{1,7},{3,1},{5,3},{7,5},{8,14},{10,8},{12,... | collective-permute-start | bytes 786440 | tf_op jit(solution)/shard_map/ppermute | solution.py:31
  44.1 12.5 %collective-permute-start.4 = (bf16[64,2048]{1,0:T(8,128)(2,1)}, bf16[64,2048]{1,0:T(8,128)(2,1)S(1)}, u32[]{:S(2)}, u32[]{:S(2)}) collective-permute-start(bf16[64,2048]{1,0:T(8,128)(2,1)} %bitcast.12.refs_0_), channel_id=1, source_target_pairs={{0,2},{2,4},{4,6},{6,0},{1,3},{3,5},{5,7},{7,1},{8,10},{10,12},{12... | collective-permute-start | bytes 786440 | tf_op jit(solution)/shard_map/ppermute | solution.py:31
  44.1 15.8 %collective-permute-start.5 = (bf16[64,2048]{1,0:T(8,128)(2,1)}, bf16[64,2048]{1,0:T(8,128)(2,1)S(1)}, u32[]{:S(2)}, u32[]{:S(2)}) collective-permute-start(bf16[64,2048]{1,0:T(8,128)(2,1)} %bitcast.12.refs_0_), channel_id=1, source_target_pairs={{0,4},{2,6},{4,0},{6,2},{1,5},{3,7},{5,1},{7,3},{8,12},{10,14},{12... | collective-permute-start | bytes 786440 | tf_op jit(solution)/shard_map/ppermute | solution.py:31
  45.8 14.5 %collective-permute-start.7 = (bf16[64,2048]{1,0:T(8,128)(2,1)}, bf16[64,2048]{1,0:T(8,128)(2,1)S(1)}, u32[]{:S(2)}, u32[]{:S(2)}) collective-permute-start(bf16[64,2048]{1,0:T(8,128)(2,1)} %bitcast.12.refs_0_), channel_id=1, source_target_pairs={{0,1},{1,0},{2,3},{3,2},{4,5},{5,4},{6,7},{7,6},{8,9},{9,8},{10,11... | collective-permute-start | bytes 786440 | tf_op jit(solution)/shard_map/ppermute | solution.py:31
  55.1 5.2 %collective-permute-start.10 = (bf16[64,2048]{1,0:T(8,128)(2,1)S(1)}, bf16[64,2048]{1,0:T(8,128)(2,1)S(1)}, u32[]{:S(2)}, u32[]{:S(2)}) collective-permute-start(bf16[64,2048]{1,0:T(8,128)(2,1)S(1)} %collective-permute-done.6.refs_3_), channel_id=1, source_target_pairs={{0,1},{1,0},{2,3},{3,2},{4,5},{5,4},{6,7},{7,6},{8,9},{9,8},{10,11... | collective-permute-start | bytes 786440 | tf_op jit(solution)/shard_map/ppermute | solution.py:31
  56.6 4.5 %collective-permute-start.8 = (bf16[64,2048]{1,0:T(8,128)(2,1)S(1)}, bf16[64,2048]{1,0:T(8,128)(2,1)S(1)}, u32[]{:S(2)}, u32[]{:S(2)}) collective-permute-start(bf16[64,2048]{1,0:T(8,128)(2,1)S(1)} %collective-permute-done.4.refs_1_), channel_id=1, source_target_pairs={{0,1},{1,0},{2,3},{3,2},{4,5},{5,4},{6,7},{7,6},{8,9},{9,8},{10,11... | collective-permute-start | bytes 786440 | tf_op jit(solution)/shard_map/ppermute | solution.py:31
  59.9 1.5 collective-permute-start.9
  59.9 16.1 %collective-permute-start.15 = (bf16[528,1024]{1,0:T(8,128)(2,1)}, bf16[528,1024]{1,0:T(8,128)(2,1)S(1)}, u32[]{:S(2)}, u32[]{:S(2)}) collective-permute-start(bf16[528,1024]{1,0:T(8,128)(2,1)} %pack.5), channel_id=1, source_target_pairs={{0,4},{1,129},{2,6},{3,131},{4,0},{5,133},{6,2},{7,135},{8,12},{9,... | collective-permute-start | bytes 3244040 | tf_op jit(solution)/shard_map/ppermute | solution.py:39
  61.4 1.2 copy-start.3
  62.6 8.5 %copy-start.1 = (bf16[1,4,256,2048]{3,2,1,0:T(8,128)(2,1)S(1)}, bf16[1,4,256,2048]{3,2,1,0:T(8,128)(2,1)}, u32[]{:S(2)}) copy-start(bf16[1,4,256,2048]{3,2,1,0:T(8,128)(2,1)} %param.10) | copy-start | bytes 12582916
  65.3 6.7 %copy-start.4 = (bf16[512,256]{1,0:T(8,128)(2,1)}, bf16[512,256]{1,0:T(8,128)(2,1)S(1)}, u32[]{:S(2)}) copy-start(bf16[512,256]{1,0:T(8,128)(2,1)S(1)} %get-tuple-element.39) | copy-start | bytes 786436
  65.3 6.7 %copy-start.6 = (bf16[512,256]{1,0:T(8,128)(2,1)}, bf16[512,256]{1,0:T(8,128)(2,1)S(1)}, u32[]{:S(2)}) copy-start(bf16[512,256]{1,0:T(8,128)(2,1)S(1)} %get-tuple-element.40) | copy-start | bytes 786436
  65.3 1.6 collective-permute-start.11
  67.0 20.3 %copy-start.10 = (f32[1,2048]{1,0:T(1,128)S(1)}, f32[1,2048]{1,0:T(1,128)}, u32[]{:S(2)}) copy-start(f32[1,2048]{1,0:T(1,128)} %bias.1) | copy-start | bytes 24580
  67.0 14.6 %collective-permute-start.12 = (bf16[2,512,256]{2,1,0:T(8,128)(2,1)S(1)}, bf16[2,512,256]{2,1,0:T(8,128)(2,1)S(1)}, u32[]{:S(2)}, u32[]{:S(2)}) collective-permute-start(bf16[2,512,256]{2,1,0:T(8,128)(2,1)S(1)} %pad_maximum_fusion.a0), channel_id=1, source_target_pairs={{0,2},{1,65},{2,4},{3,67},{4,6},{5,69},{6,0},{7,71},{8,10},{9,73},... | collective-permute-start | bytes 1572872 | tf_op jit(solution)/shard_map/ppermute | solution.py:39
  67.1 20.2 %collective-permute-start.13 = (bf16[2,512,256]{2,1,0:T(8,128)(2,1)S(1)}, bf16[2,512,256]{2,1,0:T(8,128)(2,1)S(1)}, u32[]{:S(2)}, u32[]{:S(2)}) collective-permute-start(bf16[2,512,256]{2,1,0:T(8,128)(2,1)S(1)} %pad_maximum_fusion.a0), channel_id=1, source_target_pairs={{0,4},{1,129},{2,6},{3,131},{4,0},{5,133},{6,2},{7,135},{8,12},{9,... | collective-permute-start | bytes 1572872 | tf_op jit(solution)/shard_map/ppermute | solution.py:39
  69.3 18.0 %collective-permute-start.14 = (bf16[2,512,256]{2,1,0:T(8,128)(2,1)S(1)}, bf16[2,512,256]{2,1,0:T(8,128)(2,1)S(1)}, u32[]{:S(2)}, u32[]{:S(2)}) collective-permute-start(bf16[2,512,256]{2,1,0:T(8,128)(2,1)S(1)} %pad_maximum_fusion.a0), channel_id=1, source_target_pairs={{0,6},{1,193},{2,0},{3,195},{4,2},{5,197},{6,4},{7,199},{8,14},{9,... | collective-permute-start | bytes 1572872 | tf_op jit(solution)/shard_map/ppermute | solution.py:39
  76.0 17.3 %copy-start.9 = (bf16[528,1024]{1,0:T(8,128)(2,1)}, bf16[528,1024]{1,0:T(8,128)(2,1)S(1)}, u32[]{:S(2)}) copy-start(bf16[528,1024]{1,0:T(8,128)(2,1)S(1)} %collective-permute-done.15.w2) | copy-start | bytes 3244036
  76.0 20.0 %copy-start.5 = (bf16[512,256]{1,0:T(8,128)(2,1)S(1)}, bf16[512,256]{1,0:T(8,128)(2,1)}, u32[]{:S(2)}) copy-start(bf16[512,256]{1,0:T(8,128)(2,1)} %copy-done.4) | copy-start | bytes 786436
  76.0 20.2 %copy-start.7 = (bf16[512,256]{1,0:T(8,128)(2,1)S(1)}, bf16[512,256]{1,0:T(8,128)(2,1)}, u32[]{:S(2)}) copy-start(bf16[512,256]{1,0:T(8,128)(2,1)} %copy-done.6) | copy-start | bytes 786436
  93.3 24.1 %slice-start = ((bf16[528,1024]{1,0:T(8,128)(2,1)}), bf16[4,1024]{1,0:T(4,128)(2,1)S(1)}, s32[]{:S(2)}) async-start(bf16[528,1024]{1,0:T(8,128)(2,1)} %copy-done.9), calls=%async_computation.4 | async-start | bytes 16384 | tf_op jit(solution)/shard_map/slice | solution.py:267
  93.3 9.8 %collective-permute-start.16 = (bf16[8,16,1024]{2,1,0:T(8,128)(2,1)}, bf16[8,16,1024]{2,1,0:T(8,128)(2,1)S(1)}, u32[]{:S(2)}, u32[]{:S(2)}) collective-permute-start(bf16[8,16,1024]{2,1,0:T(8,128)(2,1)} %get-tuple-element.45), channel_id=1, source_target_pairs={{0,64},{1,3},{2,66},{3,5},{4,68},{5,7},{6,70},{7,1},{8,72},{9,11},... | collective-permute-start | bytes 786440 | tf_op jit(solution)/shard_map/ppermute | solution.py:47
  93.4 9.7 %collective-permute-start.17 = (bf16[8,16,1024]{2,1,0:T(8,128)(2,1)}, bf16[8,16,1024]{2,1,0:T(8,128)(2,1)S(1)}, u32[]{:S(2)}, u32[]{:S(2)}) collective-permute-start(bf16[8,16,1024]{2,1,0:T(8,128)(2,1)} %get-tuple-element.46), channel_id=1, source_target_pairs={{0,128},{1,5},{2,130},{3,7},{4,132},{5,1},{6,134},{7,3},{8,136},{9... | collective-permute-start | bytes 786440 | tf_op jit(solution)/shard_map/ppermute | solution.py:47
  94.7 9.1 %collective-permute-start.18 = (bf16[8,16,1024]{2,1,0:T(8,128)(2,1)}, bf16[8,16,1024]{2,1,0:T(8,128)(2,1)S(1)}, u32[]{:S(2)}, u32[]{:S(2)}) collective-permute-start(bf16[8,16,1024]{2,1,0:T(8,128)(2,1)} %get-tuple-element.47), channel_id=1, source_target_pairs={{0,192},{1,7},{2,194},{3,1},{4,196},{5,3},{6,198},{7,5},{8,200},{9... | collective-permute-start | bytes 786440 | tf_op jit(solution)/shard_map/ppermute | solution.py:47
  104.6 12.8 %all-to-all-start.2 = ((bf16[8,16,1024]{2,1,0:T(8,128)(2,1)}), bf16[8,16,1024]{2,1,0:T(8,128)(2,1)S(1)}, u32[]{:S(2)}, u32[]{:S(2)}) async-start(bf16[8,16,1024]{2,1,0:T(8,128)(2,1)} %add_convert_fusion), calls=%async_computation.2 | async-start | bytes 524288 | tf_op jit(solution)/shard_map/all_to_all | solution.py:277
  129.5 8.8 %collective-permute-start.19 = (bf16[8,16,1024]{2,1,0:T(8,128)(2,1)S(1)}, bf16[8,16,1024]{2,1,0:T(8,128)(2,1)S(1)}, u32[]{:S(2)}, u32[]{:S(2)}) collective-permute-start(bf16[8,16,1024]{2,1,0:T(8,128)(2,1)S(1)} %all_to_all.21.refs_0_), channel_id=1, source_target_pairs={{0,64},{1,3},{2,66},{3,5},{4,68},{5,7},{6,70},{7,1},{8,72},{9,11},... | collective-permute-start | bytes 786440 | tf_op jit(solution)/shard_map/ppermute | solution.py:47
  134.9 7.0 %collective-permute-start.20 = (bf16[8,16,1024]{2,1,0:T(8,128)(2,1)S(1)}, bf16[8,16,1024]{2,1,0:T(8,128)(2,1)S(1)}, u32[]{:S(2)}, u32[]{:S(2)}) collective-permute-start(bf16[8,16,1024]{2,1,0:T(8,128)(2,1)S(1)} %all_to_all.21.refs_0_), channel_id=1, source_target_pairs={{0,128},{1,5},{2,130},{3,7},{4,132},{5,1},{6,134},{7,3},{8,136},{9... | collective-permute-start | bytes 786440 | tf_op jit(solution)/shard_map/ppermute | solution.py:47
  134.9 7.0 %collective-permute-start.21 = (bf16[8,16,1024]{2,1,0:T(8,128)(2,1)S(1)}, bf16[8,16,1024]{2,1,0:T(8,128)(2,1)S(1)}, u32[]{:S(2)}, u32[]{:S(2)}) collective-permute-start(bf16[8,16,1024]{2,1,0:T(8,128)(2,1)S(1)} %all_to_all.21.refs_0_), channel_id=1, source_target_pairs={{0,192},{1,7},{2,194},{3,1},{4,196},{5,3},{6,198},{7,5},{8,200},{9... | collective-permute-start | bytes 786440 | tf_op jit(solution)/shard_map/ppermute | solution.py:47
  142.8 15.2 %collective-permute-start.24 = (bf16[32,16,1024]{2,1,0:T(8,128)(2,1)S(1)}, bf16[32,16,1024]{2,1,0:T(8,128)(2,1)S(1)}, u32[]{:S(2)}, u32[]{:S(2)}) collective-permute-start(bf16[32,16,1024]{2,1,0:T(8,128)(2,1)S(1)} %collect.1.refs_0_), channel_id=1, source_target_pairs={{0,2},{1,65},{2,4},{3,67},{4,6},{5,69},{6,0},{7,71},{8,10},{9,73},... | collective-permute-start | bytes 3145736 | tf_op jit(solution)/shard_map/ppermute | solution.py:39
  142.9 20.6 %collective-permute-start.22 = (bf16[32,16,1024]{2,1,0:T(8,128)(2,1)S(1)}, bf16[32,16,1024]{2,1,0:T(8,128)(2,1)S(1)}, u32[]{:S(2)}, u32[]{:S(2)}) collective-permute-start(bf16[32,16,1024]{2,1,0:T(8,128)(2,1)S(1)} %collect.1.refs_0_), channel_id=1, source_target_pairs={{0,6},{1,193},{2,0},{3,195},{4,2},{5,197},{6,4},{7,199},{8,14},{9,... | collective-permute-start | bytes 3145736 | tf_op jit(solution)/shard_map/ppermute | solution.py:39
  145.6 20.3 %collective-permute-start.28 = (bf16[32,16,1024]{2,1,0:T(8,128)(2,1)S(1)}, bf16[32,16,1024]{2,1,0:T(8,128)(2,1)S(1)}, u32[]{:S(2)}, u32[]{:S(2)}) collective-permute-start(bf16[32,16,1024]{2,1,0:T(8,128)(2,1)S(1)} %collect.1.refs_0_), channel_id=1, source_target_pairs={{0,1},{1,0},{2,3},{3,2},{4,5},{5,4},{6,7},{7,6},{8,9},{9,8},{10,11... | collective-permute-start | bytes 3145736 | tf_op jit(solution)/shard_map/ppermute | solution.py:31
  158.1 10.2 %collective-permute-start.27 = (bf16[32,16,1024]{2,1,0:T(8,128)(2,1)S(1)}, bf16[32,16,1024]{2,1,0:T(8,128)(2,1)S(1)}, u32[]{:S(2)}, u32[]{:S(2)}) collective-permute-start(bf16[32,16,1024]{2,1,0:T(8,128)(2,1)S(1)} %collective-permute-done.24.refs_0_), channel_id=1, source_target_pairs={{0,1},{1,0},{2,3},{3,2},{4,5},{5,4},{6,7},{7,6},{8,9},{9,8},{10,11... | collective-permute-start | bytes 3145736 | tf_op jit(solution)/shard_map/ppermute | solution.py:31
  163.5 7.1 %collective-permute-start.26 = (bf16[32,16,1024]{2,1,0:T(8,128)(2,1)S(1)}, bf16[32,16,1024]{2,1,0:T(8,128)(2,1)S(1)}, u32[]{:S(2)}, u32[]{:S(2)}) collective-permute-start(bf16[32,16,1024]{2,1,0:T(8,128)(2,1)S(1)} %collective-permute-done.22.refs_0_), channel_id=1, source_target_pairs={{0,1},{1,0},{2,3},{3,2},{4,5},{5,4},{6,7},{7,6},{8,9},{9,8},{10,11... | collective-permute-start | bytes 3145736 | tf_op jit(solution)/shard_map/ppermute | solution.py:31
  163.6 9.4 %collective-permute-start.23 = (bf16[16,16,1024]{2,1,0:T(8,128)(2,1)S(1)}, bf16[16,16,1024]{2,1,0:T(8,128)(2,1)S(1)}, u32[]{:S(2)}, u32[]{:S(2)}) collective-permute-start(bf16[16,16,1024]{2,1,0:T(8,128)(2,1)S(1)} %slice.46), channel_id=1, source_target_pairs={{0,6},{1,193},{2,0},{3,195},{4,2},{5,197},{6,4},{7,199},{8,14},{9,... | collective-permute-start | bytes 1572872 | tf_op jit(solution)/shard_map/ppermute | solution.py:39
  165.2 9.8 %collective-permute-start.25 = (bf16[16,16,1024]{2,1,0:T(8,128)(2,1)S(1)}, bf16[16,16,1024]{2,1,0:T(8,128)(2,1)S(1)}, u32[]{:S(2)}, u32[]{:S(2)}) collective-permute-start(bf16[16,16,1024]{2,1,0:T(8,128)(2,1)S(1)} %slice.47), channel_id=1, source_target_pairs={{0,2},{1,65},{2,4},{3,67},{4,6},{5,69},{6,0},{7,71},{8,10},{9,73},... | collective-permute-start | bytes 1572872 | tf_op jit(solution)/shard_map/ppermute | solution.py:39
  175.0 4.1 %collective-permute-start.29 = (bf16[16,16,1024]{2,1,0:T(8,128)(2,1)S(1)}, bf16[16,16,1024]{2,1,0:T(8,128)(2,1)S(1)}, u32[]{:S(2)}, u32[]{:S(2)}) collective-permute-start(bf16[16,16,1024]{2,1,0:T(8,128)(2,1)S(1)} %collective-permute-done.23.refs_0_), channel_id=1, source_target_pairs={{0,1},{1,0},{2,3},{3,2},{4,5},{5,4},{6,7},{7,6},{8,9},{9,8},{10,11... | collective-permute-start | bytes 1572872 | tf_op jit(solution)/shard_map/ppermute | solution.py:31
  177.6 2.3 %collective-permute-start.30 = (bf16[16,16,1024]{2,1,0:T(8,128)(2,1)S(1)}, bf16[16,16,1024]{2,1,0:T(8,128)(2,1)S(1)}, u32[]{:S(2)}, u32[]{:S(2)}) collective-permute-start(bf16[16,16,1024]{2,1,0:T(8,128)(2,1)S(1)} %collective-permute-done.25.refs_1_), channel_id=1, source_target_pairs={{0,1},{1,0},{2,3},{3,2},{4,5},{5,4},{6,7},{7,6},{8,9},{9,8},{10,11... | collective-permute-start | bytes 1572872 | tf_op jit(solution)/shard_map/ppermute | solution.py:31

commit v4 on v3

--- a/solution.py
+++ b/solution.py
@@ -71,16 +71,30 @@
     )(*pieces, weight, bias, place)
 
 
-def decoder_kernel(where, a0, a1, a2, a3, w0, w1, w2, w3, bias, *refs):
-    outs, total = refs[:-1], refs[-1]
-    feats = a0.shape[2]
+def products(where, steps, acts, weights):
+    x, core = where[0], where[3]
+    value = 0.0
+    for step, a, w in zip(steps, acts, weights):
+        feats = a.shape[2]
+        term = jnp.dot(a[0], w[:feats, :], preferred_element_type=F32)
+        term += jnp.dot(a[1], w[feats:2 * feats, :], preferred_element_type=F32)
+        value += term if step == 0 else jnp.where((core == 0) | (x >= step), term, 0.0)
+    return value
+
+
+def early_kernel(steps, where, *refs):
+    count = len(steps)
+    acts, weights, (bias, out) = refs[:count], refs[count:2 * count], refs[2 * count:]
     x, z, y, core = (where[i] for i in range(4))
     adds_bias = (z == 0) & (((core == 0) & (x == y)) | ((core == 1) & (y == 0)))
-    value = jnp.where(adds_bias, bias[...], 0.0)
-    for i, (a, w) in enumerate(((a0, w0), (a1, w1), (a2, w2), (a3, w3))):
-        term = jnp.dot(a[0], w[:feats, :], preferred_element_type=F32)
-        term += jnp.dot(a[1], w[feats:2 * feats, :], preferred_element_type=F32)
-        value += term if i == 0 else jnp.where((core == 0) | (x >= i), term, 0.0)
+    out[...] = jnp.where(adds_bias, bias[...], 0.0) + products(where, steps, acts, weights)
+
+
+def late_kernel(steps, where, *refs):
+    count = len(steps)
+    acts, weights, early, outs, total = refs[:count], refs[count:2 * count], refs[2 * count], refs[2 * count + 1:-1], refs[-1]
+    x, y, core = where[0], where[2], where[3]
+    value = early[...] + products(where, steps, acts, weights)
     total[...] = jnp.where((core == 1) | (y >= x), value, 0.0)
     first = jnp.where(core == 0, x, y)
     for step, out in enumerate(outs):
@@ -89,27 +103,38 @@
         out[...] = total[pl.ds(start, span), :].astype(BF).reshape(out.shape)
 
 
-def decode(where, acts, weights, bias):
+def decode(steps, where, acts, weights, bias=None, early=None):
+    acts, weights = [acts[step] for step in steps], [weights[step] for step in steps]
     cores, tokens, feats = acts[0].shape
     rows, width = weights[0].shape
     part, cols = tokens // XZ, 256
     blocks = width // cols
-    return pl.pallas_call(
-        decoder_kernel,
+    if early is None:
+        kernel, last = early_kernel, bias
+        last_spec = pl.BlockSpec((1, cols), lambda n, where: (0, where[3] * blocks + n))
+        out_specs = pl.BlockSpec((tokens, cols), lambda n, _: (0, n))
+        out_shape, scratch = jax.ShapeDtypeStruct((tokens, width), F32), []
+    else:
+        kernel, last = late_kernel, early
+        last_spec = pl.BlockSpec((tokens, cols), lambda n, _: (0, n))
+        out_specs = [pl.BlockSpec((NZ, part, cols), lambda n, _: (0, 0, n))] * NX
+        out_shape, scratch = [jax.ShapeDtypeStruct((NZ, part, width), BF)] * NX, [pltpu.VMEM((tokens, cols), F32)]
+    return pl.pallas_call(
+        functools.partial(kernel, steps),
         grid_spec=pltpu.PrefetchScalarGridSpec(
             num_scalar_prefetch=1,
             grid=(blocks,),
-            in_specs=[pl.BlockSpec((cores, tokens, feats), lambda n, _: (0, 0, 0))] * NY
-            + [pl.BlockSpec((rows, cols), lambda n, _: (0, n))] * NY
-            + [pl.BlockSpec((1, cols), lambda n, where: (0, where[3] * blocks + n))],
-            out_specs=[pl.BlockSpec((NZ, part, cols), lambda n, _: (0, 0, n))] * NX,
-            scratch_shapes=[pltpu.VMEM((tokens, cols), F32)],
-        ),
-        out_shape=[jax.ShapeDtypeStruct((NZ, part, width), BF)] * NX,
-        compiler_params=pltpu.CompilerParams(vmem_limit_bytes=VMEM_LIMIT),
-        cost_estimate=pl.CostEstimate(flops=22 * 10**8, bytes_accessed=8 * 10**6, transcendentals=0),
+            in_specs=[pl.BlockSpec((cores, tokens, feats), lambda n, _: (0, 0, 0))] * len(steps)
+            + [pl.BlockSpec((rows, cols), lambda n, _: (0, n))] * len(steps)
+            + [last_spec],
+            out_specs=out_specs,
+            scratch_shapes=scratch,
+        ),
+        out_shape=out_shape,
+        compiler_params=pltpu.CompilerParams(vmem_limit_bytes=VMEM_LIMIT),
+        cost_estimate=pl.CostEstimate(flops=55 * 10**7 * len(steps), bytes_accessed=4 * 10**6, transcendentals=0),
         name="decode",
-    )(where, *acts, *weights, bias)
+    )(where, *acts, *weights, last)
 
 
 def sinks_at(where, step):
@@ -118,11 +143,12 @@
     return lax.rem(first + NY - step, NY), lax.rem(second + NY - step, NY)
 
 
-def gradient_kernel(step, count, where, *refs):
-    own, other, (mine, give), out = refs[:count], refs[count:2 * count], refs[2 * count:2 * count + 2], refs[-1]
-    half = pl.program_id(0)
+def gradient_kernel(step, halves, count, where, *refs):
+    (mine, give), out = refs[count * len(halves):count * len(halves) + 2], refs[-1]
+    half = pl.program_id(0) + halves[0]
     sinks = sinks_at(where, step)
-    for i, (blocks, activity) in enumerate(((own, mine), (other, give))):
+    for k, i in enumerate(halves):
+        blocks, activity = refs[k * count:(k + 1) * count], (mine, give)[i]
 
         @pl.when((half == i) & (sinks[i] >= where[0]))
         def _():
@@ -138,31 +164,35 @@
             out[...] = jnp.zeros(out.shape, BF)
 
 
-def gradient(step, where, layers, own, other, mine, give, before):
-    _, part, cols = own[0].shape
+def gradient(step, where, layers, given, mine, give, before):
+    halves = tuple(sorted(given))
+    pieces = [piece for i in halves for piece in given[i]]
+    count = len(pieces) // len(halves)
+    _, part, cols = pieces[0].shape
     feats, tokens = mine.shape
     more = [] if before is None else [before]
 
     def place(half, where):
+        half = half + halves[0]
         first, second = sinks_at(where, step)
         return jnp.where(half == 0, first, second), 0, jnp.where(half == 0, where[3], 1 - where[3])
 
     return pl.pallas_call(
-        functools.partial(gradient_kernel, step, len(own)),
+        functools.partial(gradient_kernel, step, halves, count),
         grid_spec=pltpu.PrefetchScalarGridSpec(
             num_scalar_prefetch=1,
-            grid=(NC,),
-            in_specs=[pl.BlockSpec((piece.shape[0], part, cols), lambda h, _: (0, 0, 0)) for piece in own] * 2
+            grid=(len(halves),),
+            in_specs=[pl.BlockSpec((piece.shape[0], part, cols), lambda h, _: (0, 0, 0)) for piece in pieces]
             + [pl.BlockSpec((feats, tokens), lambda h, _: (0, 0))] * 2
             + [pl.BlockSpec(memory_space=pl.ANY)] * len(more),
             out_specs=pl.BlockSpec((1, feats, cols), place),
         ),
         out_shape=jax.ShapeDtypeStruct((layers, feats, NC * cols), BF),
-        input_output_aliases={2 * len(own) + 3: 0} if more else {},
+        input_output_aliases={len(pieces) + 3: 0} if more else {},
         compiler_params=pltpu.CompilerParams(vmem_limit_bytes=VMEM_LIMIT),
         cost_estimate=pl.CostEstimate(flops=55 * 10**7, bytes_accessed=4 * 10**6, transcendentals=0),
         name="gradient",
-    )(where, *own, *other, mine, give, *more)
+    )(where, *pieces, mine, give, *more)
 
 
 def collect_kernel(where, *refs):
@@ -262,7 +292,9 @@
 
     act = jnp.stack([own, shift(away, "c", 1)])
     acts = [act] + [ring(act, step) for step in range(1, NY)]
-    parts = decode(where, acts, weights, dec_bias)
+    early = decode((0, 1, 3), where, acts, weights, bias=dec_bias)
+    acts[2], early = lax.optimization_barrier((acts[2], early))
+    parts = decode((2,), where, acts, weights, early=early)
 
     wanted = jnp.concatenate([w[2 * feats:2 * feats + 2 * mine] for w in weights])
     q = jnp.arange(NY * NC * mine)
@@ -284,11 +316,13 @@
     middle = XZ // 2
     far = [ring(after[:middle], 3), ring(before[middle:], 1)]
     grads = None
-    for step, pieces in ((0, [block]), (1, [before]), (3, [after]), (2, far)):
-        if step == 2:
-            *pieces, grads = lax.optimization_barrier((*pieces, grads))
-        others = [shift(piece, "c", 1) for piece in pieces]
-        grads = gradient(step, where, layers, pieces, others, own, away, grads)
+    for step, pieces in ((0, [block]), (1, [before]), (3, [after])):
+        given = {0: pieces, 1: [shift(piece, "c", 1) for piece in pieces]}
+        grads = gradient(step, where, layers, given, own, away, grads)
+    *far, grads = lax.optimization_barrier((*far, grads))
+    others = [shift(piece, "c", 1) for piece in far]
+    grads = gradient(2, where, layers, {0: far}, own, away, grads)
+    grads = gradient(2, where, layers, {1: others}, own, away, grads)
     return grads[None]
 
 

time: 183 us -> 181 us (0.989)
  starting transfers between devices: 59.4 us -> 53.4 us
    ppermute x15, starting transfers between devices: 30.3 us -> 23.2 us  [shift(): lax.ppermute(value, axis, [(i, (i + step) % size) for i in range(size)])]
    pallas_call x5 -> x7, Pallas kernels: 15.5 us -> 17.8 us  [the longest x5 10.7 us: gradient(): pl.pallas_call(functools.partial(gradient_kernel, step, halves, count), g...]
    unnamed x23 -> x31, local copies, waits for them, and re-layouts: 5.81 us -> 7.8 us
  transfers between devices with their start and end apart: 33 -> 33, of which waited for: 18 -> 16; matrix products, arithmetic and copies ran while one was open for 1% -> 1% of each run, Pallas kernels for 8% -> 11%
where the time goes in v4:
time: 181 us
  waiting for transfers between devices  57.4 us (32%)
  starting transfers between devices  53.4 us (30%)
  blocking collectives  28.4 us (16%)
  Pallas kernels  25.2 us (14%)
  local copies, waits for them, and re-layouts  13 us (7%)
  other arithmetic  2.64 us (1%)
    ppermute x10, waiting for transfers between devices, ring(): return lax.ppermute(value, ALL, pairs)  24.3 us
    ppermute x15, starting transfers between devices, shift(): lax.ppermute(value, axis, [(i, (i + step) % size) for i in range(size)])  23.2 us
    all_to_all x1, blocking collectives, body(): rows = lax.all_to_all(rows, 'z', 0, 0, tiled=True).reshape(XZ * mine, width)  16.5 us
    ppermute x6, waiting for transfers between devices, cross(): return lax.ppermute(value, ALL, pairs)  13.3 us
    ppermute x6, starting transfers between devices, cross(): return lax.ppermute(value, ALL, pairs)  12.2 us
    all_to_all x1, blocking collectives, body(): lax.all_to_all(jnp.broadcast_to(cotangent[None], (NZ,) + cotangent.shape)...  11.9 us
    ppermute x10, starting transfers between devices, ring(): return lax.ppermute(value, ALL, pairs)  11.4 us
    ppermute x15, waiting for transfers between devices, shift(): lax.ppermute(value, axis, [(i, (i + step) % size) for i in range(size)])  11.3 us
  transfers between devices with their start and end apart: 33, of which 16 were waited for; matrix products, arithmetic and copies ran while one was open for 1% of the time, Pallas kernels for 11%

profile of v4, /device:TPU:1, one launch (start us, length us, event | category | flops | bytes accessed | tf_op | source)
XLA Modules:
  0.0 180.7 jit_solution(1427485111977637285)
XLA Ops:
  0.0 0.8 reshape.384
  0.8 1.4 copy.33
  2.2 3.1 %dynamic-slice_bitcast_fusion = bf16[4,256,1024]{2,1,0:T(8,128)(2,1)} fusion(bf16[1,4,256,2048]{3,2,1,0:T(8,128)(2,1)} %param.10, s32[]{:T(128)S(6)} %select_n.251), kind=kLoop, calls=%fused_computation.1 | loop fusion | bytes 4194308 | tf_op jit(solution)/shard_map/dynamic_slice | solution.py:267
  5.5 3.3 %collective-permute-start = (bf16[4,256,1024]{2,1,0:T(8,128)(2,1)}, bf16[4,256,1024]{2,1,0:T(8,128)(2,1)S(1)}, u32[]{:S(2)}, u32[]{:S(2)}) collective-permute-start(bf16[4,256,1024]{2,1,0:T(8,128)(2,1)} %dynamic-slice_bitcast_fusion), channel_id=1, source_target_pairs={{0,1},{1,0},{2,3},{3,2},{4,5},{5,4},{6,7},{7,6},{8,9},{9,8},{10,11... | collective-permute-start | bytes 6291464 | tf_op jit(solution)/shard_map/ppermute | solution.py:31
  8.9 3.3 %all-to-all-start = ((bf16[4,2,2048]{2,1,0:T(2,128)(2,1)}), bf16[4,2,2048]{2,1,0:T(2,128)(2,1)S(1)}, u32[]{:S(2)}, u32[]{:S(2)}) async-start(bf16[4,2,2048]{2,1,0:T(2,128)(2,1)} %bitcast.27), calls=%async_computation | async-start | bytes 65536 | tf_op jit(solution)/shard_map/all_to_all | solution.py:275
  12.6 0.3 collective-permute-done.other
  12.8 2.2 %copy-done = bf16[1,4,256,2048]{3,2,1,0:T(8,128)(2,1)S(1)} copy-done((bf16[1,4,256,2048]{3,2,1,0:T(8,128)(2,1)S(1)}, bf16[1,4,256,2048]{3,2,1,0:T(8,128)(2,1)}, u32[]{:S(2)}) %copy-start) | copy-done | bytes 4194328
  15.0 0.9 pack.6
  15.9 1.0 copy-done.6
  16.9 0.9 pack.5
  17.8 1.0 copy-done.5
  18.8 0.9 pack.4
  19.8 1.0 copy-done.7
  20.8 1.0 collective-permute-start.2
  21.8 1.7 collective-permute-start.3
  23.5 16.5 %all_to_all.20 = bf16[8,8,2048]{2,1,0:T(8,128)(2,1)} all-to-all(bf16[8,8,2048]{2,1,0:T(8,128)(2,1)S(1)} %broadcast_in_dim.41), channel_id=1, replica_groups=mesh['x'=4,'z'=8,'y'=4,'c'=2] {'z'}, dimensions={0} | all-to-all | bytes 524288 | tf_op jit(solution)/shard_map/all_to_all | solution.py:279
  40.0 5.4 %collective-permute-start.6 = (bf16[64,2048]{1,0:T(8,128)(2,1)}, bf16[64,2048]{1,0:T(8,128)(2,1)}, u32[]{:S(2)}, u32[]{:S(2)}) collective-permute-start(bf16[64,2048]{1,0:T(8,128)(2,1)} %bitcast.12.refs_0_), channel_id=1, source_target_pairs={{0,6},{2,0},{4,2},{6,4},{1,7},{3,1},{5,3},{7,5},{8,14},{10,8},{12,... | collective-permute-start | bytes 786440 | tf_op jit(solution)/shard_map/ppermute | solution.py:31
  45.4 1.6 collective-permute-start.5
  47.1 1.4 collective-permute-start.7
  48.5 7.9 %collective-permute-done.6.refs_3_ = bf16[64,2048]{1,0:T(8,128)(2,1)} collective-permute-done((bf16[64,2048]{1,0:T(8,128)(2,1)}, bf16[64,2048]{1,0:T(8,128)(2,1)}, u32[]{:S(2)}, u32[]{:S(2)}) %collective-permute-start.6) | collective-permute-done | bytes 262176 | tf_op jit(solution)/shard_map/ppermute | solution.py:31
  56.4 1.5 collective-permute-start.10
  57.8 3.4 %collective-permute-start.8 = (bf16[64,2048]{1,0:T(8,128)(2,1)}, bf16[64,2048]{1,0:T(8,128)(2,1)S(1)}, u32[]{:S(2)}, u32[]{:S(2)}) collective-permute-start(bf16[64,2048]{1,0:T(8,128)(2,1)} %collective-permute-done.4.refs_1_), channel_id=1, source_target_pairs={{0,1},{1,0},{2,3},{3,2},{4,5},{5,4},{6,7},{7,6},{8,9},{9,8},{10,11... | collective-permute-start | bytes 786440 | tf_op jit(solution)/shard_map/ppermute | solution.py:31
  61.3 0.3 fusion.refs_10_
  61.7 0.9 collective-permute-done.8.refs_5_
  62.6 0.4 collective-permute-done.9.refs_6_
  63.0 1.2 copy-done.8
  64.2 2.9 %encode.1 = (bf16[512,256]{1,0:T(8,128)(2,1)S(1)}, bf16[512,256]{1,0:T(8,128)(2,1)S(1)}) custom-call(bf16[64,2048]{1,0:T(8,128)(2,1)} %bitcast.12.refs_0_, bf16[64,2048]{1,0:T(8,128)(2,1)} %collective-permute-done.4.refs_1_, bf16[64,2048]{1,0:T(8,128)(2,1)} %collective-permute-done.5.refs_2_, bf16[64,2048]{1,0:T(8,128)(2,1)} %collective-permute-done.6.refs_3_, ...), custom_call_target="tpu_custom_call" | custom-call | flops 800000000 | bytes 4000000 | tf_op jit(solution)/shard_map/encode/pallas_call | solution.py:64
  67.1 0.5 collective-permute-start.11
  67.6 1.2 collective-permute-done.11
  68.9 2.7 %collective-permute-start.14 = (bf16[2,512,256]{2,1,0:T(8,128)(2,1)S(1)}, bf16[2,512,256]{2,1,0:T(8,128)(2,1)S(1)}, u32[]{:S(2)}, u32[]{:S(2)}) collective-permute-start(bf16[2,512,256]{2,1,0:T(8,128)(2,1)S(1)} %pad_maximum_fusion.refs_0_), channel_id=1, source_target_pairs={{0,6},{1,193},{2,0},{3,195},{4,2},{5,197},{6,4},{7,199},{8,14},{9,... | collective-permute-start | bytes 1572872 | tf_op jit(solution)/shard_map/ppermute | solution.py:39
  71.6 0.5 collective-permute-start.12
  72.1 0.9 pack.7.refs_3_
  73.0 10.3 %collective-permute-done.13.refs_1_ = bf16[2,512,256]{2,1,0:T(8,128)(2,1)S(1)} collective-permute-done((bf16[2,512,256]{2,1,0:T(8,128)(2,1)S(1)}, bf16[2,512,256]{2,1,0:T(8,128)(2,1)S(1)}, u32[]{:S(2)}, u32[]{:S(2)}) %collective-permute-start.13) | collective-permute-done | bytes 524320 | tf_op jit(solution)/shard_map/ppermute | solution.py:39
  83.3 4.6 %decode.2.refs_2_ = f32[512,1024]{1,0:T(8,128)S(1)} custom-call(s32[4]{0:T(128)S(1)} %pad_add_fusion.1.where, bf16[2,512,256]{2,1,0:T(8,128)(2,1)S(1)} %pad_maximum_fusion.refs_0_, bf16[2,512,256]{2,1,0:T(8,128)(2,1)S(1)} %collective-permute-done.13.refs_1_, bf16[2,512,256]{2,1,0:T(8,128)(2,1)S(1)} %collective-permute-done.14.refs_2_, ...), custom_call_target="tpu_custom_call" | custom-call | flops 1650000000 | bytes 4000000 | tf_op jit(solution)/shard_map/decode/pallas_call | solution.py:122
  87.9 1.1 collective-permute-done.12.refs_0_
  89.0 2.5 %decode.3 = (bf16[8,16,1024]{2,1,0:T(8,128)(2,1)S(1)}, bf16[8,16,1024]{2,1,0:T(8,128)(2,1)S(1)}, bf16[8,16,1024]{2,1,0:T(8,128)(2,1)S(1)}, bf16[8,16,1024]{2,1,0:T(8,128)(2,1)S(1)}) custom-call(s32[4]{0:T(128)S(1)} %pad_add_fusion.1.where, bf16[2,512,256]{2,1,0:T(8,128)(2,1)S(1)} %collective-permute-done.12.refs_0_, ...), custom_call_target="tpu_custom_call" | custom-call | flops 550000000 | bytes 4000000 | tf_op jit(solution)/shard_map/decode/pallas_call | solution.py:122
  91.6 1.7 collective-permute-start.17
  93.3 1.5 collective-permute-start.18
  95.1 6.0 %collective-permute-done.16 = bf16[8,16,1024]{2,1,0:T(8,128)(2,1)S(1)} collective-permute-done((bf16[8,16,1024]{2,1,0:T(8,128)(2,1)S(1)}, bf16[8,16,1024]{2,1,0:T(8,128)(2,1)S(1)}, u32[]{:S(2)}, u32[]{:S(2)}) %collective-permute-start.16) | collective-permute-done | bytes 262176 | tf_op jit(solution)/shard_map/ppermute | solution.py:47
  101.1 0.7 collective-permute-done.18
  101.9 1.9 %add_convert_fusion = bf16[8,16,1024]{2,1,0:T(8,128)(2,1)} fusion(bf16[8,16,1024]{2,1,0:T(8,128)(2,1)} %collective-permute-done.18, bf16[8,16,1024]{2,1,0:T(8,128)(2,1)} %collective-permute-done.17, bf16[8,16,1024]{2,1,0:T(8,128)(2,1)S(1)} %collective-permute-done.16, bf16[8,16,1024]{2,1,0:T(8,128)(2,1)S(1)} %get-tuple-element.52), kind=kLoop, calls=%fused_computation.8 | loop fusion | flops 1048576 | bytes 1310720 | tf_op jit(solution)/shard_map/convert_element_type | solution.py:308
  103.8 3.4 %all-to-all-start.2 = ((bf16[8,16,1024]{2,1,0:T(8,128)(2,1)}), bf16[8,16,1024]{2,1,0:T(8,128)(2,1)S(1)}, u32[]{:S(2)}, u32[]{:S(2)}) async-start(bf16[8,16,1024]{2,1,0:T(8,128)(2,1)} %add_convert_fusion), calls=%async_computation.2 | async-start | bytes 524288 | tf_op jit(solution)/shard_map/all_to_all | solution.py:309
  107.2 0.7 slice.39
  108.0 8.6 %all-to-all-done.2 = bf16[8,16,1024]{2,1,0:T(8,128)(2,1)S(1)} async-done(((bf16[8,16,1024]{2,1,0:T(8,128)(2,1)}), bf16[8,16,1024]{2,1,0:T(8,128)(2,1)S(1)}, u32[]{:S(2)}, u32[]{:S(2)}) %all-to-all-start.2) | async-done | bytes 262176 | tf_op jit(solution)/shard_map/all_to_all | solution.py:309
  116.8 11.9 %all_to_all.21.refs_0_ = bf16[8,16,1024]{2,1,0:T(8,128)(2,1)S(1)} all-to-all(bf16[8,16,1024]{2,1,0:T(8,128)(2,1)S(1)} %broadcast_in_dim.46), channel_id=1, replica_groups=mesh['x'=4,'z'=8,'y'=4,'c'=2] {'z'}, dimensions={0} | all-to-all | bytes 524288 | tf_op jit(solution)/shard_map/all_to_all | solution.py:313
  128.7 5.8 %collective-permute-start.19 = (bf16[8,16,1024]{2,1,0:T(8,128)(2,1)S(1)}, bf16[8,16,1024]{2,1,0:T(8,128)(2,1)S(1)}, u32[]{:S(2)}, u32[]{:S(2)}) collective-permute-start(bf16[8,16,1024]{2,1,0:T(8,128)(2,1)S(1)} %all_to_all.21.refs_0_), channel_id=1, source_target_pairs={{0,64},{1,3},{2,66},{3,5},{4,68},{5,7},{6,70},{7,1},{8,72},{9,11},... | collective-permute-start | bytes 786440 | tf_op jit(solution)/shard_map/ppermute | solution.py:47
  134.6 3.1 %collective-permute-start.20 = (bf16[8,16,1024]{2,1,0:T(8,128)(2,1)S(1)}, bf16[8,16,1024]{2,1,0:T(8,128)(2,1)S(1)}, u32[]{:S(2)}, u32[]{:S(2)}) collective-permute-start(bf16[8,16,1024]{2,1,0:T(8,128)(2,1)S(1)} %all_to_all.21.refs_0_), channel_id=1, source_target_pairs={{0,128},{1,5},{2,130},{3,7},{4,132},{5,1},{6,134},{7,3},{8,136},{9... | collective-permute-start | bytes 786440 | tf_op jit(solution)/shard_map/ppermute | solution.py:47
  137.6 2.8 %collective-permute-done.19.refs_1_ = bf16[8,16,1024]{2,1,0:T(8,128)(2,1)S(1)} collective-permute-done((bf16[8,16,1024]{2,1,0:T(8,128)(2,1)S(1)}, bf16[8,16,1024]{2,1,0:T(8,128)(2,1)S(1)}, u32[]{:S(2)}, u32[]{:S(2)}) %collective-permute-start.19) | collective-permute-done | bytes 262176 | tf_op jit(solution)/shard_map/ppermute | solution.py:47
  140.4 3.8 %collective-permute-done.20.refs_2_ = bf16[8,16,1024]{2,1,0:T(8,128)(2,1)S(1)} collective-permute-done((bf16[8,16,1024]{2,1,0:T(8,128)(2,1)S(1)}, bf16[8,16,1024]{2,1,0:T(8,128)(2,1)S(1)}, u32[]{:S(2)}, u32[]{:S(2)}) %collective-permute-start.20) | collective-permute-done | bytes 262176 | tf_op jit(solution)/shard_map/ppermute | solution.py:47
  144.2 0.8 collect.1.refs_0_
  145.2 2.7 %collective-permute-start.22 = (bf16[32,16,1024]{2,1,0:T(8,128)(2,1)S(1)}, bf16[32,16,1024]{2,1,0:T(8,128)(2,1)S(1)}, u32[]{:S(2)}, u32[]{:S(2)}) collective-permute-start(bf16[32,16,1024]{2,1,0:T(8,128)(2,1)S(1)} %collect.1.refs_0_), channel_id=1, source_target_pairs={{0,6},{1,193},{2,0},{3,195},{4,2},{5,197},{6,4},{7,199},{8,14},{9,... | collective-permute-start | bytes 3145736 | tf_op jit(solution)/shard_map/ppermute | solution.py:39
  147.8 2.0 %collective-permute-start.28 = (bf16[32,16,1024]{2,1,0:T(8,128)(2,1)S(1)}, bf16[32,16,1024]{2,1,0:T(8,128)(2,1)S(1)}, u32[]{:S(2)}, u32[]{:S(2)}) collective-permute-start(bf16[32,16,1024]{2,1,0:T(8,128)(2,1)S(1)} %collect.1.refs_0_), channel_id=1, source_target_pairs={{0,1},{1,0},{2,3},{3,2},{4,5},{5,4},{6,7},{7,6},{8,9},{9,8},{10,11... | collective-permute-start | bytes 3145736 | tf_op jit(solution)/shard_map/ppermute | solution.py:31
  149.8 10.5 %collective-permute-done.24.refs_0_ = bf16[32,16,1024]{2,1,0:T(8,128)(2,1)S(1)} collective-permute-done((bf16[32,16,1024]{2,1,0:T(8,128)(2,1)S(1)}, bf16[32,16,1024]{2,1,0:T(8,128)(2,1)S(1)}, u32[]{:S(2)}, u32[]{:S(2)}) %collective-permute-start.24) | collective-permute-done | bytes 1048608 | tf_op jit(solution)/shard_map/ppermute | solution.py:39
  160.3 2.2 %collective-permute-start.27 = (bf16[32,16,1024]{2,1,0:T(8,128)(2,1)S(1)}, bf16[32,16,1024]{2,1,0:T(8,128)(2,1)S(1)}, u32[]{:S(2)}, u32[]{:S(2)}) collective-permute-start(bf16[32,16,1024]{2,1,0:T(8,128)(2,1)S(1)} %collective-permute-done.24.refs_0_), channel_id=1, source_target_pairs={{0,1},{1,0},{2,3},{3,2},{4,5},{5,4},{6,7},{7,6},{8,9},{9,8},{10,11... | collective-permute-start | bytes 3145736 | tf_op jit(solution)/shard_map/ppermute | solution.py:31
  162.5 2.4 %collective-permute-start.23 = (bf16[16,16,1024]{2,1,0:T(8,128)(2,1)S(1)}, bf16[16,16,1024]{2,1,0:T(8,128)(2,1)S(1)}, u32[]{:S(2)}, u32[]{:S(2)}) collective-permute-start(bf16[16,16,1024]{2,1,0:T(8,128)(2,1)S(1)} %slice.46), channel_id=1, source_target_pairs={{0,6},{1,193},{2,0},{3,195},{4,2},{5,197},{6,4},{7,199},{8,14},{9,... | collective-permute-start | bytes 1572872 | tf_op jit(solution)/shard_map/ppermute | solution.py:39
  164.9 0.3 collective-permute-start.25
  165.3 2.4 %gradient.5.refs_4_ = bf16[4,256,2048]{2,1,0:T(8,128)(2,1)} custom-call(s32[4]{0:T(128)S(1)} %pad_add_fusion.1.where, bf16[32,16,1024]{2,1,0:T(8,128)(2,1)S(1)} %collect.1.refs_0_, bf16[32,16,1024]{2,1,0:T(8,128)(2,1)S(1)} %collective-permute-done.28.refs_1_, bf16[256,512]{1,0:T(8,128)(2,1)S(1)} %bitcast.32, bf16[256,512]{1,0:T(8,128)(2,1)S(1)} %bitcast.37), custom_call_target="tpu_custom_call" | custom-call | flops 550000000 | bytes 4000000 | tf_op jit(solution)/shard_map/gradient/pallas_call | solution.py:180
  167.7 2.4 %gradient.6.refs_4_ = bf16[4,256,2048]{2,1,0:T(8,128)(2,1)} custom-call(s32[4]{0:T(128)S(1)} %pad_add_fusion.1.where, bf16[32,16,1024]{2,1,0:T(8,128)(2,1)S(1)} %collective-permute-done.24.refs_0_, bf16[32,16,1024]{2,1,0:T(8,128)(2,1)S(1)} %collective-permute-done.27.refs_1_, bf16[256,512]{1,0:T(8,128)(2,1)S(1)} %bitcast.33, ...), custom_call_target="tpu_custom_call", output_to_operand_aliasing={{}: (5, {})} | custom-call | flops 550000000 | bytes 4000000 | tf_op jit(solution)/shard_map/gradient/pallas_call | solution.py:180
  170.0 2.4 %gradient.7.refs_4_ = bf16[4,256,2048]{2,1,0:T(8,128)(2,1)} custom-call(s32[4]{0:T(128)S(1)} %pad_add_fusion.1.where, bf16[32,16,1024]{2,1,0:T(8,128)(2,1)S(1)} %collective-permute-done.22.refs_0_, bf16[32,16,1024]{2,1,0:T(8,128)(2,1)S(1)} %collective-permute-done.26.refs_1_, bf16[256,512]{1,0:T(8,128)(2,1)S(1)} %bitcast.34, ...), custom_call_target="tpu_custom_call", output_to_operand_aliasing={{}: (5, {})} | custom-call | flops 550000000 | bytes 4000000 | tf_op jit(solution)/shard_map/gradient/pallas_call | solution.py:180
  172.4 2.4 %collective-permute-done.25.refs_1_ = bf16[16,16,1024]{2,1,0:T(8,128)(2,1)S(1)} collective-permute-done((bf16[16,16,1024]{2,1,0:T(8,128)(2,1)S(1)}, bf16[16,16,1024]{2,1,0:T(8,128)(2,1)S(1)}, u32[]{:S(2)}, u32[]{:S(2)}) %collective-permute-start.25) | collective-permute-done | bytes 524320 | tf_op jit(solution)/shard_map/ppermute | solution.py:39
  174.8 1.9 %collective-permute-start.29 = (bf16[16,16,1024]{2,1,0:T(8,128)(2,1)S(1)}, bf16[16,16,1024]{2,1,0:T(8,128)(2,1)S(1)}, u32[]{:S(2)}, u32[]{:S(2)}) collective-permute-start(bf16[16,16,1024]{2,1,0:T(8,128)(2,1)S(1)} %collective-permute-done.23.refs_0_), channel_id=1, source_target_pairs={{0,1},{1,0},{2,3},{3,2},{4,5},{5,4},{6,7},{7,6},{8,9},{9,8},{10,11... | collective-permute-start | bytes 1572872 | tf_op jit(solution)/shard_map/ppermute | solution.py:31
  176.6 1.8 gradient.8.refs_4_
  178.4 0.5 collective-permute-done.30.refs_1_
  178.9 1.8 gradient.9
  (79 shorter events, 1.9 us)
Async XLA Ops:
  5.5 7.3 %collective-permute-start = (bf16[4,256,1024]{2,1,0:T(8,128)(2,1)}, bf16[4,256,1024]{2,1,0:T(8,128)(2,1)S(1)}, u32[]{:S(2)}, u32[]{:S(2)}) collective-permute-start(bf16[4,256,1024]{2,1,0:T(8,128)(2,1)} %dynamic-slice_bitcast_fusion), channel_id=1, source_target_pairs={{0,1},{1,0},{2,3},{3,2},{4,5},{5,4},{6,7},{7,6},{8,9},{9,8},{10,11... | collective-permute-start | bytes 6291464 | tf_op jit(solution)/shard_map/ppermute | solution.py:31
  8.8 3.7 %collective-permute-start.1 = (bf16[4,2,1024]{2,1,0:T(2,128)(2,1)S(1)}, bf16[4,2,1024]{2,1,0:T(2,128)(2,1)S(1)}, u32[]{:S(2)}, u32[]{:S(2)}) collective-permute-start(bf16[4,2,1024]{2,1,0:T(2,128)(2,1)S(1)} %get-tuple-element.62), channel_id=1, source_target_pairs={{0,1},{1,0},{2,3},{3,2},{4,5},{5,4},{6,7},{7,6},{8,9},{9,8},{10,11... | collective-permute-start | bytes 49160 | tf_op jit(solution)/shard_map/ppermute | solution.py:31
  8.9 11.8 %all-to-all-start = ((bf16[4,2,2048]{2,1,0:T(2,128)(2,1)}), bf16[4,2,2048]{2,1,0:T(2,128)(2,1)S(1)}, u32[]{:S(2)}, u32[]{:S(2)}) async-start(bf16[4,2,2048]{2,1,0:T(2,128)(2,1)} %bitcast.27), calls=%async_computation | async-start | bytes 65536 | tf_op jit(solution)/shard_map/all_to_all | solution.py:275
  12.8 2.2 %copy-start = (bf16[1,4,256,2048]{3,2,1,0:T(8,128)(2,1)S(1)}, bf16[1,4,256,2048]{3,2,1,0:T(8,128)(2,1)}, u32[]{:S(2)}) copy-start(bf16[1,4,256,2048]{3,2,1,0:T(8,128)(2,1)} %param.10) | copy-start | bytes 12582916
  15.9 1.0 copy-start.6
  17.8 1.0 copy-start.5
  18.8 44.2 %copy-start.14 = (f32[1,256]{1,0:T(1,128)S(1)}, f32[1,256]{1,0:T(1,128)}, u32[]{:S(2)}) copy-start(f32[1,256]{1,0:T(1,128)} %refs_9_.1) | copy-start | bytes 3076
  19.7 1.0 copy-start.7
  20.8 19.2 %collective-permute-start.2 = (bf16[528,1024]{1,0:T(8,128)(2,1)}, bf16[528,1024]{1,0:T(8,128)(2,1)S(1)}, u32[]{:S(2)}, u32[]{:S(2)}) collective-permute-start(bf16[528,1024]{1,0:T(8,128)(2,1)} %copy-done.7), channel_id=1, source_target_pairs={{0,2},{1,65},{2,4},{3,67},{4,6},{5,69},{6,0},{7,71},{8,10},{9,73},... | collective-permute-start | bytes 3244040 | tf_op jit(solution)/shard_map/ppermute | solution.py:39
  21.8 18.2 %collective-permute-start.3 = (bf16[528,1024]{1,0:T(8,128)(2,1)}, bf16[528,1024]{1,0:T(8,128)(2,1)}, u32[]{:S(2)}, u32[]{:S(2)}) collective-permute-start(bf16[528,1024]{1,0:T(8,128)(2,1)} %copy-done.6), channel_id=1, source_target_pairs={{0,6},{1,193},{2,0},{3,195},{4,2},{5,197},{6,4},{7,199},{8,14},{9,... | collective-permute-start | bytes 3244040 | tf_op jit(solution)/shard_map/ppermute | solution.py:39
  40.0 27.2 %copy-start.2 = (bf16[528,1024]{1,0:T(8,128)(2,1)}, bf16[528,1024]{1,0:T(8,128)(2,1)S(1)}, u32[]{:S(2)}) copy-start(bf16[528,1024]{1,0:T(8,128)(2,1)S(1)} %collective-permute-done.2.refs_4_) | copy-start | bytes 3244036
  40.0 16.4 %collective-permute-start.6 = (bf16[64,2048]{1,0:T(8,128)(2,1)}, bf16[64,2048]{1,0:T(8,128)(2,1)}, u32[]{:S(2)}, u32[]{:S(2)}) collective-permute-start(bf16[64,2048]{1,0:T(8,128)(2,1)} %bitcast.12.refs_0_), channel_id=1, source_target_pairs={{0,6},{2,0},{4,2},{6,4},{1,7},{3,1},{5,3},{7,5},{8,14},{10,8},{12,... | collective-permute-start | bytes 786440 | tf_op jit(solution)/shard_map/ppermute | solution.py:31
  45.4 12.5 %collective-permute-start.4 = (bf16[64,2048]{1,0:T(8,128)(2,1)}, bf16[64,2048]{1,0:T(8,128)(2,1)}, u32[]{:S(2)}, u32[]{:S(2)}) collective-permute-start(bf16[64,2048]{1,0:T(8,128)(2,1)} %bitcast.12.refs_0_), channel_id=1, source_target_pairs={{0,2},{2,4},{4,6},{6,0},{1,3},{3,5},{5,7},{7,1},{8,10},{10,12},{12... | collective-permute-start | bytes 786440 | tf_op jit(solution)/shard_map/ppermute | solution.py:31
  45.4 15.9 %collective-permute-start.5 = (bf16[64,2048]{1,0:T(8,128)(2,1)}, bf16[64,2048]{1,0:T(8,128)(2,1)}, u32[]{:S(2)}, u32[]{:S(2)}) collective-permute-start(bf16[64,2048]{1,0:T(8,128)(2,1)} %bitcast.12.refs_0_), channel_id=1, source_target_pairs={{0,4},{2,6},{4,0},{6,2},{1,5},{3,7},{5,1},{7,3},{8,12},{10,14},{12... | collective-permute-start | bytes 786440 | tf_op jit(solution)/shard_map/ppermute | solution.py:31
  47.1 14.6 %collective-permute-start.7 = (bf16[64,2048]{1,0:T(8,128)(2,1)}, bf16[64,2048]{1,0:T(8,128)(2,1)S(1)}, u32[]{:S(2)}, u32[]{:S(2)}) collective-permute-start(bf16[64,2048]{1,0:T(8,128)(2,1)} %bitcast.12.refs_0_), channel_id=1, source_target_pairs={{0,1},{1,0},{2,3},{3,2},{4,5},{5,4},{6,7},{7,6},{8,9},{9,8},{10,11... | collective-permute-start | bytes 786440 | tf_op jit(solution)/shard_map/ppermute | solution.py:31
  56.4 5.4 %collective-permute-start.10 = (bf16[64,2048]{1,0:T(8,128)(2,1)}, bf16[64,2048]{1,0:T(8,128)(2,1)S(1)}, u32[]{:S(2)}, u32[]{:S(2)}) collective-permute-start(bf16[64,2048]{1,0:T(8,128)(2,1)} %collective-permute-done.6.refs_3_), channel_id=1, source_target_pairs={{0,1},{1,0},{2,3},{3,2},{4,5},{5,4},{6,7},{7,6},{8,9},{9,8},{10,11... | collective-permute-start | bytes 786440 | tf_op jit(solution)/shard_map/ppermute | solution.py:31
  57.8 4.8 %collective-permute-start.8 = (bf16[64,2048]{1,0:T(8,128)(2,1)}, bf16[64,2048]{1,0:T(8,128)(2,1)S(1)}, u32[]{:S(2)}, u32[]{:S(2)}) collective-permute-start(bf16[64,2048]{1,0:T(8,128)(2,1)} %collective-permute-done.4.refs_1_), channel_id=1, source_target_pairs={{0,1},{1,0},{2,3},{3,2},{4,5},{5,4},{6,7},{7,6},{8,9},{9,8},{10,11... | collective-permute-start | bytes 786440 | tf_op jit(solution)/shard_map/ppermute | solution.py:31
  61.2 1.7 collective-permute-start.9
  61.6 27.4 %collective-permute-start.15 = (bf16[528,1024]{1,0:T(8,128)(2,1)}, bf16[528,1024]{1,0:T(8,128)(2,1)S(1)}, u32[]{:S(2)}, u32[]{:S(2)}) collective-permute-start(bf16[528,1024]{1,0:T(8,128)(2,1)} %copy-done.5), channel_id=1, source_target_pairs={{0,4},{1,129},{2,6},{3,131},{4,0},{5,133},{6,2},{7,135},{8,12},{9,... | collective-permute-start | bytes 3244040 | tf_op jit(solution)/shard_map/ppermute | solution.py:39
  63.0 1.2 copy-start.8
  64.2 7.9 %copy-start.1 = (bf16[1,4,256,2048]{3,2,1,0:T(8,128)(2,1)S(1)}, bf16[1,4,256,2048]{3,2,1,0:T(8,128)(2,1)}, u32[]{:S(2)}) copy-start(bf16[1,4,256,2048]{3,2,1,0:T(8,128)(2,1)} %param.10) | copy-start | bytes 12582916
  67.1 1.8 %copy-start.11 = (bf16[512,256]{1,0:T(8,128)(2,1)}, bf16[512,256]{1,0:T(8,128)(2,1)S(1)}, u32[]{:S(2)}) copy-start(bf16[512,256]{1,0:T(8,128)(2,1)S(1)} %get-tuple-element.42) | copy-start | bytes 786436
  67.1 5.9 %copy-start.9 = (bf16[512,256]{1,0:T(8,128)(2,1)}, bf16[512,256]{1,0:T(8,128)(2,1)S(1)}, u32[]{:S(2)}) copy-start(bf16[512,256]{1,0:T(8,128)(2,1)S(1)} %get-tuple-element.41) | copy-start | bytes 786436
  67.1 1.6 collective-permute-start.11
  68.8 14.5 %copy-start.3 = (bf16[528,1024]{1,0:T(8,128)(2,1)S(1)}, bf16[528,1024]{1,0:T(8,128)(2,1)}, u32[]{:S(2)}) copy-start(bf16[528,1024]{1,0:T(8,128)(2,1)} %copy-done.2) | copy-start | bytes 3244036
  68.8 14.5 %copy-start.13 = (f32[1,2048]{1,0:T(1,128)S(1)}, f32[1,2048]{1,0:T(1,128)}, u32[]{:S(2)}) copy-start(f32[1,2048]{1,0:T(1,128)} %refs_6_.1) | copy-start | bytes 24580
  68.8 14.5 %collective-permute-start.13 = (bf16[2,512,256]{2,1,0:T(8,128)(2,1)S(1)}, bf16[2,512,256]{2,1,0:T(8,128)(2,1)S(1)}, u32[]{:S(2)}, u32[]{:S(2)}) collective-permute-start(bf16[2,512,256]{2,1,0:T(8,128)(2,1)S(1)} %pad_maximum_fusion.refs_0_), channel_id=1, source_target_pairs={{0,2},{1,65},{2,4},{3,67},{4,6},{5,69},{6,0},{7,71},{8,10},{9,73},... | collective-permute-start | bytes 1572872 | tf_op jit(solution)/shard_map/ppermute | solution.py:39
  68.9 14.4 %collective-permute-start.14 = (bf16[2,512,256]{2,1,0:T(8,128)(2,1)S(1)}, bf16[2,512,256]{2,1,0:T(8,128)(2,1)S(1)}, u32[]{:S(2)}, u32[]{:S(2)}) collective-permute-start(bf16[2,512,256]{2,1,0:T(8,128)(2,1)S(1)} %pad_maximum_fusion.refs_0_), channel_id=1, source_target_pairs={{0,6},{1,193},{2,0},{3,195},{4,2},{5,197},{6,4},{7,199},{8,14},{9,... | collective-permute-start | bytes 1572872 | tf_op jit(solution)/shard_map/ppermute | solution.py:39
  71.6 17.4 %collective-permute-start.12 = (bf16[2,512,256]{2,1,0:T(8,128)(2,1)S(1)}, bf16[2,512,256]{2,1,0:T(8,128)(2,1)S(1)}, u32[]{:S(2)}, u32[]{:S(2)}) collective-permute-start(bf16[2,512,256]{2,1,0:T(8,128)(2,1)S(1)} %pad_maximum_fusion.refs_0_), channel_id=1, source_target_pairs={{0,4},{1,129},{2,6},{3,131},{4,0},{5,133},{6,2},{7,135},{8,12},{9,... | collective-permute-start | bytes 1572872 | tf_op jit(solution)/shard_map/ppermute | solution.py:39
  87.9 6.9 %copy-start.10 = (bf16[512,256]{1,0:T(8,128)(2,1)S(1)}, bf16[512,256]{1,0:T(8,128)(2,1)}, u32[]{:S(2)}) copy-start(bf16[512,256]{1,0:T(8,128)(2,1)} %copy-done.9) | copy-start | bytes 786436
  87.9 7.0 %copy-start.12 = (bf16[512,256]{1,0:T(8,128)(2,1)S(1)}, bf16[512,256]{1,0:T(8,128)(2,1)}, u32[]{:S(2)}) copy-start(bf16[512,256]{1,0:T(8,128)(2,1)} %copy-done.11) | copy-start | bytes 786436
  89.0 4.3 %copy-start.4 = (bf16[528,1024]{1,0:T(8,128)(2,1)}, bf16[528,1024]{1,0:T(8,128)(2,1)S(1)}, u32[]{:S(2)}) copy-start(bf16[528,1024]{1,0:T(8,128)(2,1)S(1)} %collective-permute-done.15.refs_1_) | copy-start | bytes 3244036
  91.5 25.1 %slice-start = ((bf16[528,1024]{1,0:T(8,128)(2,1)}), bf16[4,1024]{1,0:T(4,128)(2,1)S(1)}, s32[]{:S(2)}) async-start(bf16[528,1024]{1,0:T(8,128)(2,1)} %copy-done.2), calls=%async_computation.4 | async-start | bytes 16384 | tf_op jit(solution)/shard_map/slice | solution.py:299
  91.5 9.6 %collective-permute-start.16 = (bf16[8,16,1024]{2,1,0:T(8,128)(2,1)S(1)}, bf16[8,16,1024]{2,1,0:T(8,128)(2,1)S(1)}, u32[]{:S(2)}, u32[]{:S(2)}) collective-permute-start(bf16[8,16,1024]{2,1,0:T(8,128)(2,1)S(1)} %get-tuple-element.49), channel_id=1, source_target_pairs={{0,64},{1,3},{2,66},{3,5},{4,68},{5,7},{6,70},{7,1},{8,72},{9,11},... | collective-permute-start | bytes 786440 | tf_op jit(solution)/shard_map/ppermute | solution.py:47
  91.6 9.5 %collective-permute-start.17 = (bf16[8,16,1024]{2,1,0:T(8,128)(2,1)S(1)}, bf16[8,16,1024]{2,1,0:T(8,128)(2,1)}, u32[]{:S(2)}, u32[]{:S(2)}) collective-permute-start(bf16[8,16,1024]{2,1,0:T(8,128)(2,1)S(1)} %get-tuple-element.50), channel_id=1, source_target_pairs={{0,128},{1,5},{2,130},{3,7},{4,132},{5,1},{6,134},{7,3},{8,136},{9... | collective-permute-start | bytes 786440 | tf_op jit(solution)/shard_map/ppermute | solution.py:47
  93.3 8.6 %collective-permute-start.18 = (bf16[8,16,1024]{2,1,0:T(8,128)(2,1)S(1)}, bf16[8,16,1024]{2,1,0:T(8,128)(2,1)}, u32[]{:S(2)}, u32[]{:S(2)}) collective-permute-start(bf16[8,16,1024]{2,1,0:T(8,128)(2,1)S(1)} %get-tuple-element.51), channel_id=1, source_target_pairs={{0,192},{1,7},{2,194},{3,1},{4,196},{5,3},{6,198},{7,5},{8,200},{9... | collective-permute-start | bytes 786440 | tf_op jit(solution)/shard_map/ppermute | solution.py:47
  94.8 21.8 %slice-start.1 = ((bf16[528,1024]{1,0:T(8,128)(2,1)}), bf16[4,1024]{1,0:T(4,128)(2,1)S(1)}, s32[]{:S(2)}) async-start(bf16[528,1024]{1,0:T(8,128)(2,1)} %copy-done.4), calls=%async_computation.5 | async-start | bytes 16384 | tf_op jit(solution)/shard_map/slice | solution.py:299
  103.8 12.8 %all-to-all-start.2 = ((bf16[8,16,1024]{2,1,0:T(8,128)(2,1)}), bf16[8,16,1024]{2,1,0:T(8,128)(2,1)S(1)}, u32[]{:S(2)}, u32[]{:S(2)}) async-start(bf16[8,16,1024]{2,1,0:T(8,128)(2,1)} %add_convert_fusion), calls=%async_computation.2 | async-start | bytes 524288 | tf_op jit(solution)/shard_map/all_to_all | solution.py:309
  128.7 11.7 %collective-permute-start.19 = (bf16[8,16,1024]{2,1,0:T(8,128)(2,1)S(1)}, bf16[8,16,1024]{2,1,0:T(8,128)(2,1)S(1)}, u32[]{:S(2)}, u32[]{:S(2)}) collective-permute-start(bf16[8,16,1024]{2,1,0:T(8,128)(2,1)S(1)} %all_to_all.21.refs_0_), channel_id=1, source_target_pairs={{0,64},{1,3},{2,66},{3,5},{4,68},{5,7},{6,70},{7,1},{8,72},{9,11},... | collective-permute-start | bytes 786440 | tf_op jit(solution)/shard_map/ppermute | solution.py:47
  134.6 9.6 %collective-permute-start.20 = (bf16[8,16,1024]{2,1,0:T(8,128)(2,1)S(1)}, bf16[8,16,1024]{2,1,0:T(8,128)(2,1)S(1)}, u32[]{:S(2)}, u32[]{:S(2)}) collective-permute-start(bf16[8,16,1024]{2,1,0:T(8,128)(2,1)S(1)} %all_to_all.21.refs_0_), channel_id=1, source_target_pairs={{0,128},{1,5},{2,130},{3,7},{4,132},{5,1},{6,134},{7,3},{8,136},{9... | collective-permute-start | bytes 786440 | tf_op jit(solution)/shard_map/ppermute | solution.py:47
  137.6 6.6 %collective-permute-start.21 = (bf16[8,16,1024]{2,1,0:T(8,128)(2,1)S(1)}, bf16[8,16,1024]{2,1,0:T(8,128)(2,1)S(1)}, u32[]{:S(2)}, u32[]{:S(2)}) collective-permute-start(bf16[8,16,1024]{2,1,0:T(8,128)(2,1)S(1)} %all_to_all.21.refs_0_), channel_id=1, source_target_pairs={{0,192},{1,7},{2,194},{3,1},{4,196},{5,3},{6,198},{7,5},{8,200},{9... | collective-permute-start | bytes 786440 | tf_op jit(solution)/shard_map/ppermute | solution.py:47
  145.1 15.2 %collective-permute-start.24 = (bf16[32,16,1024]{2,1,0:T(8,128)(2,1)S(1)}, bf16[32,16,1024]{2,1,0:T(8,128)(2,1)S(1)}, u32[]{:S(2)}, u32[]{:S(2)}) collective-permute-start(bf16[32,16,1024]{2,1,0:T(8,128)(2,1)S(1)} %collect.1.refs_0_), channel_id=1, source_target_pairs={{0,2},{1,65},{2,4},{3,67},{4,6},{5,69},{6,0},{7,71},{8,10},{9,73},... | collective-permute-start | bytes 3145736 | tf_op jit(solution)/shard_map/ppermute | solution.py:39
  145.2 17.3 %collective-permute-start.22 = (bf16[32,16,1024]{2,1,0:T(8,128)(2,1)S(1)}, bf16[32,16,1024]{2,1,0:T(8,128)(2,1)S(1)}, u32[]{:S(2)}, u32[]{:S(2)}) collective-permute-start(bf16[32,16,1024]{2,1,0:T(8,128)(2,1)S(1)} %collect.1.refs_0_), channel_id=1, source_target_pairs={{0,6},{1,193},{2,0},{3,195},{4,2},{5,197},{6,4},{7,199},{8,14},{9,... | collective-permute-start | bytes 3145736 | tf_op jit(solution)/shard_map/ppermute | solution.py:39
  147.8 17.4 %collective-permute-start.28 = (bf16[32,16,1024]{2,1,0:T(8,128)(2,1)S(1)}, bf16[32,16,1024]{2,1,0:T(8,128)(2,1)S(1)}, u32[]{:S(2)}, u32[]{:S(2)}) collective-permute-start(bf16[32,16,1024]{2,1,0:T(8,128)(2,1)S(1)} %collect.1.refs_0_), channel_id=1, source_target_pairs={{0,1},{1,0},{2,3},{3,2},{4,5},{5,4},{6,7},{7,6},{8,9},{9,8},{10,11... | collective-permute-start | bytes 3145736 | tf_op jit(solution)/shard_map/ppermute | solution.py:31
  160.3 7.4 %collective-permute-start.27 = (bf16[32,16,1024]{2,1,0:T(8,128)(2,1)S(1)}, bf16[32,16,1024]{2,1,0:T(8,128)(2,1)S(1)}, u32[]{:S(2)}, u32[]{:S(2)}) collective-permute-start(bf16[32,16,1024]{2,1,0:T(8,128)(2,1)S(1)} %collective-permute-done.24.refs_0_), channel_id=1, source_target_pairs={{0,1},{1,0},{2,3},{3,2},{4,5},{5,4},{6,7},{7,6},{8,9},{9,8},{10,11... | collective-permute-start | bytes 3145736 | tf_op jit(solution)/shard_map/ppermute | solution.py:31
  162.5 7.6 %collective-permute-start.26 = (bf16[32,16,1024]{2,1,0:T(8,128)(2,1)S(1)}, bf16[32,16,1024]{2,1,0:T(8,128)(2,1)S(1)}, u32[]{:S(2)}, u32[]{:S(2)}) collective-permute-start(bf16[32,16,1024]{2,1,0:T(8,128)(2,1)S(1)} %collective-permute-done.22.refs_0_), channel_id=1, source_target_pairs={{0,1},{1,0},{2,3},{3,2},{4,5},{5,4},{6,7},{7,6},{8,9},{9,8},{10,11... | collective-permute-start | bytes 3145736 | tf_op jit(solution)/shard_map/ppermute | solution.py:31
  162.5 9.9 %collective-permute-start.23 = (bf16[16,16,1024]{2,1,0:T(8,128)(2,1)S(1)}, bf16[16,16,1024]{2,1,0:T(8,128)(2,1)S(1)}, u32[]{:S(2)}, u32[]{:S(2)}) collective-permute-start(bf16[16,16,1024]{2,1,0:T(8,128)(2,1)S(1)} %slice.46), channel_id=1, source_target_pairs={{0,6},{1,193},{2,0},{3,195},{4,2},{5,197},{6,4},{7,199},{8,14},{9,... | collective-permute-start | bytes 1572872 | tf_op jit(solution)/shard_map/ppermute | solution.py:39
  164.9 9.8 %collective-permute-start.25 = (bf16[16,16,1024]{2,1,0:T(8,128)(2,1)S(1)}, bf16[16,16,1024]{2,1,0:T(8,128)(2,1)S(1)}, u32[]{:S(2)}, u32[]{:S(2)}) collective-permute-start(bf16[16,16,1024]{2,1,0:T(8,128)(2,1)S(1)} %slice.47), channel_id=1, source_target_pairs={{0,2},{1,65},{2,4},{3,67},{4,6},{5,69},{6,0},{7,71},{8,10},{9,73},... | collective-permute-start | bytes 1572872 | tf_op jit(solution)/shard_map/ppermute | solution.py:39
  174.8 3.7 %collective-permute-start.29 = (bf16[16,16,1024]{2,1,0:T(8,128)(2,1)S(1)}, bf16[16,16,1024]{2,1,0:T(8,128)(2,1)S(1)}, u32[]{:S(2)}, u32[]{:S(2)}) collective-permute-start(bf16[16,16,1024]{2,1,0:T(8,128)(2,1)S(1)} %collective-permute-done.23.refs_0_), channel_id=1, source_target_pairs={{0,1},{1,0},{2,3},{3,2},{4,5},{5,4},{6,7},{7,6},{8,9},{9,8},{10,11... | collective-permute-start | bytes 1572872 | tf_op jit(solution)/shard_map/ppermute | solution.py:31
  176.6 2.3 %collective-permute-start.30 = (bf16[16,16,1024]{2,1,0:T(8,128)(2,1)S(1)}, bf16[16,16,1024]{2,1,0:T(8,128)(2,1)S(1)}, u32[]{:S(2)}, u32[]{:S(2)}) collective-permute-start(bf16[16,16,1024]{2,1,0:T(8,128)(2,1)S(1)} %collective-permute-done.25.refs_1_), channel_id=1, source_target_pairs={{0,1},{1,0},{2,3},{3,2},{4,5},{5,4},{6,7},{7,6},{8,9},{9,8},{10,11... | collective-permute-start | bytes 1572872 | tf_op jit(solution)/shard_map/ppermute | solution.py:31

commit v5 on v4

--- a/solution.py
+++ b/solution.py
@@ -221,37 +221,43 @@
     )(where, *pieces)
 
 
-def pack_kernel(where, own, other, target, out):
-    feats = own.shape[1]
-    out[:feats, :] = own[0]
-    out[feats:2 * feats, :] = other[0]
-    out[2 * feats:, :] = target[0]
-
-
-def pack(step, where, weight, other, target):
+def pack_kernel(where, *refs):
+    outs = refs[3 * len(refs) // 4:]
+    for i, out in enumerate(outs):
+        own, other, target = refs[3 * i:3 * i + 3]
+        feats = own.shape[1]
+        out[:feats, :] = own[0]
+        out[feats:2 * feats, :] = other[0]
+        out[2 * feats:, :] = target[0]
+
+
+def pack(steps, where, weight, other, target):
     layers, feats, half = other.shape
     extra = target.shape[1]
-
-    def sink(where):
-        return lax.rem(jnp.where(where[3] == 0, where[2], where[0]) + step, NY)
-
+    in_specs = []
+    for step in steps:
+
+        def sink(where, step=step):
+            return lax.rem(jnp.where(where[3] == 0, where[2], where[0]) + step, NY)
+
+        in_specs += [
+            pl.BlockSpec((1, feats, half // 2), lambda n, where, sink=sink: (sink(where), 0, where[3] * 2 + n)),
+            pl.BlockSpec((1, feats, half // 2), lambda n, where, sink=sink: (sink(where), 0, n)),
+            pl.BlockSpec((1, extra, half // 2), lambda n, where, sink=sink: (sink(where), 0, n)),
+        ]
     return pl.pallas_call(
         pack_kernel,
         grid_spec=pltpu.PrefetchScalarGridSpec(
             num_scalar_prefetch=1,
             grid=(2,),
-            in_specs=[
-                pl.BlockSpec((1, feats, half // 2), lambda n, where: (sink(where), 0, where[3] * 2 + n)),
-                pl.BlockSpec((1, feats, half // 2), lambda n, where: (sink(where), 0, n)),
-                pl.BlockSpec((1, extra, half // 2), lambda n, where: (sink(where), 0, n)),
-            ],
-            out_specs=pl.BlockSpec((2 * feats + extra, half // 2), lambda n, where: (0, n)),
-        ),
-        out_shape=jax.ShapeDtypeStruct((2 * feats + extra, half), BF),
-        compiler_params=pltpu.CompilerParams(vmem_limit_bytes=VMEM_LIMIT),
-        cost_estimate=pl.CostEstimate(flops=0, bytes_accessed=2 * 10**6, transcendentals=0),
+            in_specs=in_specs,
+            out_specs=[pl.BlockSpec((2 * feats + extra, half // 2), lambda n, where: (0, n))] * len(steps),
+        ),
+        out_shape=[jax.ShapeDtypeStruct((2 * feats + extra, half), BF)] * len(steps),
+        compiler_params=pltpu.CompilerParams(vmem_limit_bytes=VMEM_LIMIT),
+        cost_estimate=pl.CostEstimate(flops=0, bytes_accessed=2 * 10**6 * len(steps), transcendentals=0),
         name="pack",
-    )(where, weight, other, target)
+    )(where, *([weight, other, target] * len(steps)))
 
 
 def body(resid, target, enc_weight, enc_bias, dec_weight, dec_bias):
@@ -271,7 +277,7 @@
     rows, give, aims, where = lax.optimization_barrier((rows, give, aims, where))
     extra = jnp.concatenate([aims[0], shift(aims[1], "c", 1), jnp.zeros((layers, 16 - 2 * mine, half), BF)], axis=1)
     give = shift(give, "c", 1)
-    weights = [pack(step, where, dec_weight[0], give, extra) for step in range(NY)]
+    weights = [*pack((0,), where, dec_weight[0], give, extra), *pack((1, 2, 3), where, dec_weight[0], give, extra)]
     rows = lax.all_to_all(rows, "x", 0, 0, tiled=True)
     rows, *sent = lax.optimization_barrier((rows, *weights[1:]))
     weights = weights[:1] + [ring(piece, step) for step, piece in enumerate(sent, 1)]

time: 181 us -> 180 us (level)
    pallas_call x4 -> x2, Pallas kernels: 3.67 us -> 2.55 us  [pack(): pl.pallas_call(pack_kernel, grid_spec=pltpu.PrefetchScalarGridSpec(num_sc...]
where the time goes in v5:
time: 180 us
  waiting for transfers between devices  57.5 us (32%)
  starting transfers between devices  53.5 us (30%)
  blocking collectives  28.3 us (16%)
  Pallas kernels  24.1 us (13%)
  local copies, waits for them, and re-layouts  13 us (7%)
  other arithmetic  2.63 us (1%)
    ppermute x10, waiting for transfers between devices, ring(): return lax.ppermute(value, ALL, pairs)  24.3 us
    ppermute x15, starting transfers between devices, shift(): lax.ppermute(value, axis, [(i, (i + step) % size) for i in range(size)])  23.2 us
    all_to_all x1, blocking collectives, body(): rows = lax.all_to_all(rows, 'z', 0, 0, tiled=True).reshape(XZ * mine, width)  16.5 us
    ppermute x6, waiting for transfers between devices, cross(): return lax.ppermute(value, ALL, pairs)  13.3 us
    ppermute x6, starting transfers between devices, cross(): return lax.ppermute(value, ALL, pairs)  12.3 us
    all_to_all x1, blocking collectives, body(): lax.all_to_all(jnp.broadcast_to(cotangent[None], (NZ,) + cotangent.shape)...  11.8 us
    ppermute x10, starting transfers between devices, ring(): return lax.ppermute(value, ALL, pairs)  11.4 us
    ppermute x15, waiting for transfers between devices, shift(): lax.ppermute(value, axis, [(i, (i + step) % size) for i in range(size)])  11.3 us
  transfers between devices with their start and end apart: 33, of which 16 were waited for; matrix products, arithmetic and copies ran while one was open for 1% of the time, Pallas kernels for 11%

profile of v5, /device:TPU:1, one launch (start us, length us, event | category | flops | bytes accessed | tf_op | source)
XLA Modules:
  0.0 179.6 jit_solution(17306524916328274509)
XLA Ops:
  0.0 0.8 reshape.384
  0.8 1.4 copy.33
  2.2 3.1 %dynamic-slice_bitcast_fusion = bf16[4,256,1024]{2,1,0:T(8,128)(2,1)} fusion(bf16[1,4,256,2048]{3,2,1,0:T(8,128)(2,1)} %param.10, s32[]{:T(128)S(6)} %select_n.251), kind=kLoop, calls=%fused_computation.1 | loop fusion | bytes 4194308 | tf_op jit(solution)/shard_map/dynamic_slice | solution.py:273
  5.5 3.3 %collective-permute-start = (bf16[4,256,1024]{2,1,0:T(8,128)(2,1)}, bf16[4,256,1024]{2,1,0:T(8,128)(2,1)S(1)}, u32[]{:S(2)}, u32[]{:S(2)}) collective-permute-start(bf16[4,256,1024]{2,1,0:T(8,128)(2,1)} %dynamic-slice_bitcast_fusion), channel_id=1, source_target_pairs={{0,1},{1,0},{2,3},{3,2},{4,5},{5,4},{6,7},{7,6},{8,9},{9,8},{10,11... | collective-permute-start | bytes 6291464 | tf_op jit(solution)/shard_map/ppermute | solution.py:31
  8.9 3.3 %all-to-all-start = ((bf16[4,2,2048]{2,1,0:T(2,128)(2,1)}), bf16[4,2,2048]{2,1,0:T(2,128)(2,1)S(1)}, u32[]{:S(2)}, u32[]{:S(2)}) async-start(bf16[4,2,2048]{2,1,0:T(2,128)(2,1)} %bitcast.27), calls=%async_computation | async-start | bytes 65536 | tf_op jit(solution)/shard_map/all_to_all | solution.py:281
  12.3 0.2 collective-permute-done.1
  12.6 0.3 collective-permute-done.refs_1_.refs_4_.refs_7_
  12.8 2.2 %copy-done = bf16[1,4,256,2048]{3,2,1,0:T(8,128)(2,1)S(1)} copy-done((bf16[1,4,256,2048]{3,2,1,0:T(8,128)(2,1)S(1)}, bf16[1,4,256,2048]{3,2,1,0:T(8,128)(2,1)}, u32[]{:S(2)}) %copy-start) | copy-done | bytes 4194328
  15.0 1.6 pack.2
  16.7 1.0 copy-done.12
  17.6 1.0 copy-done.13
  18.6 1.0 copy-done.14
  19.6 1.0 collective-permute-start.2
  20.6 1.7 collective-permute-start.3
  22.3 16.5 %all_to_all.20 = bf16[8,8,2048]{2,1,0:T(8,128)(2,1)} all-to-all(bf16[8,8,2048]{2,1,0:T(8,128)(2,1)S(1)} %broadcast_in_dim.41), channel_id=1, replica_groups=mesh['x'=4,'z'=8,'y'=4,'c'=2] {'z'}, dimensions={0} | all-to-all | bytes 524288 | tf_op jit(solution)/shard_map/all_to_all | solution.py:285
  38.8 5.4 %collective-permute-start.6 = (bf16[64,2048]{1,0:T(8,128)(2,1)}, bf16[64,2048]{1,0:T(8,128)(2,1)}, u32[]{:S(2)}, u32[]{:S(2)}) collective-permute-start(bf16[64,2048]{1,0:T(8,128)(2,1)} %bitcast.12.refs_0_), channel_id=1, source_target_pairs={{0,6},{2,0},{4,2},{6,4},{1,7},{3,1},{5,3},{7,5},{8,14},{10,8},{12,... | collective-permute-start | bytes 786440 | tf_op jit(solution)/shard_map/ppermute | solution.py:31
  44.2 1.6 collective-permute-start.5
  45.9 1.4 collective-permute-start.7
  47.3 7.9 %collective-permute-done.6.refs_3_ = bf16[64,2048]{1,0:T(8,128)(2,1)} collective-permute-done((bf16[64,2048]{1,0:T(8,128)(2,1)}, bf16[64,2048]{1,0:T(8,128)(2,1)}, u32[]{:S(2)}, u32[]{:S(2)}) %collective-permute-start.6) | collective-permute-done | bytes 262176 | tf_op jit(solution)/shard_map/ppermute | solution.py:31
  55.2 1.5 collective-permute-start.10
  56.7 3.4 %collective-permute-start.8 = (bf16[64,2048]{1,0:T(8,128)(2,1)}, bf16[64,2048]{1,0:T(8,128)(2,1)S(1)}, u32[]{:S(2)}, u32[]{:S(2)}) collective-permute-start(bf16[64,2048]{1,0:T(8,128)(2,1)} %collective-permute-done.4.refs_1_), channel_id=1, source_target_pairs={{0,1},{1,0},{2,3},{3,2},{4,5},{5,4},{6,7},{7,6},{8,9},{9,8},{10,11... | collective-permute-start | bytes 786440 | tf_op jit(solution)/shard_map/ppermute | solution.py:31
  60.1 0.3 fusion.refs_10_
  60.6 0.9 collective-permute-done.8.refs_5_
  61.5 0.4 collective-permute-done.9.refs_6_
  61.9 1.2 copy-done.5
  63.1 2.9 %encode.1 = (bf16[512,256]{1,0:T(8,128)(2,1)S(1)}, bf16[512,256]{1,0:T(8,128)(2,1)S(1)}) custom-call(bf16[64,2048]{1,0:T(8,128)(2,1)} %bitcast.12.refs_0_, bf16[64,2048]{1,0:T(8,128)(2,1)} %collective-permute-done.4.refs_1_, bf16[64,2048]{1,0:T(8,128)(2,1)} %collective-permute-done.5.refs_2_, bf16[64,2048]{1,0:T(8,128)(2,1)} %collective-permute-done.6.refs_3_, ...), custom_call_target="tpu_custom_call" | custom-call | flops 800000000 | bytes 4000000 | tf_op jit(solution)/shard_map/encode/pallas_call | solution.py:64
  66.0 0.5 collective-permute-start.11
  66.5 1.2 collective-permute-done.11
  67.8 2.7 %collective-permute-start.14 = (bf16[2,512,256]{2,1,0:T(8,128)(2,1)S(1)}, bf16[2,512,256]{2,1,0:T(8,128)(2,1)S(1)}, u32[]{:S(2)}, u32[]{:S(2)}) collective-permute-start(bf16[2,512,256]{2,1,0:T(8,128)(2,1)S(1)} %pad_maximum_fusion.refs_0_), channel_id=1, source_target_pairs={{0,6},{1,193},{2,0},{3,195},{4,2},{5,197},{6,4},{7,199},{8,14},{9,... | collective-permute-start | bytes 1572872 | tf_op jit(solution)/shard_map/ppermute | solution.py:39
  70.5 0.5 collective-permute-start.12
  71.0 0.9 pack.3.refs_3_
  71.9 10.3 %collective-permute-done.13.refs_1_ = bf16[2,512,256]{2,1,0:T(8,128)(2,1)S(1)} collective-permute-done((bf16[2,512,256]{2,1,0:T(8,128)(2,1)S(1)}, bf16[2,512,256]{2,1,0:T(8,128)(2,1)S(1)}, u32[]{:S(2)}, u32[]{:S(2)}) %collective-permute-start.13) | collective-permute-done | bytes 524320 | tf_op jit(solution)/shard_map/ppermute | solution.py:39
  82.2 4.6 %decode.2.refs_2_ = f32[512,1024]{1,0:T(8,128)S(1)} custom-call(s32[4]{0:T(128)S(1)} %pad_add_fusion.1.where, bf16[2,512,256]{2,1,0:T(8,128)(2,1)S(1)} %pad_maximum_fusion.refs_0_, bf16[2,512,256]{2,1,0:T(8,128)(2,1)S(1)} %collective-permute-done.13.refs_1_, bf16[2,512,256]{2,1,0:T(8,128)(2,1)S(1)} %collective-permute-done.14.refs_2_, ...), custom_call_target="tpu_custom_call" | custom-call | flops 1650000000 | bytes 4000000 | tf_op jit(solution)/shard_map/decode/pallas_call | solution.py:122
  86.8 1.1 collective-permute-done.12.refs_0_
  87.8 2.5 %decode.3 = (bf16[8,16,1024]{2,1,0:T(8,128)(2,1)S(1)}, bf16[8,16,1024]{2,1,0:T(8,128)(2,1)S(1)}, bf16[8,16,1024]{2,1,0:T(8,128)(2,1)S(1)}, bf16[8,16,1024]{2,1,0:T(8,128)(2,1)S(1)}) custom-call(s32[4]{0:T(128)S(1)} %pad_add_fusion.1.where, bf16[2,512,256]{2,1,0:T(8,128)(2,1)S(1)} %collective-permute-done.12.refs_0_, ...), custom_call_target="tpu_custom_call" | custom-call | flops 550000000 | bytes 4000000 | tf_op jit(solution)/shard_map/decode/pallas_call | solution.py:122
  90.5 1.7 collective-permute-start.17
  92.2 1.5 collective-permute-start.18
  94.0 6.0 %collective-permute-done.16 = bf16[8,16,1024]{2,1,0:T(8,128)(2,1)S(1)} collective-permute-done((bf16[8,16,1024]{2,1,0:T(8,128)(2,1)S(1)}, bf16[8,16,1024]{2,1,0:T(8,128)(2,1)S(1)}, u32[]{:S(2)}, u32[]{:S(2)}) %collective-permute-start.16) | collective-permute-done | bytes 262176 | tf_op jit(solution)/shard_map/ppermute | solution.py:47
  100.0 0.7 collective-permute-done.18
  100.7 1.9 %add_convert_fusion = bf16[8,16,1024]{2,1,0:T(8,128)(2,1)} fusion(bf16[8,16,1024]{2,1,0:T(8,128)(2,1)} %collective-permute-done.18, bf16[8,16,1024]{2,1,0:T(8,128)(2,1)} %collective-permute-done.17, bf16[8,16,1024]{2,1,0:T(8,128)(2,1)S(1)} %collective-permute-done.16, bf16[8,16,1024]{2,1,0:T(8,128)(2,1)S(1)} %get-tuple-element.58), kind=kLoop, calls=%fused_computation.8 | loop fusion | flops 1048576 | bytes 1310720 | tf_op jit(solution)/shard_map/convert_element_type | solution.py:314
  102.6 3.4 %all-to-all-start.2 = ((bf16[8,16,1024]{2,1,0:T(8,128)(2,1)}), bf16[8,16,1024]{2,1,0:T(8,128)(2,1)S(1)}, u32[]{:S(2)}, u32[]{:S(2)}) async-start(bf16[8,16,1024]{2,1,0:T(8,128)(2,1)} %add_convert_fusion), calls=%async_computation.2 | async-start | bytes 524288 | tf_op jit(solution)/shard_map/all_to_all | solution.py:315
  106.1 0.7 slice.39
  106.8 8.6 %all-to-all-done.2 = bf16[8,16,1024]{2,1,0:T(8,128)(2,1)S(1)} async-done(((bf16[8,16,1024]{2,1,0:T(8,128)(2,1)}), bf16[8,16,1024]{2,1,0:T(8,128)(2,1)S(1)}, u32[]{:S(2)}, u32[]{:S(2)}) %all-to-all-start.2) | async-done | bytes 262176 | tf_op jit(solution)/shard_map/all_to_all | solution.py:315
  115.5 0.1 fusion.2
  115.7 11.8 %all_to_all.21.refs_0_ = bf16[8,16,1024]{2,1,0:T(8,128)(2,1)S(1)} all-to-all(bf16[8,16,1024]{2,1,0:T(8,128)(2,1)S(1)} %broadcast_in_dim.46), channel_id=1, replica_groups=mesh['x'=4,'z'=8,'y'=4,'c'=2] {'z'}, dimensions={0} | all-to-all | bytes 524288 | tf_op jit(solution)/shard_map/all_to_all | solution.py:319
  127.5 5.9 %collective-permute-start.19 = (bf16[8,16,1024]{2,1,0:T(8,128)(2,1)S(1)}, bf16[8,16,1024]{2,1,0:T(8,128)(2,1)S(1)}, u32[]{:S(2)}, u32[]{:S(2)}) collective-permute-start(bf16[8,16,1024]{2,1,0:T(8,128)(2,1)S(1)} %all_to_all.21.refs_0_), channel_id=1, source_target_pairs={{0,64},{1,3},{2,66},{3,5},{4,68},{5,7},{6,70},{7,1},{8,72},{9,11},... | collective-permute-start | bytes 786440 | tf_op jit(solution)/shard_map/ppermute | solution.py:47
  133.4 3.1 %collective-permute-start.20 = (bf16[8,16,1024]{2,1,0:T(8,128)(2,1)S(1)}, bf16[8,16,1024]{2,1,0:T(8,128)(2,1)S(1)}, u32[]{:S(2)}, u32[]{:S(2)}) collective-permute-start(bf16[8,16,1024]{2,1,0:T(8,128)(2,1)S(1)} %all_to_all.21.refs_0_), channel_id=1, source_target_pairs={{0,128},{1,5},{2,130},{3,7},{4,132},{5,1},{6,134},{7,3},{8,136},{9... | collective-permute-start | bytes 786440 | tf_op jit(solution)/shard_map/ppermute | solution.py:47
  136.5 2.7 %collective-permute-done.19.refs_1_ = bf16[8,16,1024]{2,1,0:T(8,128)(2,1)S(1)} collective-permute-done((bf16[8,16,1024]{2,1,0:T(8,128)(2,1)S(1)}, bf16[8,16,1024]{2,1,0:T(8,128)(2,1)S(1)}, u32[]{:S(2)}, u32[]{:S(2)}) %collective-permute-start.19) | collective-permute-done | bytes 262176 | tf_op jit(solution)/shard_map/ppermute | solution.py:47
  139.3 3.8 %collective-permute-done.20.refs_2_ = bf16[8,16,1024]{2,1,0:T(8,128)(2,1)S(1)} collective-permute-done((bf16[8,16,1024]{2,1,0:T(8,128)(2,1)S(1)}, bf16[8,16,1024]{2,1,0:T(8,128)(2,1)S(1)}, u32[]{:S(2)}, u32[]{:S(2)}) %collective-permute-start.20) | collective-permute-done | bytes 262176 | tf_op jit(solution)/shard_map/ppermute | solution.py:47
  143.1 0.8 collect.1.refs_0_
  144.0 2.7 %collective-permute-start.22 = (bf16[32,16,1024]{2,1,0:T(8,128)(2,1)S(1)}, bf16[32,16,1024]{2,1,0:T(8,128)(2,1)S(1)}, u32[]{:S(2)}, u32[]{:S(2)}) collective-permute-start(bf16[32,16,1024]{2,1,0:T(8,128)(2,1)S(1)} %collect.1.refs_0_), channel_id=1, source_target_pairs={{0,6},{1,193},{2,0},{3,195},{4,2},{5,197},{6,4},{7,199},{8,14},{9,... | collective-permute-start | bytes 3145736 | tf_op jit(solution)/shard_map/ppermute | solution.py:39
  146.7 2.0 %collective-permute-start.28 = (bf16[32,16,1024]{2,1,0:T(8,128)(2,1)S(1)}, bf16[32,16,1024]{2,1,0:T(8,128)(2,1)S(1)}, u32[]{:S(2)}, u32[]{:S(2)}) collective-permute-start(bf16[32,16,1024]{2,1,0:T(8,128)(2,1)S(1)} %collect.1.refs_0_), channel_id=1, source_target_pairs={{0,1},{1,0},{2,3},{3,2},{4,5},{5,4},{6,7},{7,6},{8,9},{9,8},{10,11... | collective-permute-start | bytes 3145736 | tf_op jit(solution)/shard_map/ppermute | solution.py:31
  148.6 10.5 %collective-permute-done.24.refs_0_ = bf16[32,16,1024]{2,1,0:T(8,128)(2,1)S(1)} collective-permute-done((bf16[32,16,1024]{2,1,0:T(8,128)(2,1)S(1)}, bf16[32,16,1024]{2,1,0:T(8,128)(2,1)S(1)}, u32[]{:S(2)}, u32[]{:S(2)}) %collective-permute-start.24) | collective-permute-done | bytes 1048608 | tf_op jit(solution)/shard_map/ppermute | solution.py:39
  159.2 2.2 %collective-permute-start.27 = (bf16[32,16,1024]{2,1,0:T(8,128)(2,1)S(1)}, bf16[32,16,1024]{2,1,0:T(8,128)(2,1)S(1)}, u32[]{:S(2)}, u32[]{:S(2)}) collective-permute-start(bf16[32,16,1024]{2,1,0:T(8,128)(2,1)S(1)} %collective-permute-done.24.refs_0_), channel_id=1, source_target_pairs={{0,1},{1,0},{2,3},{3,2},{4,5},{5,4},{6,7},{7,6},{8,9},{9,8},{10,11... | collective-permute-start | bytes 3145736 | tf_op jit(solution)/shard_map/ppermute | solution.py:31
  161.4 2.4 %collective-permute-start.23 = (bf16[16,16,1024]{2,1,0:T(8,128)(2,1)S(1)}, bf16[16,16,1024]{2,1,0:T(8,128)(2,1)S(1)}, u32[]{:S(2)}, u32[]{:S(2)}) collective-permute-start(bf16[16,16,1024]{2,1,0:T(8,128)(2,1)S(1)} %slice.46), channel_id=1, source_target_pairs={{0,6},{1,193},{2,0},{3,195},{4,2},{5,197},{6,4},{7,199},{8,14},{9,... | collective-permute-start | bytes 1572872 | tf_op jit(solution)/shard_map/ppermute | solution.py:39
  163.8 0.3 collective-permute-start.25
  164.1 2.4 %gradient.5.refs_4_ = bf16[4,256,2048]{2,1,0:T(8,128)(2,1)} custom-call(s32[4]{0:T(128)S(1)} %pad_add_fusion.1.where, bf16[32,16,1024]{2,1,0:T(8,128)(2,1)S(1)} %collect.1.refs_0_, bf16[32,16,1024]{2,1,0:T(8,128)(2,1)S(1)} %collective-permute-done.28.refs_1_, bf16[256,512]{1,0:T(8,128)(2,1)S(1)} %bitcast.32, bf16[256,512]{1,0:T(8,128)(2,1)S(1)} %bitcast.37), custom_call_target="tpu_custom_call" | custom-call | flops 550000000 | bytes 4000000 | tf_op jit(solution)/shard_map/gradient/pallas_call | solution.py:180
  166.5 2.4 %gradient.6.refs_4_ = bf16[4,256,2048]{2,1,0:T(8,128)(2,1)} custom-call(s32[4]{0:T(128)S(1)} %pad_add_fusion.1.where, bf16[32,16,1024]{2,1,0:T(8,128)(2,1)S(1)} %collective-permute-done.24.refs_0_, bf16[32,16,1024]{2,1,0:T(8,128)(2,1)S(1)} %collective-permute-done.27.refs_1_, bf16[256,512]{1,0:T(8,128)(2,1)S(1)} %bitcast.33, ...), custom_call_target="tpu_custom_call", output_to_operand_aliasing={{}: (5, {})} | custom-call | flops 550000000 | bytes 4000000 | tf_op jit(solution)/shard_map/gradient/pallas_call | solution.py:180
  168.9 2.4 %gradient.7.refs_4_ = bf16[4,256,2048]{2,1,0:T(8,128)(2,1)} custom-call(s32[4]{0:T(128)S(1)} %pad_add_fusion.1.where, bf16[32,16,1024]{2,1,0:T(8,128)(2,1)S(1)} %collective-permute-done.22.refs_0_, bf16[32,16,1024]{2,1,0:T(8,128)(2,1)S(1)} %collective-permute-done.26.refs_1_, bf16[256,512]{1,0:T(8,128)(2,1)S(1)} %bitcast.34, ...), custom_call_target="tpu_custom_call", output_to_operand_aliasing={{}: (5, {})} | custom-call | flops 550000000 | bytes 4000000 | tf_op jit(solution)/shard_map/gradient/pallas_call | solution.py:180
  171.3 2.4 %collective-permute-done.25.refs_1_ = bf16[16,16,1024]{2,1,0:T(8,128)(2,1)S(1)} collective-permute-done((bf16[16,16,1024]{2,1,0:T(8,128)(2,1)S(1)}, bf16[16,16,1024]{2,1,0:T(8,128)(2,1)S(1)}, u32[]{:S(2)}, u32[]{:S(2)}) %collective-permute-start.25) | collective-permute-done | bytes 524320 | tf_op jit(solution)/shard_map/ppermute | solution.py:39
  173.6 1.9 %collective-permute-start.29 = (bf16[16,16,1024]{2,1,0:T(8,128)(2,1)S(1)}, bf16[16,16,1024]{2,1,0:T(8,128)(2,1)S(1)}, u32[]{:S(2)}, u32[]{:S(2)}) collective-permute-start(bf16[16,16,1024]{2,1,0:T(8,128)(2,1)S(1)} %collective-permute-done.23.refs_0_), channel_id=1, source_target_pairs={{0,1},{1,0},{2,3},{3,2},{4,5},{5,4},{6,7},{7,6},{8,9},{9,8},{10,11... | collective-permute-start | bytes 1572872 | tf_op jit(solution)/shard_map/ppermute | solution.py:31
  175.5 1.8 gradient.8.refs_4_
  177.3 0.5 collective-permute-done.30.refs_1_
  177.8 1.8 gradient.9
  (77 shorter events, 1.6 us)
Async XLA Ops:
  5.5 7.3 %collective-permute-start = (bf16[4,256,1024]{2,1,0:T(8,128)(2,1)}, bf16[4,256,1024]{2,1,0:T(8,128)(2,1)S(1)}, u32[]{:S(2)}, u32[]{:S(2)}) collective-permute-start(bf16[4,256,1024]{2,1,0:T(8,128)(2,1)} %dynamic-slice_bitcast_fusion), channel_id=1, source_target_pairs={{0,1},{1,0},{2,3},{3,2},{4,5},{5,4},{6,7},{7,6},{8,9},{9,8},{10,11... | collective-permute-start | bytes 6291464 | tf_op jit(solution)/shard_map/ppermute | solution.py:31
  8.8 3.7 %collective-permute-start.1 = (bf16[4,2,1024]{2,1,0:T(2,128)(2,1)S(1)}, bf16[4,2,1024]{2,1,0:T(2,128)(2,1)S(1)}, u32[]{:S(2)}, u32[]{:S(2)}) collective-permute-start(bf16[4,2,1024]{2,1,0:T(2,128)(2,1)S(1)} %get-tuple-element.68), channel_id=1, source_target_pairs={{0,1},{1,0},{2,3},{3,2},{4,5},{5,4},{6,7},{7,6},{8,9},{9,8},{10,11... | collective-permute-start | bytes 49160 | tf_op jit(solution)/shard_map/ppermute | solution.py:31
  8.9 10.7 %all-to-all-start = ((bf16[4,2,2048]{2,1,0:T(2,128)(2,1)}), bf16[4,2,2048]{2,1,0:T(2,128)(2,1)S(1)}, u32[]{:S(2)}, u32[]{:S(2)}) async-start(bf16[4,2,2048]{2,1,0:T(2,128)(2,1)} %bitcast.27), calls=%async_computation | async-start | bytes 65536 | tf_op jit(solution)/shard_map/all_to_all | solution.py:281
  12.8 2.2 %copy-start = (bf16[1,4,256,2048]{3,2,1,0:T(8,128)(2,1)S(1)}, bf16[1,4,256,2048]{3,2,1,0:T(8,128)(2,1)}, u32[]{:S(2)}) copy-start(bf16[1,4,256,2048]{3,2,1,0:T(8,128)(2,1)} %param.10) | copy-start | bytes 12582916
  15.0 46.9 %copy-start.11 = (f32[1,256]{1,0:T(1,128)S(1)}, f32[1,256]{1,0:T(1,128)}, u32[]{:S(2)}) copy-start(f32[1,256]{1,0:T(1,128)} %refs_9_.1) | copy-start | bytes 3076
  16.6 1.0 copy-start.12
  17.6 1.0 copy-start.13
  18.6 1.0 copy-start.14
  19.6 19.2 %collective-permute-start.2 = (bf16[528,1024]{1,0:T(8,128)(2,1)}, bf16[528,1024]{1,0:T(8,128)(2,1)S(1)}, u32[]{:S(2)}, u32[]{:S(2)}) collective-permute-start(bf16[528,1024]{1,0:T(8,128)(2,1)} %copy-done.14), channel_id=1, source_target_pairs={{0,2},{1,65},{2,4},{3,67},{4,6},{5,69},{6,0},{7,71},{8,10},{9,73},... | collective-permute-start | bytes 3244040 | tf_op jit(solution)/shard_map/ppermute | solution.py:39
  20.6 18.2 %collective-permute-start.3 = (bf16[528,1024]{1,0:T(8,128)(2,1)}, bf16[528,1024]{1,0:T(8,128)(2,1)}, u32[]{:S(2)}, u32[]{:S(2)}) collective-permute-start(bf16[528,1024]{1,0:T(8,128)(2,1)} %copy-done.13), channel_id=1, source_target_pairs={{0,6},{1,193},{2,0},{3,195},{4,2},{5,197},{6,4},{7,199},{8,14},{9,... | collective-permute-start | bytes 3244040 | tf_op jit(solution)/shard_map/ppermute | solution.py:39
  38.8 27.2 %copy-start.2 = (bf16[528,1024]{1,0:T(8,128)(2,1)}, bf16[528,1024]{1,0:T(8,128)(2,1)S(1)}, u32[]{:S(2)}) copy-start(bf16[528,1024]{1,0:T(8,128)(2,1)S(1)} %collective-permute-done.2.refs_4_) | copy-start | bytes 3244036
  38.8 16.4 %collective-permute-start.6 = (bf16[64,2048]{1,0:T(8,128)(2,1)}, bf16[64,2048]{1,0:T(8,128)(2,1)}, u32[]{:S(2)}, u32[]{:S(2)}) collective-permute-start(bf16[64,2048]{1,0:T(8,128)(2,1)} %bitcast.12.refs_0_), channel_id=1, source_target_pairs={{0,6},{2,0},{4,2},{6,4},{1,7},{3,1},{5,3},{7,5},{8,14},{10,8},{12,... | collective-permute-start | bytes 786440 | tf_op jit(solution)/shard_map/ppermute | solution.py:31
  44.2 12.5 %collective-permute-start.4 = (bf16[64,2048]{1,0:T(8,128)(2,1)}, bf16[64,2048]{1,0:T(8,128)(2,1)}, u32[]{:S(2)}, u32[]{:S(2)}) collective-permute-start(bf16[64,2048]{1,0:T(8,128)(2,1)} %bitcast.12.refs_0_), channel_id=1, source_target_pairs={{0,2},{2,4},{4,6},{6,0},{1,3},{3,5},{5,7},{7,1},{8,10},{10,12},{12... | collective-permute-start | bytes 786440 | tf_op jit(solution)/shard_map/ppermute | solution.py:31
  44.2 15.9 %collective-permute-start.5 = (bf16[64,2048]{1,0:T(8,128)(2,1)}, bf16[64,2048]{1,0:T(8,128)(2,1)}, u32[]{:S(2)}, u32[]{:S(2)}) collective-permute-start(bf16[64,2048]{1,0:T(8,128)(2,1)} %bitcast.12.refs_0_), channel_id=1, source_target_pairs={{0,4},{2,6},{4,0},{6,2},{1,5},{3,7},{5,1},{7,3},{8,12},{10,14},{12... | collective-permute-start | bytes 786440 | tf_op jit(solution)/shard_map/ppermute | solution.py:31
  45.9 14.6 %collective-permute-start.7 = (bf16[64,2048]{1,0:T(8,128)(2,1)}, bf16[64,2048]{1,0:T(8,128)(2,1)S(1)}, u32[]{:S(2)}, u32[]{:S(2)}) collective-permute-start(bf16[64,2048]{1,0:T(8,128)(2,1)} %bitcast.12.refs_0_), channel_id=1, source_target_pairs={{0,1},{1,0},{2,3},{3,2},{4,5},{5,4},{6,7},{7,6},{8,9},{9,8},{10,11... | collective-permute-start | bytes 786440 | tf_op jit(solution)/shard_map/ppermute | solution.py:31
  55.2 5.4 %collective-permute-start.10 = (bf16[64,2048]{1,0:T(8,128)(2,1)}, bf16[64,2048]{1,0:T(8,128)(2,1)S(1)}, u32[]{:S(2)}, u32[]{:S(2)}) collective-permute-start(bf16[64,2048]{1,0:T(8,128)(2,1)} %collective-permute-done.6.refs_3_), channel_id=1, source_target_pairs={{0,1},{1,0},{2,3},{3,2},{4,5},{5,4},{6,7},{7,6},{8,9},{9,8},{10,11... | collective-permute-start | bytes 786440 | tf_op jit(solution)/shard_map/ppermute | solution.py:31
  56.7 4.8 %collective-permute-start.8 = (bf16[64,2048]{1,0:T(8,128)(2,1)}, bf16[64,2048]{1,0:T(8,128)(2,1)S(1)}, u32[]{:S(2)}, u32[]{:S(2)}) collective-permute-start(bf16[64,2048]{1,0:T(8,128)(2,1)} %collective-permute-done.4.refs_1_), channel_id=1, source_target_pairs={{0,1},{1,0},{2,3},{3,2},{4,5},{5,4},{6,7},{7,6},{8,9},{9,8},{10,11... | collective-permute-start | bytes 786440 | tf_op jit(solution)/shard_map/ppermute | solution.py:31
  60.1 1.7 collective-permute-start.9
  60.5 27.4 %collective-permute-start.15 = (bf16[528,1024]{1,0:T(8,128)(2,1)}, bf16[528,1024]{1,0:T(8,128)(2,1)S(1)}, u32[]{:S(2)}, u32[]{:S(2)}) collective-permute-start(bf16[528,1024]{1,0:T(8,128)(2,1)} %copy-done.12), channel_id=1, source_target_pairs={{0,4},{1,129},{2,6},{3,131},{4,0},{5,133},{6,2},{7,135},{8,12},{9,... | collective-permute-start | bytes 3244040 | tf_op jit(solution)/shard_map/ppermute | solution.py:39
  61.9 1.2 copy-start.5
  63.1 7.9 %copy-start.1 = (bf16[1,4,256,2048]{3,2,1,0:T(8,128)(2,1)S(1)}, bf16[1,4,256,2048]{3,2,1,0:T(8,128)(2,1)}, u32[]{:S(2)}) copy-start(bf16[1,4,256,2048]{3,2,1,0:T(8,128)(2,1)} %param.10) | copy-start | bytes 12582916
  66.0 1.8 %copy-start.8 = (bf16[512,256]{1,0:T(8,128)(2,1)}, bf16[512,256]{1,0:T(8,128)(2,1)S(1)}, u32[]{:S(2)}) copy-start(bf16[512,256]{1,0:T(8,128)(2,1)S(1)} %get-tuple-element.48) | copy-start | bytes 786436
  66.0 5.9 %copy-start.6 = (bf16[512,256]{1,0:T(8,128)(2,1)}, bf16[512,256]{1,0:T(8,128)(2,1)S(1)}, u32[]{:S(2)}) copy-start(bf16[512,256]{1,0:T(8,128)(2,1)S(1)} %get-tuple-element.47) | copy-start | bytes 786436
  66.0 1.6 collective-permute-start.11
  67.7 14.5 %copy-start.3 = (bf16[528,1024]{1,0:T(8,128)(2,1)S(1)}, bf16[528,1024]{1,0:T(8,128)(2,1)}, u32[]{:S(2)}) copy-start(bf16[528,1024]{1,0:T(8,128)(2,1)} %copy-done.2) | copy-start | bytes 3244036
  67.7 14.5 %copy-start.10 = (f32[1,2048]{1,0:T(1,128)S(1)}, f32[1,2048]{1,0:T(1,128)}, u32[]{:S(2)}) copy-start(f32[1,2048]{1,0:T(1,128)} %refs_6_.1) | copy-start | bytes 24580
  67.7 14.5 %collective-permute-start.13 = (bf16[2,512,256]{2,1,0:T(8,128)(2,1)S(1)}, bf16[2,512,256]{2,1,0:T(8,128)(2,1)S(1)}, u32[]{:S(2)}, u32[]{:S(2)}) collective-permute-start(bf16[2,512,256]{2,1,0:T(8,128)(2,1)S(1)} %pad_maximum_fusion.refs_0_), channel_id=1, source_target_pairs={{0,2},{1,65},{2,4},{3,67},{4,6},{5,69},{6,0},{7,71},{8,10},{9,73},... | collective-permute-start | bytes 1572872 | tf_op jit(solution)/shard_map/ppermute | solution.py:39
  67.8 14.4 %collective-permute-start.14 = (bf16[2,512,256]{2,1,0:T(8,128)(2,1)S(1)}, bf16[2,512,256]{2,1,0:T(8,128)(2,1)S(1)}, u32[]{:S(2)}, u32[]{:S(2)}) collective-permute-start(bf16[2,512,256]{2,1,0:T(8,128)(2,1)S(1)} %pad_maximum_fusion.refs_0_), channel_id=1, source_target_pairs={{0,6},{1,193},{2,0},{3,195},{4,2},{5,197},{6,4},{7,199},{8,14},{9,... | collective-permute-start | bytes 1572872 | tf_op jit(solution)/shard_map/ppermute | solution.py:39
  70.5 17.4 %collective-permute-start.12 = (bf16[2,512,256]{2,1,0:T(8,128)(2,1)S(1)}, bf16[2,512,256]{2,1,0:T(8,128)(2,1)S(1)}, u32[]{:S(2)}, u32[]{:S(2)}) collective-permute-start(bf16[2,512,256]{2,1,0:T(8,128)(2,1)S(1)} %pad_maximum_fusion.refs_0_), channel_id=1, source_target_pairs={{0,4},{1,129},{2,6},{3,131},{4,0},{5,133},{6,2},{7,135},{8,12},{9,... | collective-permute-start | bytes 1572872 | tf_op jit(solution)/shard_map/ppermute | solution.py:39
  86.8 6.9 %copy-start.7 = (bf16[512,256]{1,0:T(8,128)(2,1)S(1)}, bf16[512,256]{1,0:T(8,128)(2,1)}, u32[]{:S(2)}) copy-start(bf16[512,256]{1,0:T(8,128)(2,1)} %copy-done.6) | copy-start | bytes 786436
  86.8 7.0 %copy-start.9 = (bf16[512,256]{1,0:T(8,128)(2,1)S(1)}, bf16[512,256]{1,0:T(8,128)(2,1)}, u32[]{:S(2)}) copy-start(bf16[512,256]{1,0:T(8,128)(2,1)} %copy-done.8) | copy-start | bytes 786436
  87.8 4.3 %copy-start.4 = (bf16[528,1024]{1,0:T(8,128)(2,1)}, bf16[528,1024]{1,0:T(8,128)(2,1)S(1)}, u32[]{:S(2)}) copy-start(bf16[528,1024]{1,0:T(8,128)(2,1)S(1)} %collective-permute-done.15.refs_1_) | copy-start | bytes 3244036
  90.4 25.1 %slice-start = ((bf16[528,1024]{1,0:T(8,128)(2,1)}), bf16[4,1024]{1,0:T(4,128)(2,1)S(1)}, s32[]{:S(2)}) async-start(bf16[528,1024]{1,0:T(8,128)(2,1)} %copy-done.2), calls=%async_computation.4 | async-start | bytes 16384 | tf_op jit(solution)/shard_map/slice | solution.py:305
  90.4 9.6 %collective-permute-start.16 = (bf16[8,16,1024]{2,1,0:T(8,128)(2,1)S(1)}, bf16[8,16,1024]{2,1,0:T(8,128)(2,1)S(1)}, u32[]{:S(2)}, u32[]{:S(2)}) collective-permute-start(bf16[8,16,1024]{2,1,0:T(8,128)(2,1)S(1)} %get-tuple-element.55), channel_id=1, source_target_pairs={{0,64},{1,3},{2,66},{3,5},{4,68},{5,7},{6,70},{7,1},{8,72},{9,11},... | collective-permute-start | bytes 786440 | tf_op jit(solution)/shard_map/ppermute | solution.py:47
  90.5 9.5 %collective-permute-start.17 = (bf16[8,16,1024]{2,1,0:T(8,128)(2,1)S(1)}, bf16[8,16,1024]{2,1,0:T(8,128)(2,1)}, u32[]{:S(2)}, u32[]{:S(2)}) collective-permute-start(bf16[8,16,1024]{2,1,0:T(8,128)(2,1)S(1)} %get-tuple-element.56), channel_id=1, source_target_pairs={{0,128},{1,5},{2,130},{3,7},{4,132},{5,1},{6,134},{7,3},{8,136},{9... | collective-permute-start | bytes 786440 | tf_op jit(solution)/shard_map/ppermute | solution.py:47
  92.2 8.6 %collective-permute-start.18 = (bf16[8,16,1024]{2,1,0:T(8,128)(2,1)S(1)}, bf16[8,16,1024]{2,1,0:T(8,128)(2,1)}, u32[]{:S(2)}, u32[]{:S(2)}) collective-permute-start(bf16[8,16,1024]{2,1,0:T(8,128)(2,1)S(1)} %get-tuple-element.57), channel_id=1, source_target_pairs={{0,192},{1,7},{2,194},{3,1},{4,196},{5,3},{6,198},{7,5},{8,200},{9... | collective-permute-start | bytes 786440 | tf_op jit(solution)/shard_map/ppermute | solution.py:47
  93.6 21.8 %slice-start.1 = ((bf16[528,1024]{1,0:T(8,128)(2,1)}), bf16[4,1024]{1,0:T(4,128)(2,1)S(1)}, s32[]{:S(2)}) async-start(bf16[528,1024]{1,0:T(8,128)(2,1)} %copy-done.4), calls=%async_computation.5 | async-start | bytes 16384 | tf_op jit(solution)/shard_map/slice | solution.py:305
  102.6 12.8 %all-to-all-start.2 = ((bf16[8,16,1024]{2,1,0:T(8,128)(2,1)}), bf16[8,16,1024]{2,1,0:T(8,128)(2,1)S(1)}, u32[]{:S(2)}, u32[]{:S(2)}) async-start(bf16[8,16,1024]{2,1,0:T(8,128)(2,1)} %add_convert_fusion), calls=%async_computation.2 | async-start | bytes 524288 | tf_op jit(solution)/shard_map/all_to_all | solution.py:315
  127.5 11.8 %collective-permute-start.19 = (bf16[8,16,1024]{2,1,0:T(8,128)(2,1)S(1)}, bf16[8,16,1024]{2,1,0:T(8,128)(2,1)S(1)}, u32[]{:S(2)}, u32[]{:S(2)}) collective-permute-start(bf16[8,16,1024]{2,1,0:T(8,128)(2,1)S(1)} %all_to_all.21.refs_0_), channel_id=1, source_target_pairs={{0,64},{1,3},{2,66},{3,5},{4,68},{5,7},{6,70},{7,1},{8,72},{9,11},... | collective-permute-start | bytes 786440 | tf_op jit(solution)/shard_map/ppermute | solution.py:47
  133.4 9.6 %collective-permute-start.20 = (bf16[8,16,1024]{2,1,0:T(8,128)(2,1)S(1)}, bf16[8,16,1024]{2,1,0:T(8,128)(2,1)S(1)}, u32[]{:S(2)}, u32[]{:S(2)}) collective-permute-start(bf16[8,16,1024]{2,1,0:T(8,128)(2,1)S(1)} %all_to_all.21.refs_0_), channel_id=1, source_target_pairs={{0,128},{1,5},{2,130},{3,7},{4,132},{5,1},{6,134},{7,3},{8,136},{9... | collective-permute-start | bytes 786440 | tf_op jit(solution)/shard_map/ppermute | solution.py:47
  136.5 6.6 %collective-permute-start.21 = (bf16[8,16,1024]{2,1,0:T(8,128)(2,1)S(1)}, bf16[8,16,1024]{2,1,0:T(8,128)(2,1)S(1)}, u32[]{:S(2)}, u32[]{:S(2)}) collective-permute-start(bf16[8,16,1024]{2,1,0:T(8,128)(2,1)S(1)} %all_to_all.21.refs_0_), channel_id=1, source_target_pairs={{0,192},{1,7},{2,194},{3,1},{4,196},{5,3},{6,198},{7,5},{8,200},{9... | collective-permute-start | bytes 786440 | tf_op jit(solution)/shard_map/ppermute | solution.py:47
  143.9 15.2 %collective-permute-start.24 = (bf16[32,16,1024]{2,1,0:T(8,128)(2,1)S(1)}, bf16[32,16,1024]{2,1,0:T(8,128)(2,1)S(1)}, u32[]{:S(2)}, u32[]{:S(2)}) collective-permute-start(bf16[32,16,1024]{2,1,0:T(8,128)(2,1)S(1)} %collect.1.refs_0_), channel_id=1, source_target_pairs={{0,2},{1,65},{2,4},{3,67},{4,6},{5,69},{6,0},{7,71},{8,10},{9,73},... | collective-permute-start | bytes 3145736 | tf_op jit(solution)/shard_map/ppermute | solution.py:39
  144.0 17.3 %collective-permute-start.22 = (bf16[32,16,1024]{2,1,0:T(8,128)(2,1)S(1)}, bf16[32,16,1024]{2,1,0:T(8,128)(2,1)S(1)}, u32[]{:S(2)}, u32[]{:S(2)}) collective-permute-start(bf16[32,16,1024]{2,1,0:T(8,128)(2,1)S(1)} %collect.1.refs_0_), channel_id=1, source_target_pairs={{0,6},{1,193},{2,0},{3,195},{4,2},{5,197},{6,4},{7,199},{8,14},{9,... | collective-permute-start | bytes 3145736 | tf_op jit(solution)/shard_map/ppermute | solution.py:39
  146.7 17.4 %collective-permute-start.28 = (bf16[32,16,1024]{2,1,0:T(8,128)(2,1)S(1)}, bf16[32,16,1024]{2,1,0:T(8,128)(2,1)S(1)}, u32[]{:S(2)}, u32[]{:S(2)}) collective-permute-start(bf16[32,16,1024]{2,1,0:T(8,128)(2,1)S(1)} %collect.1.refs_0_), channel_id=1, source_target_pairs={{0,1},{1,0},{2,3},{3,2},{4,5},{5,4},{6,7},{7,6},{8,9},{9,8},{10,11... | collective-permute-start | bytes 3145736 | tf_op jit(solution)/shard_map/ppermute | solution.py:31
  159.2 7.3 %collective-permute-start.27 = (bf16[32,16,1024]{2,1,0:T(8,128)(2,1)S(1)}, bf16[32,16,1024]{2,1,0:T(8,128)(2,1)S(1)}, u32[]{:S(2)}, u32[]{:S(2)}) collective-permute-start(bf16[32,16,1024]{2,1,0:T(8,128)(2,1)S(1)} %collective-permute-done.24.refs_0_), channel_id=1, source_target_pairs={{0,1},{1,0},{2,3},{3,2},{4,5},{5,4},{6,7},{7,6},{8,9},{9,8},{10,11... | collective-permute-start | bytes 3145736 | tf_op jit(solution)/shard_map/ppermute | solution.py:31
  161.3 7.5 %collective-permute-start.26 = (bf16[32,16,1024]{2,1,0:T(8,128)(2,1)S(1)}, bf16[32,16,1024]{2,1,0:T(8,128)(2,1)S(1)}, u32[]{:S(2)}, u32[]{:S(2)}) collective-permute-start(bf16[32,16,1024]{2,1,0:T(8,128)(2,1)S(1)} %collective-permute-done.22.refs_0_), channel_id=1, source_target_pairs={{0,1},{1,0},{2,3},{3,2},{4,5},{5,4},{6,7},{7,6},{8,9},{9,8},{10,11... | collective-permute-start | bytes 3145736 | tf_op jit(solution)/shard_map/ppermute | solution.py:31
  161.4 9.9 %collective-permute-start.23 = (bf16[16,16,1024]{2,1,0:T(8,128)(2,1)S(1)}, bf16[16,16,1024]{2,1,0:T(8,128)(2,1)S(1)}, u32[]{:S(2)}, u32[]{:S(2)}) collective-permute-start(bf16[16,16,1024]{2,1,0:T(8,128)(2,1)S(1)} %slice.46), channel_id=1, source_target_pairs={{0,6},{1,193},{2,0},{3,195},{4,2},{5,197},{6,4},{7,199},{8,14},{9,... | collective-permute-start | bytes 1572872 | tf_op jit(solution)/shard_map/ppermute | solution.py:39
  163.8 9.8 %collective-permute-start.25 = (bf16[16,16,1024]{2,1,0:T(8,128)(2,1)S(1)}, bf16[16,16,1024]{2,1,0:T(8,128)(2,1)S(1)}, u32[]{:S(2)}, u32[]{:S(2)}) collective-permute-start(bf16[16,16,1024]{2,1,0:T(8,128)(2,1)S(1)} %slice.47), channel_id=1, source_target_pairs={{0,2},{1,65},{2,4},{3,67},{4,6},{5,69},{6,0},{7,71},{8,10},{9,73},... | collective-permute-start | bytes 1572872 | tf_op jit(solution)/shard_map/ppermute | solution.py:39
  173.6 3.7 %collective-permute-start.29 = (bf16[16,16,1024]{2,1,0:T(8,128)(2,1)S(1)}, bf16[16,16,1024]{2,1,0:T(8,128)(2,1)S(1)}, u32[]{:S(2)}, u32[]{:S(2)}) collective-permute-start(bf16[16,16,1024]{2,1,0:T(8,128)(2,1)S(1)} %collective-permute-done.23.refs_0_), channel_id=1, source_target_pairs={{0,1},{1,0},{2,3},{3,2},{4,5},{5,4},{6,7},{7,6},{8,9},{9,8},{10,11... | collective-permute-start | bytes 1572872 | tf_op jit(solution)/shard_map/ppermute | solution.py:31
  175.5 2.3 %collective-permute-start.30 = (bf16[16,16,1024]{2,1,0:T(8,128)(2,1)S(1)}, bf16[16,16,1024]{2,1,0:T(8,128)(2,1)S(1)}, u32[]{:S(2)}, u32[]{:S(2)}) collective-permute-start(bf16[16,16,1024]{2,1,0:T(8,128)(2,1)S(1)} %collective-permute-done.25.refs_1_), channel_id=1, source_target_pairs={{0,1},{1,0},{2,3},{3,2},{4,5},{5,4},{6,7},{7,6},{8,9},{9,8},{10,11... | collective-permute-start | bytes 1572872 | tf_op jit(solution)/shard_map/ppermute | solution.py:31
